TPU v7x, 32 devices: a whole 2x2x4 slice. The times are simulated.
32 devices in a mesh: lat: 4 (over x, core), lon: 8 (over z, y).
Axes of the slice: x: 2, y: 2, z: 4, core: 2. Of those that a mesh axis runs over, the one named last changes fastest.
Arguments:
- features: bfloat16 [16, 256, 256], P('lat', 'lon'), may hold values from -6 to 6
- cotangent: bfloat16 [16, 256, 256], P('lat', 'lon'), may hold values from -6 to 6
- weight: bfloat16 [4, 256, 256], replicated, may hold values from -0.1875 to 0.1875
- filter_taps: bfloat16 [16, 4, 5, 64], P('lat'), may hold values from -6 to 6
- lat_ext: int32 [16], P('lat'), may hold values from 1 to 3, as said below
- lon_count: int32 [16], P('lat'), may hold values from 1 to 32, as said below
Outputs:
- output: bfloat16 [16, 256, 256], P('lat', 'lon')
- field_grad: bfloat16 [16, 256, 256], P('lat', 'lon')
- weight_grad: float32 [4, 256, 256], replicated
Inputs may be any that keep to these rules, and one draw needn't show every extreme that they name: `lat_ext`: a row uses the latitude offsets whose magnitude is below its entry. `lon_count`: a row uses the longitude offsets whose magnitude is below its entry.
All inputs are finite; a program needn't handle non-finite values.
Results may differ from a plain program's by a relative error of at most 0.006.
Values may be sent and summed in bfloat16 or wider, within the bound.
No kernel may reach another device: no remote copies, remote signals or barrier semaphores. Data moves between devices by JAX's collectives and lax.ppermute only.
A program may use at most 64 MiB of HBM per device.

v0:
```python
import math

import jax
import jax.numpy as jnp
from jax import lax
from jax.sharding import PartitionSpec as P


def extended(cells, sides, width, closed):
    for axis, dim in sides:
        count = lax.axis_size(axis)
        ends = count if closed else count - 1
        head = lax.slice_in_dim(cells, 0, width, axis=dim)
        tail = lax.slice_in_dim(cells, cells.shape[dim] - width, cells.shape[dim], axis=dim)
        cells = jnp.concatenate(
            [
                lax.ppermute(tail, axis, [(i, (i + 1) % count) for i in range(ends)]),
                cells,
                lax.ppermute(head, axis, [((i + 1) % count, i) for i in range(ends)]),
            ],
            axis=dim,
        )
    return cells


def shifted(block, axis, distance):
    devices = range(lax.axis_size(axis))
    route = [((i - distance) % len(devices), i) for i in devices]
    return lax.ppermute(block, axis, route)


def passed_along(array, axis, by):
    peers = lax.axis_size(axis)
    pairs = [(i, i + by) for i in range(peers) if 0 <= i + by < peers]
    return lax.ppermute(array, axis, pairs)


def make_filters(filter_taps, lat_ext, lon_count):
    lat_reach = filter_taps.shape[2] // 2
    half_width = filter_taps.shape[3] // 2
    lat_dist = jnp.abs(jnp.arange(filter_taps.shape[2], dtype=jnp.int32) - lat_reach)
    lon_dist = jnp.abs(jnp.arange(filter_taps.shape[3], dtype=jnp.int32) - half_width)
    support = (lat_dist[None, :, None] < lat_ext[:, None, None]) & (
        lon_dist[None, None, :] < lon_count[:, None, None]
    )
    support_size = ((2 * lat_ext - 1) * (2 * lon_count - 1)).astype(jnp.float32)
    row_scale = lax.rsqrt(support_size)
    masked = (
        filter_taps.astype(jnp.float32)
        * support[:, None].astype(jnp.float32)
        * row_scale[:, None, None, None]
    )
    return masked.astype(jnp.bfloat16)


def forward_taps(row_taps, lon_width):
    leading = row_taps.shape[:-1]
    return jnp.concatenate(
        [row_taps, jnp.zeros(leading + (lon_width + 1,), row_taps.dtype)], axis=-1
    )


def band_matrix(padded, lon_width):
    leading = padded.shape[:-1]
    repeated = jnp.tile(padded, (1,) * len(leading) + (lon_width,))
    return repeated[..., : lon_width * 3 * lon_width].reshape(leading + (lon_width, 3 * lon_width))


def per_device(features, cotangent, weight, filter_taps, lat_ext, lon_count):
    row_count, lon_width, channels = features.shape
    basis_count = weight.shape[0]
    lat_taps = filter_taps.shape[2]
    lat_reach = lat_taps // 2
    filters = make_filters(filter_taps, lat_ext, lon_count)
    band_rows = extended(features, (("lat", 0),), lat_reach, False)
    window = extended(band_rows, (("lon", 1),), lon_width, True)
    banded_all = band_matrix(forward_taps(filters, lon_width), lon_width)
    patches = jnp.stack([window[offset : offset + row_count] for offset in range(lat_taps)], axis=1)
    basis_f32 = jnp.einsum(
        "okejm,oemc->ojkc", banded_all, patches, preferred_element_type=jnp.float32
    )
    basis_out = basis_f32.astype(jnp.bfloat16)
    flat_out = basis_out.reshape(row_count * lon_width, basis_count * channels)
    flat_weight = weight.reshape(basis_count * channels, channels)
    output = jnp.dot(flat_out, flat_weight, preferred_element_type=jnp.float32).astype(jnp.bfloat16)
    output = output.reshape(row_count, lon_width, channels)
    flat_cot = cotangent.reshape(row_count * lon_width, channels)
    partial_grad = lax.dot_general(
        flat_out, flat_cot, (((0,), (0,)), ((), ())), preferred_element_type=jnp.float32
    )
    total_cells = row_count * lax.axis_size("lat") * lon_width * lax.axis_size("lon")
    summed_grad = lax.psum(partial_grad, ("lat", "lon"))
    weight_grad = (summed_grad * (1.0 / math.sqrt(total_cells))).reshape(
        basis_count, channels, channels
    )
    basis_grad = lax.dot_general(
        flat_cot, flat_weight, (((1,), (1,)), ((), ())), preferred_element_type=jnp.float32
    ).astype(jnp.bfloat16)
    basis_grad = basis_grad.reshape(row_count, lon_width, basis_count, channels)
    partial_value = jnp.zeros((row_count + 2 * lat_reach, 3 * lon_width, channels), jnp.float32)
    for offset in range(lat_taps):
        contrib = jnp.einsum(
            "okjm,ojkc->omc",
            banded_all[:, :, offset],
            basis_grad,
            preferred_element_type=jnp.float32,
        )
        partial_value = partial_value + jnp.pad(
            contrib, ((offset, 2 * lat_reach - offset), (0, 0), (0, 0))
        )
    from_west = shifted(partial_value[:, 2 * lon_width :].astype(jnp.bfloat16), "lon", 1).astype(
        jnp.float32
    )
    from_east = shifted(partial_value[:, :lon_width].astype(jnp.bfloat16), "lon", -1).astype(
        jnp.float32
    )
    center = partial_value[:, lon_width : 2 * lon_width] + from_west + from_east
    from_north = passed_along(
        center[row_count + lat_reach :].astype(jnp.bfloat16), "lat", 1
    ).astype(jnp.float32)
    from_south = passed_along(center[:lat_reach].astype(jnp.bfloat16), "lat", -1).astype(
        jnp.float32
    )
    core_rows = center[lat_reach : lat_reach + row_count]
    core_rows = core_rows + jnp.pad(from_north, ((0, row_count - lat_reach), (0, 0), (0, 0)))
    core_rows = core_rows + jnp.pad(from_south, ((row_count - lat_reach, 0), (0, 0), (0, 0)))
    field_grad = core_rows.astype(jnp.bfloat16)
    return (output, field_grad, weight_grad)


def solution(mesh):
    in_specs = (
        P("lat", "lon", None),
        P("lat", "lon", None),
        P(),
        P("lat", None, None, None),
        P("lat"),
        P("lat"),
    )
    out_specs = (P("lat", "lon", None), P("lat", "lon", None), P())
    return jax.shard_map(
        per_device, mesh=mesh, in_specs=in_specs, out_specs=out_specs, check_vma=False
    )
```

profile of v0, /device:TPU:3, one launch (start us, length us, event | category | flops | bytes accessed | tf_op | source)
XLA Modules:
  0.0 174.6 jit_solution(2255319499992352537)
XLA Ops:
  7.2 0.0 copy-start
  7.2 0.0 all-reduce.10.cloned.1.call-start
  7.2 0.0 copy-start.4
  7.2 0.0 copy-start.5
  7.2 0.8 fusion.21
  8.1 0.0 copy-start.3
  8.1 1.4 collective-permute-start
  9.5 3.2 %collective-permute-start.1 = (bf16[2,32,256]{2,1,0:T(8,128)(2,1)S(1)}, bf16[2,32,256]{2,1,0:T(8,128)(2,1)S(1)}, u32[]{:S(2)}, u32[]{:S(2)}) collective-permute-start(bf16[2,32,256]{2,1,0:T(8,128)(2,1)S(1)} %get-tuple-element.11), channel_id=1, source_target_pairs={{8,0},{16,8},{24,16},{9,1},{17,9},{25,17},{10,2},{18,10},{26,18},{... | collective-permute-start | bytes 98312 | tf_op jit(solution)/shard_map/ppermute | solution.py:19
  12.7 0.0 copy-done.4
  12.7 0.0 copy-done.5
  12.8 0.1 broadcast_compare_fusion
  12.8 0.1 broadcast_compare_fusion.1
  12.9 0.1 and_convert_fusion
  13.0 0.0 copy-done.3
  13.0 0.1 multiply_convert_fusion
  13.1 0.1 tile.4
  13.2 1.8 %tile.10 = bf16[4,4,5,3104]{3,1,2,0:T(4,128)(2,1)S(1)} reshape(bf16[4,4,5,32,97]{4,3,1,2,0:T(8,128)(2,1)S(1)} %tile.4) | data formatting | bytes 993280 | tf_op jit(solution)/shard_map/tile | solution.py:65
  15.0 0.2 slice.85
  15.2 0.0 copy-start.2
  15.2 0.5 reshape.107
  15.7 0.0 copy-done
  15.7 0.3 copy-done.2
  16.0 0.3 convolution_convert_fusion
  16.3 0.2 reshape.112
  16.5 0.2 convolution_bitcast_fusion.1
  16.8 0.2 convolution_bitcast_fusion.2
  17.0 0.2 convolution_bitcast_fusion.3
  17.3 0.2 convolution_bitcast_fusion.4
  17.5 0.2 convolution_bitcast_fusion.5
  17.8 0.1 fusion.18
  18.0 0.0 copy-start.1
  18.0 4.3 %collective-permute-start.5 = (bf16[8,32,256]{2,1,0:T(8,128)(2,1)S(1)}, bf16[8,32,256]{2,1,0:T(8,128)(2,1)S(1)}, u32[]{:S(2)}, u32[]{:S(2)}) collective-permute-start(bf16[8,32,256]{2,1,0:T(8,128)(2,1)S(1)} %get-tuple-element.8), channel_id=1, source_target_pairs={{1,0},{2,1},{3,2},{4,3},{5,4},{6,5},{7,6},{0,7},{9,8},{10,9},{11,1... | collective-permute-start | bytes 393224 | tf_op jit(solution)/shard_map/ppermute | solution.py:29
  22.3 0.0 collective-permute-start.4
  22.3 0.0 collective-permute-done
  22.3 0.0 copy-done.1
  22.3 0.0 collective-permute-done.1
  22.4 4.2 %collective-permute-start.3 = (bf16[8,32,256]{2,1,0:T(8,128)(2,1)S(1)}, bf16[8,32,256]{2,1,0:T(8,128)(2,1)S(1)}, u32[]{:S(2)}, u32[]{:S(2)}) collective-permute-start(bf16[8,32,256]{2,1,0:T(8,128)(2,1)S(1)} %constant_dynamic-update-slice_fusion), channel_id=1, source_target_pairs={{1,0},{2,1},{3,2},{4,3},{5,4},{6,5},{7,6},{0,7},{9,8},{10,9},{11,1... | collective-permute-start | bytes 393224 | tf_op jit(solution)/shard_map/ppermute | solution.py:19
  26.6 0.0 collective-permute-start.2
  26.6 0.0 collective-permute-done.5
  26.6 3.1 %collective-permute-done.4 = bf16[8,32,256]{2,1,0:T(8,128)(2,1)S(1)} collective-permute-done((bf16[8,32,256]{2,1,0:T(8,128)(2,1)S(1)}, bf16[8,32,256]{2,1,0:T(8,128)(2,1)S(1)}, u32[]{:S(2)}, u32[]{:S(2)}) %collective-permute-start.4) | collective-permute-done | bytes 131104 | tf_op jit(solution)/shard_map/ppermute | solution.py:29
  29.7 0.1 fusion.16
  29.7 0.0 collective-permute-done.3
  29.8 3.3 %collective-permute-done.2 = bf16[8,32,256]{2,1,0:T(8,128)(2,1)S(1)} collective-permute-done((bf16[8,32,256]{2,1,0:T(8,128)(2,1)S(1)}, bf16[8,32,256]{2,1,0:T(8,128)(2,1)S(1)}, u32[]{:S(2)}, u32[]{:S(2)}) %collective-permute-start.2) | collective-permute-done | bytes 131104 | tf_op jit(solution)/shard_map/ppermute | solution.py:17
  33.2 0.4 fusion.1
  33.6 0.2 copy.24
  33.8 1.3 fusion.22
  35.1 0.0 all-reduce.10.cloned.1.call-update
  35.2 5.6 %collective-permute-start.7 = (bf16[2,32,256]{2,1,0:T(8,128)(2,1)S(1)}, bf16[2,32,256]{2,1,0:T(8,128)(2,1)S(1)}, u32[]{:S(2)}, u32[]{:S(2)}) collective-permute-start(bf16[2,32,256]{2,1,0:T(8,128)(2,1)S(1)} %get-tuple-element.10), channel_id=1, source_target_pairs={{8,0},{16,8},{24,16},{9,1},{17,9},{25,17},{10,2},{18,10},{26,18},{... | collective-permute-start | bytes 98312 | tf_op jit(solution)/shard_map/ppermute | solution.py:35
  40.8 1.3 collective-permute-start.6
  42.1 0.0 collective-permute-done.7
  42.1 1.8 %collective-permute-done.6 = bf16[2,32,256]{2,1,0:T(8,128)(2,1)S(1)} collective-permute-done((bf16[2,32,256]{2,1,0:T(8,128)(2,1)S(1)}, bf16[2,32,256]{2,1,0:T(8,128)(2,1)S(1)}, u32[]{:S(2)}, u32[]{:S(2)}) %collective-permute-start.6) | collective-permute-done | bytes 32800 | tf_op jit(solution)/shard_map/ppermute | solution.py:35
  43.9 0.6 fusion.15
  44.6 0.9 convolution_convert_fusion.1
  45.4 120.0 %all-reduce.10.cloned.1.call-done = f32[1024,256]{1,0:T(8,128)} async-done(((f32[1024,256]{1,0:T(8,128)}), f32[1024,256]{1,0:T(8,128)}) %all-reduce.10.cloned.1.call-update) | async-done | bytes 1048592 | tf_op jit(solution)/shard_map/psum | solution.py:92
  165.4 2.3 %broadcast_multiply_fusion = f32[1024,256]{1,0:T(8,128)} fusion(f32[1024,256]{1,0:T(8,128)} %all-reduce.10.cloned.1.call-done), kind=kLoop, calls=%fused_computation.12 | loop fusion | flops 262144 | bytes 2097152 | tf_op jit(solution)/shard_map/mul | solution.py:93
  (16 shorter events, 0.2 us)
Async XLA Ops:
  7.2 8.5 %copy-start = (bf16[4,256,256]{2,1,0:T(8,128)(2,1)S(1)}, bf16[4,256,256]{2,1,0:T(8,128)(2,1)}, u32[]{:S(2)}) copy-start(bf16[4,256,256]{2,1,0:T(8,128)(2,1)} %param.8) | copy-start | bytes 1572868
  7.2 158.3 %all-reduce.10.cloned.1.call-start = ((), (), s32[]{:S(2)}) async-start(), calls=%async_computation | async-start | bytes 2097152 | tf_op jit(solution)/shard_map/psum | solution.py:92
  7.2 5.5 %copy-start.4 = (s32[4]{0:T(128)S(1)}, s32[4]{0:T(128)}, u32[]{:S(2)}) copy-start(s32[4]{0:T(128)} %param.11) | copy-start | bytes 52
  7.2 5.5 %copy-start.5 = (s32[4]{0:T(128)S(1)}, s32[4]{0:T(128)}, u32[]{:S(2)}) copy-start(s32[4]{0:T(128)} %param.10) | copy-start | bytes 52
  8.1 4.9 %copy-start.3 = (bf16[4,4,5,64]{3,1,2,0:T(4,128)(2,1)S(1)}, bf16[4,4,5,64]{3,1,2,0:T(4,128)(2,1)}, u32[]{:S(2)}) copy-start(bf16[4,4,5,64]{3,1,2,0:T(4,128)(2,1)} %param.9) | copy-start | bytes 30724
  8.1 14.2 %collective-permute-start = (bf16[2,32,256]{2,1,0:T(8,128)(2,1)S(1)}, bf16[2,32,256]{2,1,0:T(8,128)(2,1)S(1)}, u32[]{:S(2)}, u32[]{:S(2)}) collective-permute-start(bf16[2,32,256]{2,1,0:T(8,128)(2,1)S(1)} %get-tuple-element.12), channel_id=1, source_target_pairs={{0,8},{8,16},{16,24},{1,9},{9,17},{17,25},{2,10},{10,18},{18,26},{... | collective-permute-start | bytes 98312 | tf_op jit(solution)/shard_map/ppermute | solution.py:17
  9.5 12.8 %collective-permute-start.1 = (bf16[2,32,256]{2,1,0:T(8,128)(2,1)S(1)}, bf16[2,32,256]{2,1,0:T(8,128)(2,1)S(1)}, u32[]{:S(2)}, u32[]{:S(2)}) collective-permute-start(bf16[2,32,256]{2,1,0:T(8,128)(2,1)S(1)} %get-tuple-element.11), channel_id=1, source_target_pairs={{8,0},{16,8},{24,16},{9,1},{17,9},{25,17},{10,2},{18,10},{26,18},{... | collective-permute-start | bytes 98312 | tf_op jit(solution)/shard_map/ppermute | solution.py:19
  15.2 0.8 copy-start.2
  18.0 4.4 %copy-start.1 = (bf16[4,32,256]{2,1,0:T(8,128)(2,1)S(1)}, bf16[4,32,256]{2,1,0:T(8,128)(2,1)}, u32[]{:S(2)}) copy-start(bf16[4,32,256]{2,1,0:T(8,128)(2,1)} %param.6) | copy-start | bytes 196612
  18.0 8.6 %collective-permute-start.5 = (bf16[8,32,256]{2,1,0:T(8,128)(2,1)S(1)}, bf16[8,32,256]{2,1,0:T(8,128)(2,1)S(1)}, u32[]{:S(2)}, u32[]{:S(2)}) collective-permute-start(bf16[8,32,256]{2,1,0:T(8,128)(2,1)S(1)} %get-tuple-element.8), channel_id=1, source_target_pairs={{1,0},{2,1},{3,2},{4,3},{5,4},{6,5},{7,6},{0,7},{9,8},{10,9},{11,1... | collective-permute-start | bytes 393224 | tf_op jit(solution)/shard_map/ppermute | solution.py:29
  22.3 7.4 %collective-permute-start.4 = (bf16[8,32,256]{2,1,0:T(8,128)(2,1)S(1)}, bf16[8,32,256]{2,1,0:T(8,128)(2,1)S(1)}, u32[]{:S(2)}, u32[]{:S(2)}) collective-permute-start(bf16[8,32,256]{2,1,0:T(8,128)(2,1)S(1)} %get-tuple-element.7), channel_id=1, source_target_pairs={{7,0},{0,1},{1,2},{2,3},{3,4},{4,5},{5,6},{6,7},{15,8},{8,9},{9,10... | collective-permute-start | bytes 393224 | tf_op jit(solution)/shard_map/ppermute | solution.py:29
  22.4 7.4 %collective-permute-start.3 = (bf16[8,32,256]{2,1,0:T(8,128)(2,1)S(1)}, bf16[8,32,256]{2,1,0:T(8,128)(2,1)S(1)}, u32[]{:S(2)}, u32[]{:S(2)}) collective-permute-start(bf16[8,32,256]{2,1,0:T(8,128)(2,1)S(1)} %constant_dynamic-update-slice_fusion), channel_id=1, source_target_pairs={{1,0},{2,1},{3,2},{4,3},{5,4},{6,5},{7,6},{0,7},{9,8},{10,9},{11,1... | collective-permute-start | bytes 393224 | tf_op jit(solution)/shard_map/ppermute | solution.py:19
  26.6 6.5 %collective-permute-start.2 = (bf16[8,32,256]{2,1,0:T(8,128)(2,1)S(1)}, bf16[8,32,256]{2,1,0:T(8,128)(2,1)S(1)}, u32[]{:S(2)}, u32[]{:S(2)}) collective-permute-start(bf16[8,32,256]{2,1,0:T(8,128)(2,1)S(1)} %constant_dynamic-update-slice_fusion), channel_id=1, source_target_pairs={{0,1},{1,2},{2,3},{3,4},{4,5},{5,6},{6,7},{7,0},{8,9},{9,10},{10,1... | collective-permute-start | bytes 393224 | tf_op jit(solution)/shard_map/ppermute | solution.py:17
  35.2 7.0 %collective-permute-start.7 = (bf16[2,32,256]{2,1,0:T(8,128)(2,1)S(1)}, bf16[2,32,256]{2,1,0:T(8,128)(2,1)S(1)}, u32[]{:S(2)}, u32[]{:S(2)}) collective-permute-start(bf16[2,32,256]{2,1,0:T(8,128)(2,1)S(1)} %get-tuple-element.10), channel_id=1, source_target_pairs={{8,0},{16,8},{24,16},{9,1},{17,9},{25,17},{10,2},{18,10},{26,18},{... | collective-permute-start | bytes 98312 | tf_op jit(solution)/shard_map/ppermute | solution.py:35
  40.8 3.1 %collective-permute-start.6 = (bf16[2,32,256]{2,1,0:T(8,128)(2,1)S(1)}, bf16[2,32,256]{2,1,0:T(8,128)(2,1)S(1)}, u32[]{:S(2)}, u32[]{:S(2)}) collective-permute-start(bf16[2,32,256]{2,1,0:T(8,128)(2,1)S(1)} %get-tuple-element.9), channel_id=1, source_target_pairs={{0,8},{8,16},{16,24},{1,9},{9,17},{17,25},{2,10},{10,18},{18,26},{... | collective-permute-start | bytes 98312 | tf_op jit(solution)/shard_map/ppermute | solution.py:35
Sparse Core Ops, SparseCore 0:
  35.3 130.1 all-reduce.9
where the time goes:
time: 177 us; the launch traced here: 175 us
  waiting for transfers between devices  128 us (72%)
  starting transfers between devices  20.1 us (11%)
  between operations  14.4 us (8%)
  local copies, waits for them, and re-layouts  4.29 us (2%)
  matrix products  4.06 us (2%)
  other arithmetic  3.46 us (2%)
    psum x1, waiting for transfers between devices, per_device(): summed_grad = lax.psum(partial_grad, ('lat', 'lon'))  120 us
    ppermute x2, starting transfers between devices, extended(): lax.ppermute(head, axis, [((i + 1) % count, i) for i in range(ends)])  7.41 us
    ppermute x2, starting transfers between devices, passed_along(): return lax.ppermute(array, axis, pairs)  6.93 us
    ppermute x2, starting transfers between devices, shifted(): return lax.ppermute(block, axis, route)  4.33 us
  transfers between devices with their start and end apart: 9, of which 4 were waited for; matrix products, arithmetic and copies ran while one was open for 4% of the time, Pallas kernels for 0%

commit v1 on v0

v1 whole, which is shorter than its diff:
```python
import math

import jax
import jax.numpy as jnp
from jax import lax
from jax.sharding import PartitionSpec as P


def swap(block, axis, offset, closed):
    count = lax.axis_size(axis)
    pairs = []
    for first in range(offset, count, 2):
        second = first + 1
        if second >= count:
            if not closed:
                continue
            second %= count
        pairs += [(first, second), (second, first)]
    return lax.ppermute(block, axis, pairs)


def flip(block, axis, bit):
    count = lax.axis_size(axis)
    return lax.ppermute(block, axis, [(i, i ^ bit) for i in range(count)])


def make_filters(filter_taps, lat_ext, lon_count):
    lat_reach = filter_taps.shape[2] // 2
    half_width = filter_taps.shape[3] // 2
    lat_dist = jnp.abs(jnp.arange(filter_taps.shape[2], dtype=jnp.int32) - lat_reach)
    lon_dist = jnp.abs(jnp.arange(filter_taps.shape[3], dtype=jnp.int32) - half_width)
    support = (lat_dist[None, :, None] < lat_ext[:, None, None]) & (
        lon_dist[None, None, :] < lon_count[:, None, None]
    )
    support_size = ((2 * lat_ext - 1) * (2 * lon_count - 1)).astype(jnp.float32)
    row_scale = lax.rsqrt(support_size)
    masked = (
        filter_taps.astype(jnp.float32)
        * support[:, None].astype(jnp.float32)
        * row_scale[:, None, None, None]
    )
    return masked.astype(jnp.bfloat16)


def band_matrix(taps, lon_width, lead):
    leading = taps.shape[:-1]
    padded = jnp.concatenate(
        [
            jnp.zeros(leading + (lead,), taps.dtype),
            taps,
            jnp.zeros(leading + (lon_width + 1 - lead,), taps.dtype),
        ],
        axis=-1,
    )
    repeated = jnp.tile(padded, (1,) * len(leading) + (lon_width,))
    return repeated[..., : lon_width * 3 * lon_width].reshape(leading + (lon_width, 3 * lon_width))


def halves(block, bit_set):
    half = block.shape[0] // 2
    keep = lax.dynamic_slice_in_dim(block, bit_set * half, half, 0)
    send = lax.dynamic_slice_in_dim(block, (1 - bit_set) * half, half, 0)
    return keep, send


def all_reduce(partial):
    lat, lon = lax.axis_index("lat"), lax.axis_index("lon")
    lat_bits = [1 << b for b in range(lax.axis_size("lat").bit_length() - 1)]
    lon_bits = [1 << b for b in range(lax.axis_size("lon").bit_length() - 1)]
    scatter = [("lat", lat, b) for b in lat_bits] + [("lon", lon, lon_bits[0])]
    value = partial
    for axis, index, bit in scatter:
        keep, send = halves(value, (index // bit) % 2)
        got = flip(send.astype(jnp.bfloat16), axis, bit)
        value = keep + got.astype(jnp.float32)
    for bit in lon_bits[1:]:
        mine = value.astype(jnp.bfloat16)
        got = flip(mine, "lon", bit)
        value = mine.astype(jnp.float32) + got.astype(jnp.float32)
    whole = value.astype(jnp.bfloat16)
    for axis, index, bit in scatter[::-1]:
        got = flip(whole, axis, bit)
        upper = (index // bit) % 2 == 1
        whole = jnp.concatenate([jnp.where(upper, got, whole), jnp.where(upper, whole, got)], axis=0)
    return whole


def per_device(features, cotangent, weight, filter_taps, lat_ext, lon_count):
    row_count, lon_width, channels = features.shape
    basis_count = weight.shape[0]
    lat_taps = filter_taps.shape[2]
    lat_reach = lat_taps // 2
    lat, lon = lax.axis_index("lat"), lax.axis_index("lon")
    filters = make_filters(filter_taps, lat_ext, lon_count)

    own = jnp.concatenate([features, cotangent], axis=0)
    far = swap(own, "lon", 1, True)
    near = swap(own, "lon", 0, True)
    lon_even = lon % 2 == 0
    west = jnp.where(lon_even, far, near)
    east = jnp.where(lon_even, near, far)
    strip = jnp.concatenate([west, own, east], axis=1).reshape(
        2, row_count, 3 * lon_width, channels
    )

    lat_even = lat % 2 == 0

    def edge(array, axis, bottom):
        start = jnp.where(bottom, row_count - lat_reach, 0)
        return lax.dynamic_slice_in_dim(array, start, lat_reach, axis)

    filter_size = lat_reach * basis_count * lat_taps * filter_taps.shape[3]
    filter_rows = -(-filter_size // (16 * channels)) * 16

    def message(bottom):
        cells = edge(strip, 1, bottom).reshape(-1, channels)
        taps = edge(filters, 0, bottom).reshape(-1)
        taps = jnp.pad(taps, (0, filter_rows * channels - filter_size)).reshape(-1, channels)
        return jnp.concatenate([cells, taps], axis=0)

    across = swap(message(jnp.logical_not(lat_even)), "lat", 1, False)
    beside = swap(message(lat_even), "lat", 0, False)
    north = jnp.where(lat_even, across, beside)
    south = jnp.where(lat_even, beside, across)

    def unpack(rows):
        cells = rows[:-filter_rows].reshape(2, lat_reach, 3 * lon_width, channels)
        taps = rows[-filter_rows:].reshape(-1)[:filter_size]
        return cells, taps.reshape((lat_reach,) + filter_taps.shape[1:])

    north_cells, north_taps = unpack(north)
    south_cells, south_taps = unpack(south)
    window = jnp.concatenate([north_cells, strip, south_cells], axis=1)
    all_taps = jnp.concatenate([north_taps, filters, south_taps], axis=0)

    banded = band_matrix(filters, lon_width, 0)
    patches = jnp.stack([window[0, e : e + row_count] for e in range(lat_taps)], axis=1)
    basis_f32 = jnp.einsum("okejm,oemc->ojkc", banded, patches, preferred_element_type=jnp.float32)
    flat_out = basis_f32.astype(jnp.bfloat16).reshape(row_count * lon_width, basis_count * channels)
    flat_weight = weight.reshape(basis_count * channels, channels)
    flat_cot = cotangent.reshape(row_count * lon_width, channels)
    partial_grad = lax.dot_general(
        flat_out, flat_cot, (((0,), (0,)), ((), ())), preferred_element_type=jnp.float32
    )
    total_cells = row_count * lax.axis_size("lat") * lon_width * lax.axis_size("lon")
    weight_grad = all_reduce(partial_grad * (1.0 / math.sqrt(total_cells)))
    weight_grad = weight_grad.astype(jnp.float32).reshape(basis_count, channels, channels)

    output = jnp.dot(flat_out, flat_weight, preferred_element_type=jnp.float32).astype(jnp.bfloat16)
    output = output.reshape(row_count, lon_width, channels)

    turned = jnp.stack(
        [all_taps[lat_taps - 1 - e : lat_taps - 1 - e + row_count, :, e] for e in range(lat_taps)], axis=2
    )[..., ::-1]
    grad_banded = band_matrix(turned, lon_width, 1)
    grad_patches = jnp.stack(
        [window[1, lat_taps - 1 - e : lat_taps - 1 - e + row_count] for e in range(lat_taps)], axis=1
    )
    spread = jnp.einsum(
        "okejm,oemc->ojkc", grad_banded, grad_patches, preferred_element_type=jnp.float32
    ).astype(jnp.bfloat16)
    turned_weight = jnp.swapaxes(weight, 1, 2).reshape(basis_count * channels, channels)
    field_grad = jnp.dot(
        spread.reshape(row_count * lon_width, basis_count * channels),
        turned_weight,
        preferred_element_type=jnp.float32,
    ).astype(jnp.bfloat16)
    field_grad = field_grad.reshape(row_count, lon_width, channels)
    return (output, field_grad, weight_grad)


def solution(mesh):
    in_specs = (
        P("lat", "lon", None),
        P("lat", "lon", None),
        P(),
        P("lat", None, None, None),
        P("lat"),
        P("lat"),
    )
    out_specs = (P("lat", "lon", None), P("lat", "lon", None), P())
    return jax.shard_map(
        per_device, mesh=mesh, in_specs=in_specs, out_specs=out_specs, check_vma=False
    )
```

time: 177 us -> 61.3 us (0.35)
  the two profiles are of different devices: /device:TPU:3 before, /device:TPU:1 now
where the time goes in v1:
time: 61.3 us; the launch traced here: 61 us
  waiting for transfers between devices  21 us (34%)
  starting transfers between devices  19.7 us (32%)
  local copies, waits for them, and re-layouts  8.68 us (14%)
  other arithmetic  6.52 us (11%)
  matrix products  3.93 us (6%)
  between operations  1.2 us (2%)
    ppermute x8, waiting for transfers between devices, flip(): return lax.ppermute(block, axis, [(i, i ^ bit) for i in range(count)])  14 us
    ppermute x8, starting transfers between devices, flip(): return lax.ppermute(block, axis, [(i, i ^ bit) for i in range(count)])  10.9 us
    ppermute x4, starting transfers between devices, swap(): return lax.ppermute(block, axis, pairs)  8.74 us
    ppermute x4, waiting for transfers between devices, swap(): return lax.ppermute(block, axis, pairs)  7.04 us
    another operation x4, local copies, waits for them, and re-layouts, band_matrix(): repeated = jnp.tile(padded, (1,) * len(leading) + (lon_width,))  3.79 us
    unnamed x17, local copies, waits for them, and re-layouts  2.31 us
    unnamed x9, other arithmetic  2.15 us
    dot_general x1, matrix products, per_device(): jnp.einsum('okejm,oemc->ojkc', grad_banded, grad_patches, preferred_eleme...  1.54 us
  transfers between devices with their start and end apart: 12, of which 10 were waited for; matrix products, arithmetic and copies ran while one was open for 21% of the time, Pallas kernels for 0%

profile of v1, /device:TPU:1, one launch (start us, length us, event | category | flops | bytes accessed | tf_op | source)
XLA Modules:
  0.0 61.0 jit_solution(17119441759554167374)
XLA Ops:
  0.6 0.9 %constant_dynamic-update-slice_fusion.1 = bf16[8,32,256]{2,1,0:T(8,128)(2,1)S(1)} fusion(bf16[4,32,256]{2,1,0:T(8,128)(2,1)} %param.6), kind=kLoop, calls=%fused_computation.78 | loop fusion | bytes 131072
  1.5 0.0 copy-start.4
  1.6 0.0 copy-start.2
  1.6 5.2 %collective-permute-start = (bf16[8,32,256]{2,1,0:T(8,128)(2,1)S(1)}, bf16[8,32,256]{2,1,0:T(8,128)(2,1)S(1)}, u32[]{:S(2)}, u32[]{:S(2)}) collective-permute-start(bf16[8,32,256]{2,1,0:T(8,128)(2,1)S(1)} %constant_dynamic-update-slice_fusion), channel_id=1, source_target_pairs={{1,2},{2,1},{3,4},{4,3},{5,6},{6,5},{7,0},{0,7},{9,10},{10,9},{11,... | collective-permute-start | bytes 393224 | tf_op jit(solution)/shard_map/ppermute | solution.py:19
  6.8 0.1 broadcast_compare_fusion
  6.9 0.1 broadcast_compare_fusion.1
  6.9 0.1 and_convert_fusion
  7.0 0.1 multiply_convert_fusion
  7.1 0.1 reshape.169
  7.2 0.1 reshape.166
  7.4 2.6 %collective-permute-done = bf16[8,32,256]{2,1,0:T(8,128)(2,1)S(1)} collective-permute-done((bf16[8,32,256]{2,1,0:T(8,128)(2,1)S(1)}, bf16[8,32,256]{2,1,0:T(8,128)(2,1)S(1)}, u32[]{:S(2)}, u32[]{:S(2)}) %collective-permute-start) | collective-permute-done | bytes 131104 | tf_op jit(solution)/shard_map/ppermute | solution.py:19
  10.0 3.5 %collective-permute-done.1 = bf16[8,32,256]{2,1,0:T(8,128)(2,1)S(1)} collective-permute-done((bf16[8,32,256]{2,1,0:T(8,128)(2,1)S(1)}, bf16[8,32,256]{2,1,0:T(8,128)(2,1)S(1)}, u32[]{:S(2)}, u32[]{:S(2)}) %collective-permute-start.1) | collective-permute-done | bytes 131104 | tf_op jit(solution)/shard_map/ppermute | solution.py:19
  13.6 0.6 collective-permute-start.3
  14.2 0.7 %pad_maximum_fusion.3 = bf16[400,256]{1,0:T(8,128)(2,1)} fusion(bf16[16,256]{1,0:T(8,128)(2,1)S(1)} %reshape.167, bf16[384,256]{1,0:T(8,128)(2,1)S(1)} %bitcast.144), kind=kLoop, calls=%fused_computation.33 | loop fusion | flops 409600 | bytes 409600 | tf_op jit(solution)/shard_map/concatenate | solution.py:119
  14.9 3.0 %collective-permute-start.2 = (bf16[400,256]{1,0:T(8,128)(2,1)}, bf16[400,256]{1,0:T(8,128)(2,1)}, u32[]{:S(2)}, u32[]{:S(2)}) collective-permute-start(bf16[400,256]{1,0:T(8,128)(2,1)} %pad_maximum_fusion.3), channel_id=1, source_target_pairs={{8,16},{16,8},{9,17},{17,9},{10,18},{18,10},{11,19},{19,11},{12,20... | collective-permute-start | bytes 614408 | tf_op jit(solution)/shard_map/ppermute | solution.py:19
  18.0 0.1 tile.8
  18.1 1.8 %tile.9 = bf16[4,4,5,3104]{3,1,2,0:T(4,128)(2,1)S(1)} reshape(bf16[4,4,5,32,97]{4,3,1,2,0:T(8,128)(2,1)S(1)} %tile.8) | data formatting | bytes 993280 | tf_op jit(solution)/shard_map/tile | solution.py:55
  19.9 0.2 slice.115
  20.1 0.0 copy-start
  20.1 0.5 reshape.173
  20.6 0.1 pad.18.clone
  20.7 0.4 copy-done
  21.1 0.2 copy.29
  21.4 0.9 %collective-permute-done.2 = bf16[400,256]{1,0:T(8,128)(2,1)} collective-permute-done((bf16[400,256]{1,0:T(8,128)(2,1)}, bf16[400,256]{1,0:T(8,128)(2,1)}, u32[]{:S(2)}, u32[]{:S(2)}) %collective-permute-start.2) | collective-permute-done | bytes 204832 | tf_op jit(solution)/shard_map/ppermute | solution.py:19
  22.3 1.1 %broadcast_select_fusion.2 = (bf16[400,256]{1,0:T(8,128)(2,1)S(1)}, bf16[400,256]{1,0:T(8,128)(2,1)S(1)}) fusion(bf16[400,256]{1,0:T(8,128)(2,1)} %collective-permute-done.3, bf16[400,256]{1,0:T(8,128)(2,1)} %collective-permute-done.2, pred[]{:T(512)S(6)} %eq.24), kind=kLoop, calls=%fused_computation.35 | loop fusion | flops 204800 | bytes 819201 | tf_op jit(solution)/shard_map/jit(_where)/select_n | solution.py:124
  23.5 0.7 %fusion.9 = bf16[4,5,96,256]{3,2,0,1:T(8,128)(2,1)} fusion(bf16[2,4,96,256]{3,2,1,0:T(8,128)(2,1)S(1)} %bitcast.122, bf16[2,2,96,256]{3,2,1,0:T(8,128)(2,1)S(1)} %bitcast.132), kind=kLoop, calls=%fused_computation.39 | loop fusion | flops 393215 | bytes 786432
  24.2 0.3 fusion.2
  24.5 0.2 copy.23
  24.8 0.1 reshape.177
  24.9 0.7 %fusion.29 = bf16[4,5,96,256]{3,2,0,1:T(8,128)(2,1)} fusion(bf16[4,5,96,256]{3,2,0,1:T(8,128)(2,1)} %fusion.9, bf16[2,2,96,256]{3,2,1,0:T(8,128)(2,1)S(1)} %bitcast.135, bf16[2,4,96,256]{3,2,1,0:T(8,128)(2,1)S(1)} %bitcast.125), kind=kLoop, calls=%fused_computation.62 | loop fusion | flops 393216 | bytes 786432
  25.6 0.3 convolution_multiply_fusion
  26.0 0.1 collective-permute-start.4
  26.1 0.7 %fusion.27 = bf16[4,5,96,256]{3,2,0,1:T(8,128)(2,1)} fusion(bf16[4,5,96,256]{3,2,0,1:T(8,128)(2,1)} %fusion.29, bf16[8,96,256]{2,1,0:T(8,128)(2,1)S(1)} %pad_maximum_fusion.1), kind=kLoop, calls=%fused_computation.59 | loop fusion | bytes 393216
  26.8 0.8 %collective-permute-done.4 = bf16[512,256]{1,0:T(8,128)(2,1)S(1)} collective-permute-done((bf16[512,256]{1,0:T(8,128)(2,1)S(1)}, bf16[512,256]{1,0:T(8,128)(2,1)S(1)}, u32[]{:S(2)}, u32[]{:S(2)}) %collective-permute-start.4) | collective-permute-done | bytes 262176 | tf_op jit(solution)/shard_map/ppermute | solution.py:24
  27.6 0.1 convert_add_fusion
  27.7 0.9 %collective-permute-start.5 = (bf16[256,256]{1,0:T(8,128)(2,1)S(1)}, bf16[256,256]{1,0:T(8,128)(2,1)S(1)}, u32[]{:S(2)}, u32[]{:S(2)}) collective-permute-start(bf16[256,256]{1,0:T(8,128)(2,1)S(1)} %dynamic-slice_convert_fusion.1), channel_id=1, source_target_pairs={{0,16},{8,24},{16,0},{24,8},{1,17},{9,25},{17,1},{25,9},{2,18},{10... | collective-permute-start | bytes 393224 | tf_op jit(solution)/shard_map/ppermute | solution.py:24
  28.6 0.1 reshape.178
  28.7 4.0 %collective-permute-done.5 = bf16[256,256]{1,0:T(8,128)(2,1)S(1)} collective-permute-done((bf16[256,256]{1,0:T(8,128)(2,1)S(1)}, bf16[256,256]{1,0:T(8,128)(2,1)S(1)}, u32[]{:S(2)}, u32[]{:S(2)}) %collective-permute-start.5) | collective-permute-done | bytes 131104 | tf_op jit(solution)/shard_map/ppermute | solution.py:24
  32.7 0.1 collective-permute-start.6
  32.8 0.1 rev.3
  33.0 3.0 %collective-permute-done.6 = bf16[128,256]{1,0:T(8,128)(2,1)S(1)} collective-permute-done((bf16[128,256]{1,0:T(8,128)(2,1)S(1)}, bf16[128,256]{1,0:T(8,128)(2,1)S(1)}, u32[]{:S(2)}, u32[]{:S(2)}) %collective-permute-start.6) | collective-permute-done | bytes 65568 | tf_op jit(solution)/shard_map/ppermute | solution.py:24
  35.9 0.1 collective-permute-start.7
  36.0 0.1 maximum_maximum_fusion
  36.1 0.1 tile.20
  36.2 1.8 %tile.21 = bf16[4,4,5,3104]{3,1,2,0:T(4,128)(2,1)S(1)} reshape(bf16[4,4,5,32,97]{4,3,1,2,0:T(8,128)(2,1)S(1)} %tile.20) | data formatting | bytes 993280 | tf_op jit(solution)/shard_map/tile | solution.py:55
  38.0 0.2 slice.124
  38.2 0.5 reshape.179
  38.7 0.4 collective-permute-done.7
  39.1 1.4 %collective-permute-start.8 = (bf16[128,256]{1,0:T(8,128)(2,1)S(1)}, bf16[128,256]{1,0:T(8,128)(2,1)S(1)}, u32[]{:S(2)}, u32[]{:S(2)}) collective-permute-start(bf16[128,256]{1,0:T(8,128)(2,1)S(1)} %add_convert_fusion.1), channel_id=1, source_target_pairs={{0,4},{1,5},{2,6},{3,7},{4,0},{5,1},{6,2},{7,3},{8,12},{9,13},{10,... | collective-permute-start | bytes 196616 | tf_op jit(solution)/shard_map/ppermute | solution.py:24
  40.5 0.7 %fusion.18 = bf16[4,5,96,256]{3,2,0,1:T(8,128)(2,1)} fusion(bf16[4,5,96,256]{3,2,0,1:T(8,128)(2,1)} %fusion.27, bf16[2,4,96,256]{3,2,1,0:T(8,128)(2,1)S(1)} %bitcast.126, bf16[2,2,96,256]{3,2,1,0:T(8,128)(2,1)S(1)} %bitcast.130), kind=kLoop, calls=%fused_computation.48 | loop fusion | flops 393216 | bytes 786432
  41.2 2.0 %collective-permute-done.8 = bf16[128,256]{1,0:T(8,128)(2,1)S(1)} collective-permute-done((bf16[128,256]{1,0:T(8,128)(2,1)S(1)}, bf16[128,256]{1,0:T(8,128)(2,1)S(1)}, u32[]{:S(2)}, u32[]{:S(2)}) %collective-permute-start.8) | collective-permute-done | bytes 65568 | tf_op jit(solution)/shard_map/ppermute | solution.py:24
  43.2 1.0 %collective-permute-start.9 = (bf16[128,256]{1,0:T(8,128)(2,1)S(1)}, bf16[128,256]{1,0:T(8,128)(2,1)S(1)}, u32[]{:S(2)}, u32[]{:S(2)}) collective-permute-start(bf16[128,256]{1,0:T(8,128)(2,1)S(1)} %add_convert_fusion), channel_id=1, source_target_pairs={{0,1},{1,0},{2,3},{3,2},{4,5},{5,4},{6,7},{7,6},{8,9},{9,8},{10,11... | collective-permute-start | bytes 196616 | tf_op jit(solution)/shard_map/ppermute | solution.py:24
  44.2 0.7 %fusion.26 = bf16[4,5,96,256]{3,2,0,1:T(8,128)(2,1)} fusion(bf16[4,5,96,256]{3,2,0,1:T(8,128)(2,1)} %fusion.18, bf16[2,4,96,256]{3,2,1,0:T(8,128)(2,1)S(1)} %bitcast.127, bf16[2,2,96,256]{3,2,1,0:T(8,128)(2,1)S(1)} %bitcast.131), kind=kLoop, calls=%fused_computation.57 | loop fusion | flops 393216 | bytes 786432 | tf_op jit(solution)/shard_map/stack | solution.py:156
  44.9 1.8 %collective-permute-done.9 = bf16[128,256]{1,0:T(8,128)(2,1)S(1)} collective-permute-done((bf16[128,256]{1,0:T(8,128)(2,1)S(1)}, bf16[128,256]{1,0:T(8,128)(2,1)S(1)}, u32[]{:S(2)}, u32[]{:S(2)}) %collective-permute-start.9) | collective-permute-done | bytes 65568 | tf_op jit(solution)/shard_map/ppermute | solution.py:24
  46.8 0.4 collective-permute-start.10
  47.1 1.5 %fusion.3 = bf16[4,32,4,256]{3,1,2,0:T(8,128)(2,1)S(1)} fusion(bf16[4,4,5,32,96]{4,3,1,2,0:T(8,128)(2,1)S(1)} %reshape.179, bf16[4,5,96,256]{3,2,0,1:T(8,128)(2,1)} %fusion.26), kind=kOutput, calls=%fused_computation.6 | convolution fusion | flops 125960192 | bytes 1736704 | tf_op jit(solution)/shard_map/okejm,oemc->ojkc/dot_general | solution.py:159
  48.7 2.0 %collective-permute-done.10 = bf16[256,256]{1,0:T(8,128)(2,1)S(1)} collective-permute-done((bf16[256,256]{1,0:T(8,128)(2,1)S(1)}, bf16[256,256]{1,0:T(8,128)(2,1)S(1)}, u32[]{:S(2)}, u32[]{:S(2)}) %collective-permute-start.10) | collective-permute-done | bytes 131104 | tf_op jit(solution)/shard_map/ppermute | solution.py:24
  50.7 7.1 %collective-permute-start.11 = (bf16[512,256]{1,0:T(8,128)(2,1)S(1)}, bf16[512,256]{1,0:T(8,128)(2,1)S(1)}, u32[]{:S(2)}, u32[]{:S(2)}) collective-permute-start(bf16[512,256]{1,0:T(8,128)(2,1)S(1)} %pad_maximum_fusion.2), channel_id=1, source_target_pairs={{0,8},{8,0},{16,24},{24,16},{1,9},{9,1},{17,25},{25,17},{2,10},{10... | collective-permute-start | bytes 786440 | tf_op jit(solution)/shard_map/ppermute | solution.py:24
  57.8 0.9 %convolution_convert_fusion.1 = bf16[128,256]{1,0:T(8,128)(2,1)} fusion(bf16[128,1024]{1,0:T(8,128)(2,1)S(1)} %bitcast.137, bf16[1024,256]{1,0:T(8,128)(2,1)S(1)} %bitcast.139), kind=kOutput, calls=%fused_computation.8 | convolution fusion | flops 67141632 | bytes 851968 | tf_op jit(solution)/shard_map/dot_general | solution.py:149
  58.7 0.2 copy.28
  58.9 0.9 %convolution_convert_fusion = bf16[128,256]{1,0:T(8,128)(2,1)} fusion(bf16[128,1024]{1,0:T(8,128)(2,1)S(1)} %bitcast.141, bf16[1024,256]{1,0:T(8,128)(2,1)S(1)} %bitcast.140), kind=kOutput, calls=%fused_computation.7 | convolution fusion | flops 67141632 | bytes 851968 | tf_op jit(solution)/shard_map/dot_general | solution.py:163
  59.8 0.0 collective-permute-done.11
  59.8 0.1 broadcast_select_fusion.1
  59.9 1.1 %convert.1 = f32[4,256,256]{2,1,0:T(8,128)} convert(bf16[4,256,256]{2,1,0:T(8,128)(2,1)S(1)} %bitcast.138) | non-fusion elementwise | flops 262144 | bytes 1572864 | tf_op jit(solution)/shard_map/convert_element_type | solution.py:147
  (56 shorter events, 0.8 us)
Async XLA Ops:
  0.6 0.9 %copy-start.1 = (bf16[4,32,256]{2,1,0:T(8,128)(2,1)S(1)}, bf16[4,32,256]{2,1,0:T(8,128)(2,1)}, u32[]{:S(2)}) copy-start(bf16[4,32,256]{2,1,0:T(8,128)(2,1)} %param.7) | copy-start | bytes 196612
  1.5 5.2 %copy-start.3 = (s32[4]{0:T(128)S(1)}, s32[4]{0:T(128)}, u32[]{:S(2)}) copy-start(s32[4]{0:T(128)} %param.11) | copy-start | bytes 52
  1.5 5.2 %copy-start.4 = (s32[4]{0:T(128)S(1)}, s32[4]{0:T(128)}, u32[]{:S(2)}) copy-start(s32[4]{0:T(128)} %param.10) | copy-start | bytes 52
  1.6 5.5 %copy-start.2 = (bf16[4,4,5,64]{3,1,2,0:T(4,128)(2,1)S(1)}, bf16[4,4,5,64]{3,1,2,0:T(4,128)(2,1)}, u32[]{:S(2)}) copy-start(bf16[4,4,5,64]{3,1,2,0:T(4,128)(2,1)} %param.9) | copy-start | bytes 30724
  1.6 8.4 %collective-permute-start = (bf16[8,32,256]{2,1,0:T(8,128)(2,1)S(1)}, bf16[8,32,256]{2,1,0:T(8,128)(2,1)S(1)}, u32[]{:S(2)}, u32[]{:S(2)}) collective-permute-start(bf16[8,32,256]{2,1,0:T(8,128)(2,1)S(1)} %constant_dynamic-update-slice_fusion), channel_id=1, source_target_pairs={{1,2},{2,1},{3,4},{4,3},{5,6},{6,5},{7,0},{0,7},{9,10},{10,9},{11,... | collective-permute-start | bytes 393224 | tf_op jit(solution)/shard_map/ppermute | solution.py:19
  6.7 6.8 %collective-permute-start.1 = (bf16[8,32,256]{2,1,0:T(8,128)(2,1)S(1)}, bf16[8,32,256]{2,1,0:T(8,128)(2,1)S(1)}, u32[]{:S(2)}, u32[]{:S(2)}) collective-permute-start(bf16[8,32,256]{2,1,0:T(8,128)(2,1)S(1)} %constant_dynamic-update-slice_fusion), channel_id=1, source_target_pairs={{0,1},{1,0},{2,3},{3,2},{4,5},{5,4},{6,7},{7,6},{8,9},{9,8},{10,11... | collective-permute-start | bytes 393224 | tf_op jit(solution)/shard_map/ppermute | solution.py:19
  13.6 7.7 %collective-permute-start.3 = (bf16[400,256]{1,0:T(8,128)(2,1)S(1)}, bf16[400,256]{1,0:T(8,128)(2,1)}, u32[]{:S(2)}, u32[]{:S(2)}) collective-permute-start(bf16[400,256]{1,0:T(8,128)(2,1)S(1)} %pad_maximum_fusion.4), channel_id=1, source_target_pairs={{0,8},{8,0},{16,24},{24,16},{1,9},{9,1},{17,25},{25,17},{2,10},{10... | collective-permute-start | bytes 614408 | tf_op jit(solution)/shard_map/ppermute | solution.py:19
  14.9 7.4 %collective-permute-start.2 = (bf16[400,256]{1,0:T(8,128)(2,1)}, bf16[400,256]{1,0:T(8,128)(2,1)}, u32[]{:S(2)}, u32[]{:S(2)}) collective-permute-start(bf16[400,256]{1,0:T(8,128)(2,1)} %pad_maximum_fusion.3), channel_id=1, source_target_pairs={{8,16},{16,8},{9,17},{17,9},{10,18},{18,10},{11,19},{19,11},{12,20... | collective-permute-start | bytes 614408 | tf_op jit(solution)/shard_map/ppermute | solution.py:19
  20.1 1.0 %copy-start = (bf16[4,256,256]{2,1,0:T(8,128)(2,1)S(1)}, bf16[4,256,256]{2,1,0:T(8,128)(2,1)}, u32[]{:S(2)}) copy-start(bf16[4,256,256]{2,1,0:T(8,128)(2,1)} %param.8) | copy-start | bytes 1572868
  26.0 1.6 %collective-permute-start.4 = (bf16[512,256]{1,0:T(8,128)(2,1)S(1)}, bf16[512,256]{1,0:T(8,128)(2,1)S(1)}, u32[]{:S(2)}, u32[]{:S(2)}) collective-permute-start(bf16[512,256]{1,0:T(8,128)(2,1)S(1)} %dynamic-slice_convert_fusion), channel_id=1, source_target_pairs={{0,8},{8,0},{16,24},{24,16},{1,9},{9,1},{17,25},{25,17},{2,10},{10... | collective-permute-start | bytes 786440 | tf_op jit(solution)/shard_map/ppermute | solution.py:24
  27.7 5.0 %collective-permute-start.5 = (bf16[256,256]{1,0:T(8,128)(2,1)S(1)}, bf16[256,256]{1,0:T(8,128)(2,1)S(1)}, u32[]{:S(2)}, u32[]{:S(2)}) collective-permute-start(bf16[256,256]{1,0:T(8,128)(2,1)S(1)} %dynamic-slice_convert_fusion.1), channel_id=1, source_target_pairs={{0,16},{8,24},{16,0},{24,8},{1,17},{9,25},{17,1},{25,9},{2,18},{10... | collective-permute-start | bytes 393224 | tf_op jit(solution)/shard_map/ppermute | solution.py:24
  32.7 3.2 %collective-permute-start.6 = (bf16[128,256]{1,0:T(8,128)(2,1)S(1)}, bf16[128,256]{1,0:T(8,128)(2,1)S(1)}, u32[]{:S(2)}, u32[]{:S(2)}) collective-permute-start(bf16[128,256]{1,0:T(8,128)(2,1)S(1)} %dynamic-slice_convert_fusion.2), channel_id=1, source_target_pairs={{0,1},{1,0},{2,3},{3,2},{4,5},{5,4},{6,7},{7,6},{8,9},{9,8},{10,11... | collective-permute-start | bytes 196616 | tf_op jit(solution)/shard_map/ppermute | solution.py:24
  35.9 3.2 %collective-permute-start.7 = (bf16[128,256]{1,0:T(8,128)(2,1)S(1)}, bf16[128,256]{1,0:T(8,128)(2,1)S(1)}, u32[]{:S(2)}, u32[]{:S(2)}) collective-permute-start(bf16[128,256]{1,0:T(8,128)(2,1)S(1)} %add_convert_fusion.2), channel_id=1, source_target_pairs={{0,2},{1,3},{2,0},{3,1},{4,6},{5,7},{6,4},{7,5},{8,10},{9,11},{10,... | collective-permute-start | bytes 196616 | tf_op jit(solution)/shard_map/ppermute | solution.py:24
  39.1 4.1 %collective-permute-start.8 = (bf16[128,256]{1,0:T(8,128)(2,1)S(1)}, bf16[128,256]{1,0:T(8,128)(2,1)S(1)}, u32[]{:S(2)}, u32[]{:S(2)}) collective-permute-start(bf16[128,256]{1,0:T(8,128)(2,1)S(1)} %add_convert_fusion.1), channel_id=1, source_target_pairs={{0,4},{1,5},{2,6},{3,7},{4,0},{5,1},{6,2},{7,3},{8,12},{9,13},{10,... | collective-permute-start | bytes 196616 | tf_op jit(solution)/shard_map/ppermute | solution.py:24
  43.2 3.5 %collective-permute-start.9 = (bf16[128,256]{1,0:T(8,128)(2,1)S(1)}, bf16[128,256]{1,0:T(8,128)(2,1)S(1)}, u32[]{:S(2)}, u32[]{:S(2)}) collective-permute-start(bf16[128,256]{1,0:T(8,128)(2,1)S(1)} %add_convert_fusion), channel_id=1, source_target_pairs={{0,1},{1,0},{2,3},{3,2},{4,5},{5,4},{6,7},{7,6},{8,9},{9,8},{10,11... | collective-permute-start | bytes 196616 | tf_op jit(solution)/shard_map/ppermute | solution.py:24
  46.8 3.9 %collective-permute-start.10 = (bf16[256,256]{1,0:T(8,128)(2,1)S(1)}, bf16[256,256]{1,0:T(8,128)(2,1)S(1)}, u32[]{:S(2)}, u32[]{:S(2)}) collective-permute-start(bf16[256,256]{1,0:T(8,128)(2,1)S(1)} %pad_maximum_fusion.7), channel_id=1, source_target_pairs={{0,16},{8,24},{16,0},{24,8},{1,17},{9,25},{17,1},{25,9},{2,18},{10... | collective-permute-start | bytes 393224 | tf_op jit(solution)/shard_map/ppermute | solution.py:24
  50.7 9.1 %collective-permute-start.11 = (bf16[512,256]{1,0:T(8,128)(2,1)S(1)}, bf16[512,256]{1,0:T(8,128)(2,1)S(1)}, u32[]{:S(2)}, u32[]{:S(2)}) collective-permute-start(bf16[512,256]{1,0:T(8,128)(2,1)S(1)} %pad_maximum_fusion.2), channel_id=1, source_target_pairs={{0,8},{8,0},{16,24},{24,16},{1,9},{9,1},{17,25},{25,17},{2,10},{10... | collective-permute-start | bytes 786440 | tf_op jit(solution)/shard_map/ppermute | solution.py:24

commit v2 on v0

v2 whole, which is shorter than its diff:
```python
import functools
import math

import jax
import jax.numpy as jnp
from jax import lax
from jax.experimental import pallas as pl
from jax.experimental.pallas import tpu as pltpu
from jax.sharding import PartitionSpec as P

LANES = 128
TAP_ROWS = 8


def shift(block, axis, by):
    count = lax.axis_size(axis)
    return lax.ppermute(block, axis, [(i, (i + by) % count) for i in range(count)])


def flip(block, axis, bit):
    count = lax.axis_size(axis)
    return lax.ppermute(block, axis, [(i, i ^ bit) for i in range(count)])


def outer_swap(block, axis):
    count = lax.axis_size(axis)
    pairs = [(i, i + 1) for i in range(1, count - 1, 2)]
    return lax.ppermute(block, axis, pairs + [(b, a) for a, b in pairs])


def make_filters(filter_taps, lat_ext, lon_count):
    lat_reach = filter_taps.shape[2] // 2
    half_width = filter_taps.shape[3] // 2
    lat_dist = jnp.abs(jnp.arange(filter_taps.shape[2], dtype=jnp.int32) - lat_reach)
    lon_dist = jnp.abs(jnp.arange(filter_taps.shape[3], dtype=jnp.int32) - half_width)
    support = (lat_dist[None, :, None] < lat_ext[:, None, None]) & (
        lon_dist[None, None, :] < lon_count[:, None, None]
    )
    support_size = ((2 * lat_ext - 1) * (2 * lon_count - 1)).astype(jnp.float32)
    row_scale = lax.rsqrt(support_size)
    masked = (
        filter_taps.astype(jnp.float32)
        * support[:, None].astype(jnp.float32)
        * row_scale[:, None, None, None]
    )
    return masked.astype(jnp.bfloat16)


class Layout:
    def __init__(self, rows, reach, width, basis, channels):
        self.rows, self.reach, self.width = rows, reach, width
        self.basis, self.channels = basis, channels
        self.taps = 2 * reach + 1
        self.own = rows + reach
        self.total = 3 * rows + 2 * reach
        self.domain = 2 * rows + reach
        self.strip = 3 * width
        self.cells = 2 * rows * self.strip
        self.edge_cells = 2 * reach * self.strip

    def places(self, even):
        partner = jnp.where(even, self.own + self.rows, self.own - self.rows)
        outer = jnp.where(even, self.own - self.reach, self.own + self.rows)
        first = jnp.where(even, self.own - self.reach, self.own - self.rows)
        return partner, outer, first


def fill(lay, even, strip, partner, outer, window, taps):
    at_partner, at_outer, _ = lay.places(even)
    rows, reach, cols = lay.rows, lay.reach, lay.strip
    window[...] = jnp.zeros_like(window)
    for field in range(2):
        for row in range(rows):
            window[field, lay.own + row, :cols] = strip[field, row]
            start = (field * rows + row) * cols
            window[field, at_partner + row, :cols] = partner[start : start + cols]
        for row in range(reach):
            start = (field * reach + row) * cols
            window[field, at_outer + row, :cols] = outer[start : start + cols]


def fill_taps(lay, even, own, partner, outer, taps):
    at_partner, at_outer, _ = lay.places(even)
    per_row = lay.basis * TAP_ROWS
    taps[...] = jnp.zeros_like(taps)
    for row in range(lay.rows):
        taps[lay.own + row] = own[row * per_row : (row + 1) * per_row].astype(jnp.float32)
        start = lay.cells + row * per_row
        taps[at_partner + row] = partner[start : start + per_row].astype(jnp.float32)
    for row in range(lay.reach):
        start = lay.edge_cells + row * per_row
        taps[at_outer + row] = outer[start : start + per_row].astype(jnp.float32)


def weight_kernel(lay, scale, strip, filters, partner, outer, grad, window, taps, basis_out):
    lat, lon = lax.axis_index("lat"), lax.axis_index("lon")
    even, lon_even = lat % 2 == 0, lon % 2 == 0
    mine = (lat % 2) * 2 + lon % 2
    fill(lay, even, strip, partner, outer, window, taps)
    fill_taps(lay, even, filters, partner, outer, taps)
    _, _, first = lay.places(even)
    width, reach = lay.width, lay.reach
    lane = lax.broadcasted_iota(jnp.int32, (1, LANES), 1)
    keep_west = jnp.where((lane < width) & lon_even, 0.0, 1.0)
    keep_east = jnp.where((lane >= 2 * width) & jnp.logical_not(lon_even), 0.0, 1.0)
    at_mine = pl.multiple_of(mine * TAP_ROWS, TAP_ROWS)
    for row in range(lay.domain):
        blocks = []
        lines = taps[first + row, pl.ds(at_mine, TAP_ROWS), :LANES]
        for e in range(lay.taps):
            line = lines[e : e + 1]
            source = row + e - reach
            if row < reach and 0 <= source < reach:
                line = jnp.where(even, 0.0, line)
            tail = lay.domain - reach
            if row >= tail and tail <= source < lay.domain:
                line = jnp.where(even, line, 0.0)
            spread = jnp.broadcast_to(line, (width, LANES))
            middle = pltpu.roll(spread, 0, 1, stride=1, stride_axis=0)
            west = pltpu.roll(middle, LANES - width, 1) * keep_west
            east = pltpu.roll(middle, width, 1) * keep_east
            blocks.append(jnp.concatenate([west, middle, east], axis=0).astype(jnp.bfloat16))
        band = jnp.concatenate(blocks, axis=1)
        source = window[0, pl.ds(first + row - reach, lay.taps)].reshape(lay.taps * LANES, lay.channels)
        result = jnp.dot(band, source, preferred_element_type=jnp.float32)
        basis_out[row * lay.strip : (row + 1) * lay.strip] = result.astype(jnp.bfloat16)
    cot = window[1, pl.ds(first, lay.domain), : lay.strip].reshape(lay.domain * lay.strip, lay.channels)
    total = lax.dot_general(
        basis_out[...], cot, (((0,), (0,)), ((), ())), preferred_element_type=jnp.float32
    )
    grad[...] = (total * scale).astype(jnp.bfloat16)


def field_kernel(lay, strip, filters, partner, outer, weight, output, field_grad, window, taps, mixed):
    even = lax.axis_index("lat") % 2 == 0
    fill(lay, even, strip, partner, outer, window, taps)
    fill_taps(lay, even, filters, partner, outer, taps)
    width, reach, rows, basis = lay.width, lay.reach, lay.rows, lay.basis

    def bands(row, turned):
        blocks = []
        for n in range(lay.taps):
            at, e = (row + n - reach, lay.taps - 1 - n) if turned else (row, n)
            lanes = slice(LANES, 2 * LANES) if turned else slice(0, LANES)
            parts = []
            for k in range(basis):
                line = taps[lay.own + at, k * TAP_ROWS + e : k * TAP_ROWS + e + 1, lanes]
                spread = jnp.broadcast_to(line, (width, LANES))
                parts.append(pltpu.roll(spread, int(turned), 1, stride=1, stride_axis=0))
            blocks.append(jnp.concatenate(parts, axis=0).astype(jnp.bfloat16))
        return jnp.concatenate(blocks, axis=1)

    for field, turned, out in ((0, False, output), (1, True, field_grad)):
        for row in range(rows):
            source = window[field, lay.own + row - reach : lay.own + row + reach + 1]
            source = source.reshape(lay.taps * LANES, lay.channels)
            result = jnp.dot(bands(row, turned), source, preferred_element_type=jnp.float32)
            result = result.astype(jnp.bfloat16)
            for k in range(basis):
                mixed[k, row * width : (row + 1) * width] = result[k * width : (k + 1) * width]
        total = jnp.zeros((rows * width, lay.channels), jnp.float32)
        for k in range(basis):
            dims = (((1,), (1,)), ((), ())) if turned else (((1,), (0,)), ((), ()))
            total += lax.dot_general(mixed[k], weight[k], dims, preferred_element_type=jnp.float32)
        out[...] = total.astype(jnp.bfloat16).reshape(out.shape)


def per_device(features, cotangent, weight, filter_taps, lat_ext, lon_count):
    rows, width, channels = features.shape
    basis = weight.shape[0]
    lat_taps = filter_taps.shape[2]
    lay = Layout(rows, lat_taps // 2, width, basis, channels)
    lat, lon = lax.axis_index("lat"), lax.axis_index("lon")
    even = lat % 2 == 0

    filters = make_filters(filter_taps, lat_ext, lon_count)
    gap = jnp.zeros(filters.shape[:-1] + (LANES - filters.shape[-1],), filters.dtype)
    filters = jnp.concatenate([filters, gap, filters[..., ::-1], gap], axis=-1)
    filters = jnp.pad(filters, ((0, 0), (0, 0), (0, TAP_ROWS - lat_taps), (0, 0)))
    per_row = basis * TAP_ROWS
    filters = filters.reshape(rows * per_row, 2 * LANES)

    own = jnp.concatenate([features, cotangent], axis=0)
    west = shift(own, "lon", 1)
    east = shift(own, "lon", -1)
    strip = jnp.concatenate([west, own, east], axis=1).reshape(2, rows, lay.strip, channels)

    def edge(array, axis, size, bottom):
        start = jnp.where(bottom, array.shape[axis] - size, 0)
        return lax.dynamic_slice_in_dim(array, start, size, axis)

    outward = jnp.concatenate(
        [
            edge(strip, 1, lay.reach, jnp.logical_not(even)).reshape(-1, channels),
            edge(filters, 0, lay.reach * per_row, jnp.logical_not(even)),
        ],
        axis=0,
    )
    outer = outer_swap(outward, "lat")
    partner = flip(jnp.concatenate([strip.reshape(-1, channels), filters], axis=0), "lat", 1)

    vmem = pl.BlockSpec(memory_space=pltpu.VMEM)
    window_shape = pltpu.VMEM((2, lay.total, LANES, channels), jnp.bfloat16)
    taps_shape = pltpu.VMEM((lay.total, per_row, 2 * LANES), jnp.float32)
    total_cells = rows * lax.axis_size("lat") * width * lax.axis_size("lon")
    grad = pl.pallas_call(
        functools.partial(weight_kernel, lay, 1.0 / math.sqrt(total_cells)),
        out_shape=jax.ShapeDtypeStruct((channels, channels), jnp.bfloat16),
        in_specs=[vmem] * 4,
        out_specs=vmem,
        scratch_shapes=[
            window_shape,
            taps_shape,
            pltpu.VMEM((lay.domain * lay.strip, channels), jnp.bfloat16),
        ],
        compiler_params=pltpu.CompilerParams(vmem_limit_bytes=32 * 1024 * 1024),
        cost_estimate=pl.CostEstimate(flops=400_000_000, bytes_accessed=3_000_000, transcendentals=0),
        name="weight_partial",
    )(strip, filters, partner, outer)

    output, field_grad = pl.pallas_call(
        functools.partial(field_kernel, lay),
        out_shape=[jax.ShapeDtypeStruct(features.shape, jnp.bfloat16)] * 2,
        in_specs=[vmem] * 5,
        out_specs=[vmem] * 2,
        scratch_shapes=[
            window_shape,
            taps_shape,
            pltpu.VMEM((basis, rows * width, channels), jnp.bfloat16),
        ],
        compiler_params=pltpu.CompilerParams(vmem_limit_bytes=32 * 1024 * 1024),
        cost_estimate=pl.CostEstimate(flops=400_000_000, bytes_accessed=3_000_000, transcendentals=0),
        name="fields",
    )(strip, filters, partner, outer, weight)

    others = [("lat", 1 << b) for b in range(1, lax.axis_size("lat").bit_length() - 1)]
    others += [("lon", 1 << b) for b in range(1, lax.axis_size("lon").bit_length() - 1)]
    for axis, bit in others:
        total = grad.astype(jnp.float32) + flip(grad, axis, bit).astype(jnp.float32)
        grad = total.astype(jnp.bfloat16)
    for axis, index in (("lon", lon), ("lat", lat)):
        got = flip(grad, axis, 1)
        upper = index % 2 == 1
        grad = jnp.concatenate([jnp.where(upper, got, grad), jnp.where(upper, grad, got)], axis=0)
    weight_grad = grad.astype(jnp.float32).reshape(basis, channels, channels)
    return (output, field_grad, weight_grad)


def solution(mesh):
    in_specs = (
        P("lat", "lon", None),
        P("lat", "lon", None),
        P(),
        P("lat", None, None, None),
        P("lat"),
        P("lat"),
    )
    out_specs = (P("lat", "lon", None), P("lat", "lon", None), P())
    return jax.shard_map(
        per_device, mesh=mesh, in_specs=in_specs, out_specs=out_specs, check_vma=False
    )
```

time: 177 us -> 53.1 us (0.30)
  the two profiles are of different devices: /device:TPU:3 before, /device:TPU:1 now
where the time goes in v2:
time: 53.1 us; the launch traced here: 52.9 us
  waiting for transfers between devices  33.8 us (64%)
  starting transfers between devices  12.1 us (23%)
  Pallas kernels  3.25 us (6%)
  other arithmetic  1.83 us (3%)
  local copies, waits for them, and re-layouts  1.09 us (2%)
  between operations  0.88 us (2%)
    ppermute x6, waiting for transfers between devices, flip(): return lax.ppermute(block, axis, [(i, i ^ bit) for i in range(count)])  23.6 us
    ppermute x2, waiting for transfers between devices, shift(): lax.ppermute(block, axis, [(i, (i + by) % count) for i in range(count)])  5.82 us
    ppermute x2, starting transfers between devices, shift(): lax.ppermute(block, axis, [(i, (i + by) % count) for i in range(count)])  5.16 us
    ppermute x1, waiting for transfers between devices, outer_swap(): return lax.ppermute(block, axis, pairs + [(b, a) for a, b in pairs])  4.3 us
    ppermute x6, starting transfers between devices, flip(): return lax.ppermute(block, axis, [(i, i ^ bit) for i in range(count)])  3.91 us
    ppermute x1, starting transfers between devices, outer_swap(): return lax.ppermute(block, axis, pairs + [(b, a) for a, b in pairs])  3.03 us
    pallas_call x1, Pallas kernels, per_device(): pl.pallas_call(functools.partial(field_kernel, lay), out_shape=[jax.Shape...  1.68 us
    pallas_call x1, Pallas kernels, per_device(): pl.pallas_call(functools.partial(weight_kernel, lay, 1.0 / math.sqrt(tota...  1.58 us
  transfers between devices with their start and end apart: 9, of which 7 were waited for; matrix products, arithmetic and copies ran while one was open for 1% of the time, Pallas kernels for 3%

profile of v2, /device:TPU:1, one launch (start us, length us, event | category | flops | bytes accessed | tf_op | source)
XLA Modules:
  0.0 52.9 jit_solution(15061637722544905597)
XLA Ops:
  0.6 0.0 copy-start.1
  0.6 0.9 %constant_dynamic-update-slice_fusion.1 = bf16[8,32,256]{2,1,0:T(8,128)(2,1)S(1)} fusion(bf16[4,32,256]{2,1,0:T(8,128)(2,1)} %param.6), kind=kLoop, calls=%fused_computation.16 | loop fusion | bytes 131072
  1.5 0.0 copy-done.1
  1.5 0.0 copy-start.3
  1.5 0.0 copy-start.4
  1.6 0.0 copy-start.2
  1.6 5.2 %collective-permute-start.1 = (bf16[8,32,256]{2,1,0:T(8,128)(2,1)S(1)}, bf16[8,32,256]{2,1,0:T(8,128)(2,1)S(1)}, u32[]{:S(2)}, u32[]{:S(2)}) collective-permute-start(bf16[8,32,256]{2,1,0:T(8,128)(2,1)S(1)} %constant_dynamic-update-slice_fusion), channel_id=1, source_target_pairs={{0,7},{1,0},{2,1},{3,2},{4,3},{5,4},{6,5},{7,6},{8,15},{9,8},{10,9... | collective-permute-start | bytes 393224 | tf_op jit(solution)/shard_map/ppermute | solution.py:17
  6.7 0.0 collective-permute-start
  6.7 0.0 copy-done.3
  6.7 0.0 copy-done.4
  6.8 0.1 broadcast_compare_fusion.1
  6.8 0.1 broadcast_compare_fusion
  6.9 0.1 and_convert_fusion
  7.0 0.0 copy-done.2
  7.0 0.1 multiply_convert_fusion
  7.1 0.1 rev.3
  7.2 0.1 pad_maximum_fusion.5
  7.4 1.5 %collective-permute-done.1 = bf16[8,32,256]{2,1,0:T(8,128)(2,1)S(1)} collective-permute-done((bf16[8,32,256]{2,1,0:T(8,128)(2,1)S(1)}, bf16[8,32,256]{2,1,0:T(8,128)(2,1)S(1)}, u32[]{:S(2)}, u32[]{:S(2)}) %collective-permute-start.1) | collective-permute-done | bytes 131104 | tf_op jit(solution)/shard_map/ppermute | solution.py:17
  8.9 4.3 %collective-permute-done = bf16[8,32,256]{2,1,0:T(8,128)(2,1)S(1)} collective-permute-done((bf16[8,32,256]{2,1,0:T(8,128)(2,1)S(1)}, bf16[8,32,256]{2,1,0:T(8,128)(2,1)S(1)}, u32[]{:S(2)}, u32[]{:S(2)}) %collective-permute-start) | collective-permute-done | bytes 131104 | tf_op jit(solution)/shard_map/ppermute | solution.py:17
  13.3 2.2 %collective-permute-start.2 = (bf16[896,256]{1,0:T(8,128)(2,1)S(1)}, bf16[896,256]{1,0:T(8,128)(2,1)S(1)}, u32[]{:S(2)}, u32[]{:S(2)}) collective-permute-start(bf16[896,256]{1,0:T(8,128)(2,1)S(1)} %pad_maximum_fusion.1), channel_id=1, source_target_pairs={{0,8},{8,0},{16,24},{24,16},{1,9},{9,1},{17,25},{25,17},{2,10},{10... | collective-permute-start | bytes 1376264 | tf_op jit(solution)/shard_map/ppermute | solution.py:22
  15.5 3.0 %collective-permute-start.3 = (bf16[448,256]{1,0:T(8,128)(2,1)S(1)}, bf16[448,256]{1,0:T(8,128)(2,1)S(1)}, u32[]{:S(2)}, u32[]{:S(2)}) collective-permute-start(bf16[448,256]{1,0:T(8,128)(2,1)S(1)} %pad_maximum_fusion.4), channel_id=1, source_target_pairs={{8,16},{16,8},{9,17},{17,9},{10,18},{18,10},{11,19},{19,11},{12,20... | collective-permute-start | bytes 688136 | tf_op jit(solution)/shard_map/ppermute | solution.py:28
  18.6 4.3 %collective-permute-done.3.outer = bf16[448,256]{1,0:T(8,128)(2,1)S(1)} collective-permute-done((bf16[448,256]{1,0:T(8,128)(2,1)S(1)}, bf16[448,256]{1,0:T(8,128)(2,1)S(1)}, u32[]{:S(2)}, u32[]{:S(2)}) %collective-permute-start.3) | collective-permute-done | bytes 229408 | tf_op jit(solution)/shard_map/ppermute | solution.py:28
  22.9 0.0 collective-permute-done.2.partner
  22.9 1.6 %weight_partial.1 = bf16[256,256]{1,0:T(8,128)(2,1)S(1)} custom-call(bf16[2,4,96,256]{3,2,1,0:T(8,128)(2,1)S(1)} %bitcast.8, bf16[128,256]{1,0:T(8,128)(2,1)S(1)} %bitcast.12, bf16[896,256]{1,0:T(8,128)(2,1)S(1)} %collective-permute-done.2.partner, bf16[448,256]{1,0:T(8,128)(2,1)S(1)} %collective-permute-done.3.outer), custom_call_target="tpu_custom_call" | custom-call | flops 400000000 | bytes 3000000 | tf_op jit(solution)/shard_map/weight_partial/pallas_call | solution.py:206
  24.5 0.1 collective-permute-start.4
  24.5 5.4 %collective-permute-done.4 = bf16[256,256]{1,0:T(8,128)(2,1)S(1)} collective-permute-done((bf16[256,256]{1,0:T(8,128)(2,1)S(1)}, bf16[256,256]{1,0:T(8,128)(2,1)S(1)}, u32[]{:S(2)}, u32[]{:S(2)}) %collective-permute-start.4) | collective-permute-done | bytes 131104 | tf_op jit(solution)/shard_map/ppermute | solution.py:22
  30.0 0.1 collective-permute-start.5
  30.1 4.7 %collective-permute-done.5 = bf16[256,256]{1,0:T(8,128)(2,1)S(1)} collective-permute-done((bf16[256,256]{1,0:T(8,128)(2,1)S(1)}, bf16[256,256]{1,0:T(8,128)(2,1)S(1)}, u32[]{:S(2)}, u32[]{:S(2)}) %collective-permute-start.5) | collective-permute-done | bytes 131104 | tf_op jit(solution)/shard_map/ppermute | solution.py:22
  34.8 0.1 collective-permute-start.6
  34.9 9.1 %collective-permute-done.6 = bf16[256,256]{1,0:T(8,128)(2,1)S(1)} collective-permute-done((bf16[256,256]{1,0:T(8,128)(2,1)S(1)}, bf16[256,256]{1,0:T(8,128)(2,1)S(1)}, u32[]{:S(2)}, u32[]{:S(2)}) %collective-permute-start.6) | collective-permute-done | bytes 131104 | tf_op jit(solution)/shard_map/ppermute | solution.py:22
  44.0 0.1 collective-permute-start.7
  44.0 0.0 copy-start
  44.1 4.5 %collective-permute-done.7 = bf16[256,256]{1,0:T(8,128)(2,1)S(1)} collective-permute-done((bf16[256,256]{1,0:T(8,128)(2,1)S(1)}, bf16[256,256]{1,0:T(8,128)(2,1)S(1)}, u32[]{:S(2)}, u32[]{:S(2)}) %collective-permute-start.7) | collective-permute-done | bytes 131104 | tf_op jit(solution)/shard_map/ppermute | solution.py:22
  48.6 1.5 %collective-permute-start.8 = (bf16[512,256]{1,0:T(8,128)(2,1)S(1)}, bf16[512,256]{1,0:T(8,128)(2,1)S(1)}, u32[]{:S(2)}, u32[]{:S(2)}) collective-permute-start(bf16[512,256]{1,0:T(8,128)(2,1)S(1)} %pad_maximum_fusion.3), channel_id=1, source_target_pairs={{0,8},{8,0},{16,24},{24,16},{1,9},{9,1},{17,25},{25,17},{2,10},{10... | collective-permute-start | bytes 786440 | tf_op jit(solution)/shard_map/ppermute | solution.py:22
  50.1 0.0 copy-done
  50.1 1.7 %fields.1 = (bf16[4,32,256]{2,1,0:T(8,128)(2,1)}, bf16[4,32,256]{2,1,0:T(8,128)(2,1)}) custom-call(bf16[2,4,96,256]{3,2,1,0:T(8,128)(2,1)S(1)} %bitcast.9, bf16[128,256]{1,0:T(8,128)(2,1)S(1)} %bitcast.13, bf16[896,256]{1,0:T(8,128)(2,1)S(1)} %collective-permute-done.2.partner, bf16[448,256]{1,0:T(8,128)(2,1)S(1)} %collective-permute-done.3.outer, ...), custom_call_target="tpu_custom_call" | custom-call | flops 400000000 | bytes 3000000 | tf_op jit(solution)/shard_map/fields/pallas_call | solution.py:221
  51.7 0.0 collective-permute-done.8
  51.7 0.1 broadcast_select_fusion.1
  51.9 1.1 %convert.1 = f32[4,256,256]{2,1,0:T(8,128)} convert(bf16[4,256,256]{2,1,0:T(8,128)(2,1)S(1)} %bitcast.14) | non-fusion elementwise | flops 262144 | bytes 1572864 | tf_op jit(solution)/shard_map/convert_element_type | solution.py:245
  (18 shorter events, 0.3 us)
Async XLA Ops:
  0.6 0.9 %copy-start.1 = (bf16[4,32,256]{2,1,0:T(8,128)(2,1)S(1)}, bf16[4,32,256]{2,1,0:T(8,128)(2,1)}, u32[]{:S(2)}) copy-start(bf16[4,32,256]{2,1,0:T(8,128)(2,1)} %param.7) | copy-start | bytes 196612
  1.5 5.2 %copy-start.3 = (s32[4]{0:T(128)S(1)}, s32[4]{0:T(128)}, u32[]{:S(2)}) copy-start(s32[4]{0:T(128)} %param.10) | copy-start | bytes 52
  1.5 5.2 %copy-start.4 = (s32[4]{0:T(128)S(1)}, s32[4]{0:T(128)}, u32[]{:S(2)}) copy-start(s32[4]{0:T(128)} %param.11) | copy-start | bytes 52
  1.6 5.4 %copy-start.2 = (bf16[4,4,5,64]{3,1,2,0:T(4,128)(2,1)S(1)}, bf16[4,4,5,64]{3,1,2,0:T(4,128)(2,1)}, u32[]{:S(2)}) copy-start(bf16[4,4,5,64]{3,1,2,0:T(4,128)(2,1)} %param.9) | copy-start | bytes 30724
  1.6 7.3 %collective-permute-start.1 = (bf16[8,32,256]{2,1,0:T(8,128)(2,1)S(1)}, bf16[8,32,256]{2,1,0:T(8,128)(2,1)S(1)}, u32[]{:S(2)}, u32[]{:S(2)}) collective-permute-start(bf16[8,32,256]{2,1,0:T(8,128)(2,1)S(1)} %constant_dynamic-update-slice_fusion), channel_id=1, source_target_pairs={{0,7},{1,0},{2,1},{3,2},{4,3},{5,4},{6,5},{7,6},{8,15},{9,8},{10,9... | collective-permute-start | bytes 393224 | tf_op jit(solution)/shard_map/ppermute | solution.py:17
  6.7 6.5 %collective-permute-start = (bf16[8,32,256]{2,1,0:T(8,128)(2,1)S(1)}, bf16[8,32,256]{2,1,0:T(8,128)(2,1)S(1)}, u32[]{:S(2)}, u32[]{:S(2)}) collective-permute-start(bf16[8,32,256]{2,1,0:T(8,128)(2,1)S(1)} %constant_dynamic-update-slice_fusion), channel_id=1, source_target_pairs={{0,1},{1,2},{2,3},{3,4},{4,5},{5,6},{6,7},{7,0},{8,9},{9,10},{10,1... | collective-permute-start | bytes 393224 | tf_op jit(solution)/shard_map/ppermute | solution.py:17
  13.3 9.6 %collective-permute-start.2 = (bf16[896,256]{1,0:T(8,128)(2,1)S(1)}, bf16[896,256]{1,0:T(8,128)(2,1)S(1)}, u32[]{:S(2)}, u32[]{:S(2)}) collective-permute-start(bf16[896,256]{1,0:T(8,128)(2,1)S(1)} %pad_maximum_fusion.1), channel_id=1, source_target_pairs={{0,8},{8,0},{16,24},{24,16},{1,9},{9,1},{17,25},{25,17},{2,10},{10... | collective-permute-start | bytes 1376264 | tf_op jit(solution)/shard_map/ppermute | solution.py:22
  15.5 7.3 %collective-permute-start.3 = (bf16[448,256]{1,0:T(8,128)(2,1)S(1)}, bf16[448,256]{1,0:T(8,128)(2,1)S(1)}, u32[]{:S(2)}, u32[]{:S(2)}) collective-permute-start(bf16[448,256]{1,0:T(8,128)(2,1)S(1)} %pad_maximum_fusion.4), channel_id=1, source_target_pairs={{8,16},{16,8},{9,17},{17,9},{10,18},{18,10},{11,19},{19,11},{12,20... | collective-permute-start | bytes 688136 | tf_op jit(solution)/shard_map/ppermute | solution.py:28
  24.5 5.5 %collective-permute-start.4 = (bf16[256,256]{1,0:T(8,128)(2,1)S(1)}, bf16[256,256]{1,0:T(8,128)(2,1)S(1)}, u32[]{:S(2)}, u32[]{:S(2)}) collective-permute-start(bf16[256,256]{1,0:T(8,128)(2,1)S(1)} %weight_partial.1), channel_id=1, source_target_pairs={{0,16},{8,24},{16,0},{24,8},{1,17},{9,25},{17,1},{25,9},{2,18},{10... | collective-permute-start | bytes 393224 | tf_op jit(solution)/shard_map/ppermute | solution.py:22
  30.0 4.7 %collective-permute-start.5 = (bf16[256,256]{1,0:T(8,128)(2,1)S(1)}, bf16[256,256]{1,0:T(8,128)(2,1)S(1)}, u32[]{:S(2)}, u32[]{:S(2)}) collective-permute-start(bf16[256,256]{1,0:T(8,128)(2,1)S(1)} %add_convert_fusion.2), channel_id=1, source_target_pairs={{0,2},{1,3},{2,0},{3,1},{4,6},{5,7},{6,4},{7,5},{8,10},{9,11},{10,... | collective-permute-start | bytes 393224 | tf_op jit(solution)/shard_map/ppermute | solution.py:22
  34.8 9.1 %collective-permute-start.6 = (bf16[256,256]{1,0:T(8,128)(2,1)S(1)}, bf16[256,256]{1,0:T(8,128)(2,1)S(1)}, u32[]{:S(2)}, u32[]{:S(2)}) collective-permute-start(bf16[256,256]{1,0:T(8,128)(2,1)S(1)} %add_convert_fusion.1), channel_id=1, source_target_pairs={{0,4},{1,5},{2,6},{3,7},{4,0},{5,1},{6,2},{7,3},{8,12},{9,13},{10,... | collective-permute-start | bytes 393224 | tf_op jit(solution)/shard_map/ppermute | solution.py:22
  44.0 4.6 %collective-permute-start.7 = (bf16[256,256]{1,0:T(8,128)(2,1)S(1)}, bf16[256,256]{1,0:T(8,128)(2,1)S(1)}, u32[]{:S(2)}, u32[]{:S(2)}) collective-permute-start(bf16[256,256]{1,0:T(8,128)(2,1)S(1)} %add_convert_fusion), channel_id=1, source_target_pairs={{0,1},{1,0},{2,3},{3,2},{4,5},{5,4},{6,7},{7,6},{8,9},{9,8},{10,11... | collective-permute-start | bytes 393224 | tf_op jit(solution)/shard_map/ppermute | solution.py:22
  44.0 6.0 %copy-start = (bf16[4,256,256]{2,1,0:T(8,128)(2,1)S(1)}, bf16[4,256,256]{2,1,0:T(8,128)(2,1)}, u32[]{:S(2)}) copy-start(bf16[4,256,256]{2,1,0:T(8,128)(2,1)} %weight.1) | copy-start | bytes 1572868
  48.6 3.1 %collective-permute-start.8 = (bf16[512,256]{1,0:T(8,128)(2,1)S(1)}, bf16[512,256]{1,0:T(8,128)(2,1)S(1)}, u32[]{:S(2)}, u32[]{:S(2)}) collective-permute-start(bf16[512,256]{1,0:T(8,128)(2,1)S(1)} %pad_maximum_fusion.3), channel_id=1, source_target_pairs={{0,8},{8,0},{16,24},{24,16},{1,9},{9,1},{17,25},{25,17},{2,10},{10... | collective-permute-start | bytes 786440 | tf_op jit(solution)/shard_map/ppermute | solution.py:22

commit v3 on v2

v3 whole, which is shorter than its diff:
```python
import functools
import math

import jax
import jax.numpy as jnp
from jax import lax
from jax.experimental import pallas as pl
from jax.experimental.pallas import tpu as pltpu
from jax.sharding import PartitionSpec as P

LANES = 128
INNER_FLOPS = 300_000_000
TAP_ROWS = 8


def shift(block, axis, by):
    count = lax.axis_size(axis)
    return lax.ppermute(block, axis, [(i, (i + by) % count) for i in range(count)])


def flip(block, axis, bit):
    count = lax.axis_size(axis)
    return lax.ppermute(block, axis, [(i, i ^ bit) for i in range(count)])


def outer_swap(block, axis):
    count = lax.axis_size(axis)
    pairs = [(i, i + 1) for i in range(1, count - 1, 2)]
    return lax.ppermute(block, axis, pairs + [(b, a) for a, b in pairs])


def make_filters(filter_taps, lat_ext, lon_count, row_scale):
    lat_reach = filter_taps.shape[2] // 2
    half_width = filter_taps.shape[3] // 2
    lat_dist = jnp.abs(jnp.arange(filter_taps.shape[2], dtype=jnp.int32) - lat_reach)
    lon_dist = jnp.abs(jnp.arange(filter_taps.shape[3], dtype=jnp.int32) - half_width)
    support = (lat_dist[None, :, None] < lat_ext[:, None, None]) & (
        lon_dist[None, None, :] < lon_count[:, None, None]
    )
    masked = (
        filter_taps.astype(jnp.float32)
        * support[:, None].astype(jnp.float32)
        * row_scale[:, None, None, None]
    )
    return masked.astype(jnp.bfloat16)


class Layout:
    def __init__(self, rows, reach, width, basis, channels):
        self.rows, self.reach, self.width = rows, reach, width
        self.basis, self.channels = basis, channels
        self.taps = 2 * reach + 1
        self.strip = 3 * width
        self.per_row = basis * TAP_ROWS
        self.cells = 2 * rows * self.strip
        self.edge_cells = 2 * reach * self.strip


def put_row(lay, window, field, at, cells):
    window[field, at, : lay.strip] = cells
    window[field, at, lay.strip :] = jnp.zeros((LANES - lay.strip, lay.channels), jnp.bfloat16)


def message_row(lay, message, rows, field, row):
    start = (field * rows + row) * lay.strip
    return message[start : start + lay.strip]


def message_taps(lay, message, rows, row):
    start = 2 * rows * lay.strip + row * lay.per_row
    return message[start : start + lay.per_row].astype(jnp.float32)


def own_taps(lay, filters, row):
    return filters[row * lay.per_row : (row + 1) * lay.per_row].astype(jnp.float32)


def my_basis():
    return (lax.axis_index("lat") % 2) * 2 + lax.axis_index("lon") % 2


def strip_band(lay, line, keep_west, keep_east):
    width = lay.width
    middle = pltpu.roll(jnp.broadcast_to(line, (width, LANES)), 0, 1, stride=1, stride_axis=0)
    west = pltpu.roll(middle, LANES - width, 1) * keep_west
    east = pltpu.roll(middle, width, 1) * keep_east
    return jnp.concatenate([west, middle, east], axis=0).astype(jnp.bfloat16)


def keep_lanes(lay):
    even = lax.axis_index("lon") % 2 == 0
    lane = lax.broadcasted_iota(jnp.int32, (1, LANES), 1)
    west = jnp.where((lane < lay.width) & even, 0.0, 1.0)
    east = jnp.where((lane >= 2 * lay.width) & jnp.logical_not(even), 0.0, 1.0)
    return west, east


def product(left, right, dims):
    return lax.dot_general(left, right, (dims, ((), ())), preferred_element_type=jnp.float32)


def inner_kernel(lay, strip, filters, partner, grad, window, taps, basis_out):
    rows, reach = lay.rows, lay.reach
    even = lax.axis_index("lat") % 2 == 0
    at_own, at_partner = jnp.where(even, 0, rows), jnp.where(even, rows, 0)
    for row in range(rows):
        for field in range(2):
            put_row(lay, window, field, at_own + row, strip[field, row])
            put_row(lay, window, field, at_partner + row, message_row(lay, partner, rows, field, row))
        taps[at_own + row] = own_taps(lay, filters, row)
        taps[at_partner + row] = message_taps(lay, partner, rows, row)
    keep_west, keep_east = keep_lanes(lay)
    at_mine = pl.multiple_of(my_basis() * TAP_ROWS, TAP_ROWS)
    for row in range(2 * rows):
        lines = taps[row, pl.ds(at_mine, TAP_ROWS), :LANES]
        low, high = max(0, row - reach), min(2 * rows, row + reach + 1)
        bands = [
            strip_band(lay, lines[e : e + 1], keep_west, keep_east)
            for e in range(low - row + reach, high - row + reach)
        ]
        source = window[0, low:high].reshape((high - low) * LANES, lay.channels)
        result = product(jnp.concatenate(bands, axis=1), source, ((1,), (0,)))
        basis_out[row * lay.strip : (row + 1) * lay.strip] = result.astype(jnp.bfloat16)
    cot = window[1, :, : lay.strip].reshape(2 * rows * lay.strip, lay.channels)
    grad[...] = product(basis_out[...], cot, ((0,), (0,)))


def outer_kernel(lay, scale, strip, filters, outer, inner, grad, window, taps, basis_out):
    rows, reach = lay.rows, lay.reach
    even = lax.axis_index("lat") % 2 == 0
    at_outer, at_own = jnp.where(even, 0, reach), jnp.where(even, reach, 0)
    first = jnp.where(even, 0, rows - reach)
    for row in range(reach):
        for field in range(2):
            put_row(lay, window, field, at_own + row, strip[field, first + row])
            put_row(lay, window, field, at_outer + row, message_row(lay, outer, reach, field, row))
        taps[at_outer + row] = message_taps(lay, outer, reach, row)
        taps[at_own + row] = jnp.where(
            even, own_taps(lay, filters, row), own_taps(lay, filters, rows - reach + row)
        )
    keep_west, keep_east = keep_lanes(lay)
    at_mine = pl.multiple_of(my_basis() * TAP_ROWS, TAP_ROWS)
    nothing = jnp.zeros((lay.strip, LANES), jnp.bfloat16)
    for side in range(2):
        rows_of_bands = []
        for row in range(side * reach, (side + 1) * reach):
            lines = taps[row, pl.ds(at_mine, TAP_ROWS), :LANES]
            blocks = []
            for other in range((1 - side) * reach, (2 - side) * reach):
                e = other - row + reach
                inside = 0 <= e < lay.taps
                blocks.append(
                    strip_band(lay, lines[e : e + 1], keep_west, keep_east) if inside else nothing
                )
            rows_of_bands.append(jnp.concatenate(blocks, axis=1))
        source = window[0, (1 - side) * reach : (2 - side) * reach]
        result = product(
            jnp.concatenate(rows_of_bands, axis=0),
            source.reshape(reach * LANES, lay.channels),
            ((1,), (0,)),
        )
        start = side * reach * lay.strip
        basis_out[start : start + reach * lay.strip] = result.astype(jnp.bfloat16)
    cot = window[1, :, : lay.strip].reshape(2 * reach * lay.strip, lay.channels)
    total = inner[...] + product(basis_out[...], cot, ((0,), (0,)))
    grad[...] = (total * scale).astype(jnp.bfloat16)


def field_kernel(lay, strip, filters, partner, outer, weight, output, field_grad, window, taps, mixed):
    rows, reach, width, basis = lay.rows, lay.reach, lay.width, lay.basis
    even = lax.axis_index("lat") % 2 == 0
    at_outer, at_partner = jnp.where(even, 0, rows + reach), jnp.where(even, rows + reach, 0)
    for field in range(2):
        for row in range(rows):
            put_row(lay, window, field, reach + row, strip[field, row])
        for row in range(reach):
            near = jnp.where(
                even,
                message_row(lay, partner, rows, field, row),
                message_row(lay, partner, rows, field, rows - reach + row),
            )
            put_row(lay, window, field, at_partner + row, near)
            put_row(lay, window, field, at_outer + row, message_row(lay, outer, reach, field, row))
    for row in range(rows):
        taps[reach + row] = own_taps(lay, filters, row)
    for row in range(reach):
        taps[at_partner + row] = jnp.where(
            even,
            message_taps(lay, partner, rows, row),
            message_taps(lay, partner, rows, rows - reach + row),
        )
        taps[at_outer + row] = message_taps(lay, outer, reach, row)

    def bands(row, turned):
        blocks = []
        for n in range(lay.taps):
            at, e = (row + n, lay.taps - 1 - n) if turned else (reach + row, n)
            lanes = slice(LANES, 2 * LANES) if turned else slice(0, LANES)
            parts = []
            for k in range(basis):
                line = taps[at, k * TAP_ROWS + e : k * TAP_ROWS + e + 1, lanes]
                spread = jnp.broadcast_to(line, (width, LANES))
                parts.append(pltpu.roll(spread, int(turned), 1, stride=1, stride_axis=0))
            blocks.append(jnp.concatenate(parts, axis=0).astype(jnp.bfloat16))
        return jnp.concatenate(blocks, axis=1)

    for field, turned, out in ((0, False, output), (1, True, field_grad)):
        for row in range(rows):
            source = window[field, row : row + lay.taps].reshape(lay.taps * LANES, lay.channels)
            result = product(bands(row, turned), source, ((1,), (0,))).astype(jnp.bfloat16)
            for k in range(basis):
                mixed[k, row * width : (row + 1) * width] = result[k * width : (k + 1) * width]
        total = jnp.zeros((rows * width, lay.channels), jnp.float32)
        for k in range(basis):
            total += product(mixed[k], weight[k], ((1,), (1 if turned else 0,)))
        out[...] = total.astype(jnp.bfloat16).reshape(out.shape)


def call(kernel, outs, scratch, flops, name):
    vmem = pl.BlockSpec(memory_space=pltpu.VMEM)

    def run(*operands):
        return pl.pallas_call(
            kernel,
            out_shape=outs,
            in_specs=[vmem] * len(operands),
            out_specs=[vmem] * len(outs),
            scratch_shapes=scratch,
            compiler_params=pltpu.CompilerParams(vmem_limit_bytes=32 * 1024 * 1024),
            cost_estimate=pl.CostEstimate(flops=flops, bytes_accessed=1_000_000, transcendentals=0),
            name=name,
        )(*operands)

    return run


def per_device(features, cotangent, weight, filter_taps, lat_ext, lon_count):
    rows, width, channels = features.shape
    basis = weight.shape[0]
    lat_taps = filter_taps.shape[2]
    lay = Layout(rows, lat_taps // 2, width, basis, channels)
    lat, lon = lax.axis_index("lat"), lax.axis_index("lon")
    even = lat % 2 == 0

    own = jnp.concatenate([features, cotangent], axis=0)
    west = shift(own, "lon", 1)
    support_size = ((2 * lat_ext - 1) * (2 * lon_count - 1)).astype(jnp.float32)
    own, row_scale = lax.optimization_barrier((own, lax.rsqrt(support_size)))
    east = shift(own, "lon", -1)
    filters = make_filters(filter_taps, lat_ext, lon_count, row_scale)
    gap = jnp.zeros(filters.shape[:-1] + (LANES - filters.shape[-1],), filters.dtype)
    filters = jnp.concatenate([filters, gap, filters[..., ::-1], gap], axis=-1)
    filters = jnp.pad(filters, ((0, 0), (0, 0), (0, TAP_ROWS - lat_taps), (0, 0)))
    per_row = basis * TAP_ROWS
    filters = filters.reshape(rows * per_row, 2 * LANES)

    strip = jnp.concatenate([west, own, east], axis=1).reshape(2, rows, lay.strip, channels)

    def edge(array, axis, size, bottom):
        start = jnp.where(bottom, array.shape[axis] - size, 0)
        return lax.dynamic_slice_in_dim(array, start, size, axis)

    outward = jnp.concatenate(
        [
            edge(strip, 1, lay.reach, jnp.logical_not(even)).reshape(-1, channels),
            edge(filters, 0, lay.reach * per_row, jnp.logical_not(even)),
        ],
        axis=0,
    )
    outer = outer_swap(outward, "lat")
    partner = flip(jnp.concatenate([strip.reshape(-1, channels), filters], axis=0), "lat", 1)

    def scratch(window_rows, basis_rows):
        return [
            pltpu.VMEM((2, window_rows, LANES, channels), jnp.bfloat16),
            pltpu.VMEM((window_rows, per_row, 2 * LANES), jnp.float32),
            pltpu.VMEM((basis_rows, channels), jnp.bfloat16),
        ]

    total_cells = rows * lax.axis_size("lat") * width * lax.axis_size("lon")
    (inner,) = call(
        functools.partial(inner_kernel, lay),
        [jax.ShapeDtypeStruct((channels, channels), jnp.float32)],
        scratch(2 * rows, 2 * rows * lay.strip),
        INNER_FLOPS,
        "weight_inner",
    )(strip, filters, partner)
    (grad,) = call(
        functools.partial(outer_kernel, lay, 1.0 / math.sqrt(total_cells)),
        [jax.ShapeDtypeStruct((channels, channels), jnp.bfloat16)],
        scratch(2 * lay.reach, 2 * lay.reach * lay.strip),
        100_000_000,
        "weight_outer",
    )(strip, filters, outer, inner)
    output, field_grad = call(
        functools.partial(field_kernel, lay),
        [jax.ShapeDtypeStruct(features.shape, jnp.bfloat16)] * 2,
        scratch(rows + 2 * lay.reach, 0)[:2]
        + [pltpu.VMEM((basis, rows * width, channels), jnp.bfloat16)],
        400_000_000,
        "fields",
    )(strip, filters, partner, outer, weight)

    others = [("lat", 1 << b) for b in range(1, lax.axis_size("lat").bit_length() - 1)]
    others += [("lon", 1 << b) for b in range(1, lax.axis_size("lon").bit_length() - 1)]
    for axis, bit in others:
        total = grad.astype(jnp.float32) + flip(grad, axis, bit).astype(jnp.float32)
        grad = total.astype(jnp.bfloat16)
    for axis, index in (("lon", lon), ("lat", lat)):
        got = flip(grad, axis, 1)
        upper = index % 2 == 1
        grad = jnp.concatenate([jnp.where(upper, got, grad), jnp.where(upper, grad, got)], axis=0)
    weight_grad = grad.astype(jnp.float32).reshape(basis, channels, channels)
    return (output, field_grad, weight_grad)


def solution(mesh):
    in_specs = (
        P("lat", "lon", None),
        P("lat", "lon", None),
        P(),
        P("lat", None, None, None),
        P("lat"),
        P("lat"),
    )
    out_specs = (P("lat", "lon", None), P("lat", "lon", None), P())
    return jax.shard_map(
        per_device, mesh=mesh, in_specs=in_specs, out_specs=out_specs, check_vma=False
    )
```

time: 53.1 us -> 48.9 us (0.921)
  waiting for transfers between devices: 33.8 us -> 24.4 us
  starting transfers between devices: 12.1 us -> 17.1 us
    ppermute x6, starting transfers between devices: 3.91 us -> 8.29 us  [flip(): return lax.ppermute(block, axis, [(i, i ^ bit) for i in range(count)])]
    ppermute x6, waiting for transfers between devices: 23.6 us -> 19.3 us  [flip(): return lax.ppermute(block, axis, [(i, i ^ bit) for i in range(count)])]
    ppermute x2, waiting for transfers between devices: 5.82 us -> 1.98 us  [shift(): lax.ppermute(block, axis, [(i, (i + by) % count) for i in range(count)])]
    ppermute x1, waiting for transfers between devices: 4.3 us -> 3.07 us  [outer_swap(): return lax.ppermute(block, axis, pairs + [(b, a) for a, b in pairs])]
    ppermute x2, starting transfers between devices: 5.16 us -> 5.77 us  [shift(): lax.ppermute(block, axis, [(i, (i + by) % count) for i in range(count)])]
    pallas_call x2 -> x3, Pallas kernels: 3.25 us -> 3.43 us  [run(): pl.pallas_call(kernel, out_shape=outs, in_specs=[vmem] * len(operands), o...]
  transfers between devices with their start and end apart: 9 -> 9, of which waited for: 7 -> 6; matrix products, arithmetic and copies ran while one was open for 1% -> 1% of each run, Pallas kernels for 3% -> 6%
where the time goes in v3:
time: 48.9 us; the launch traced here: 48.7 us
  waiting for transfers between devices  24.4 us (50%)
  starting transfers between devices  17.1 us (35%)
  Pallas kernels  3.43 us (7%)
  other arithmetic  1.81 us (4%)
  local copies, waits for them, and re-layouts  1.11 us (2%)
  between operations  0.84 us (2%)
    ppermute x6, waiting for transfers between devices, flip(): return lax.ppermute(block, axis, [(i, i ^ bit) for i in range(count)])  19.3 us
    ppermute x6, starting transfers between devices, flip(): return lax.ppermute(block, axis, [(i, i ^ bit) for i in range(count)])  8.29 us
    ppermute x2, starting transfers between devices, shift(): lax.ppermute(block, axis, [(i, (i + by) % count) for i in range(count)])  5.77 us
    pallas_call x3, Pallas kernels, run(): pl.pallas_call(kernel, out_shape=outs, in_specs=[vmem] * len(operands), o...  3.43 us
    ppermute x1, waiting for transfers between devices, outer_swap(): return lax.ppermute(block, axis, pairs + [(b, a) for a, b in pairs])  3.07 us
    ppermute x1, starting transfers between devices, outer_swap(): return lax.ppermute(block, axis, pairs + [(b, a) for a, b in pairs])  3.05 us
    ppermute x2, waiting for transfers between devices, shift(): lax.ppermute(block, axis, [(i, (i + by) % count) for i in range(count)])  1.98 us
    convert_element_type x1, other arithmetic, per_device(): weight_grad = grad.astype(jnp.float32).reshape(basis, channels, channels)  1.06 us
  transfers between devices with their start and end apart: 9, of which 6 were waited for; matrix products, arithmetic and copies ran while one was open for 1% of the time, Pallas kernels for 6%

profile of v3, /device:TPU:1, one launch (start us, length us, event | category | flops | bytes accessed | tf_op | source)
XLA Modules:
  0.0 48.7 jit_solution(7584436919426422564)
XLA Ops:
  0.6 0.0 copy-start.1
  0.6 0.9 %constant_dynamic-update-slice_fusion.1 = bf16[8,32,256]{2,1,0:T(8,128)(2,1)S(1)} fusion(bf16[4,32,256]{2,1,0:T(8,128)(2,1)} %param.6), kind=kLoop, calls=%fused_computation.15 | loop fusion | bytes 131072
  1.5 0.0 copy-done.1
  1.5 0.0 copy-start.3
  1.5 0.0 copy-start.4
  1.6 0.0 copy-start.2
  1.6 2.1 %collective-permute-start = (bf16[8,32,256]{2,1,0:T(8,128)(2,1)S(1)}, bf16[8,32,256]{2,1,0:T(8,128)(2,1)S(1)}, u32[]{:S(2)}, u32[]{:S(2)}) collective-permute-start(bf16[8,32,256]{2,1,0:T(8,128)(2,1)S(1)} %constant_dynamic-update-slice_fusion), channel_id=1, source_target_pairs={{0,1},{1,2},{2,3},{3,4},{4,5},{5,6},{6,7},{7,0},{8,9},{9,10},{10,1... | collective-permute-start | bytes 393224 | tf_op jit(solution)/shard_map/ppermute | solution.py:18
  3.7 0.0 copy-done.3
  3.7 0.0 copy-done.4
  3.7 3.6 %collective-permute-start.1 = (bf16[8,32,256]{2,1,0:T(8,128)(2,1)S(1)}, bf16[8,32,256]{2,1,0:T(8,128)(2,1)S(1)}, u32[]{:S(2)}, u32[]{:S(2)}) collective-permute-start(bf16[8,32,256]{2,1,0:T(8,128)(2,1)S(1)} %constant_dynamic-update-slice_fusion), channel_id=1, source_target_pairs={{0,7},{1,0},{2,1},{3,2},{4,3},{5,4},{6,5},{7,6},{8,15},{9,8},{10,9... | collective-permute-start | bytes 393224 | tf_op jit(solution)/shard_map/ppermute | solution.py:18
  7.4 0.1 broadcast_compare_fusion.1
  7.4 0.1 broadcast_compare_fusion
  7.5 0.1 and_convert_fusion
  7.6 0.0 copy-done.2
  7.6 0.1 multiply_convert_fusion
  7.7 0.1 rev.3
  7.8 0.1 pad_maximum_fusion.4
  8.0 2.0 %collective-permute-done = bf16[8,32,256]{2,1,0:T(8,128)(2,1)S(1)} collective-permute-done((bf16[8,32,256]{2,1,0:T(8,128)(2,1)S(1)}, bf16[8,32,256]{2,1,0:T(8,128)(2,1)S(1)}, u32[]{:S(2)}, u32[]{:S(2)}) %collective-permute-start) | collective-permute-done | bytes 131104 | tf_op jit(solution)/shard_map/ppermute | solution.py:18
  10.0 0.0 collective-permute-done.1
  10.0 2.6 %collective-permute-start.2 = (bf16[896,256]{1,0:T(8,128)(2,1)S(1)}, bf16[896,256]{1,0:T(8,128)(2,1)S(1)}, u32[]{:S(2)}, u32[]{:S(2)}) collective-permute-start(bf16[896,256]{1,0:T(8,128)(2,1)S(1)} %pad_maximum_fusion.1), channel_id=1, source_target_pairs={{0,8},{8,0},{16,24},{24,16},{1,9},{9,1},{17,25},{25,17},{2,10},{10... | collective-permute-start | bytes 1376264 | tf_op jit(solution)/shard_map/ppermute | solution.py:23
  12.6 3.1 %collective-permute-start.3 = (bf16[448,256]{1,0:T(8,128)(2,1)S(1)}, bf16[448,256]{1,0:T(8,128)(2,1)S(1)}, u32[]{:S(2)}, u32[]{:S(2)}) collective-permute-start(bf16[448,256]{1,0:T(8,128)(2,1)S(1)} %pad_maximum_fusion.3), channel_id=1, source_target_pairs={{8,16},{16,8},{9,17},{17,9},{10,18},{18,10},{11,19},{19,11},{12,20... | collective-permute-start | bytes 688136 | tf_op jit(solution)/shard_map/ppermute | solution.py:29
  15.7 0.0 collective-permute-done.2.partner
  15.7 1.2 %weight_inner.1.inner = f32[256,256]{1,0:T(8,128)S(1)} custom-call(bf16[2,4,96,256]{3,2,1,0:T(8,128)(2,1)S(1)} %bitcast.8, bf16[128,256]{1,0:T(8,128)(2,1)S(1)} %bitcast.13, bf16[896,256]{1,0:T(8,128)(2,1)S(1)} %collective-permute-done.2.partner), custom_call_target="tpu_custom_call" | custom-call | flops 300000000 | bytes 1000000 | tf_op jit(solution)/shard_map/weight_inner/pallas_call | solution.py:223
  16.9 3.1 %collective-permute-done.3.outer = bf16[448,256]{1,0:T(8,128)(2,1)S(1)} collective-permute-done((bf16[448,256]{1,0:T(8,128)(2,1)S(1)}, bf16[448,256]{1,0:T(8,128)(2,1)S(1)}, u32[]{:S(2)}, u32[]{:S(2)}) %collective-permute-start.3) | collective-permute-done | bytes 229408 | tf_op jit(solution)/shard_map/ppermute | solution.py:29
  20.0 0.6 %weight_outer.1 = bf16[256,256]{1,0:T(8,128)(2,1)S(1)} custom-call(bf16[2,4,96,256]{3,2,1,0:T(8,128)(2,1)S(1)} %bitcast.9, bf16[128,256]{1,0:T(8,128)(2,1)S(1)} %bitcast.14, bf16[448,256]{1,0:T(8,128)(2,1)S(1)} %collective-permute-done.3.outer, f32[256,256]{1,0:T(8,128)S(1)} %weight_inner.1.inner), custom_call_target="tpu_custom_call" | custom-call | flops 100000000 | bytes 1000000 | tf_op jit(solution)/shard_map/weight_outer/pallas_call | solution.py:223
  20.6 0.1 collective-permute-start.4
  20.7 5.5 %collective-permute-done.4 = bf16[256,256]{1,0:T(8,128)(2,1)S(1)} collective-permute-done((bf16[256,256]{1,0:T(8,128)(2,1)S(1)}, bf16[256,256]{1,0:T(8,128)(2,1)S(1)}, u32[]{:S(2)}, u32[]{:S(2)}) %collective-permute-start.4) | collective-permute-done | bytes 131104 | tf_op jit(solution)/shard_map/ppermute | solution.py:23
  26.2 0.9 %collective-permute-start.5 = (bf16[256,256]{1,0:T(8,128)(2,1)S(1)}, bf16[256,256]{1,0:T(8,128)(2,1)S(1)}, u32[]{:S(2)}, u32[]{:S(2)}) collective-permute-start(bf16[256,256]{1,0:T(8,128)(2,1)S(1)} %add_convert_fusion.2), channel_id=1, source_target_pairs={{0,2},{1,3},{2,0},{3,1},{4,6},{5,7},{6,4},{7,5},{8,10},{9,11},{10,... | collective-permute-start | bytes 393224 | tf_op jit(solution)/shard_map/ppermute | solution.py:23
  27.1 3.8 %collective-permute-done.5 = bf16[256,256]{1,0:T(8,128)(2,1)S(1)} collective-permute-done((bf16[256,256]{1,0:T(8,128)(2,1)S(1)}, bf16[256,256]{1,0:T(8,128)(2,1)S(1)}, u32[]{:S(2)}, u32[]{:S(2)}) %collective-permute-start.5) | collective-permute-done | bytes 131104 | tf_op jit(solution)/shard_map/ppermute | solution.py:23
  31.0 2.0 %collective-permute-start.6 = (bf16[256,256]{1,0:T(8,128)(2,1)S(1)}, bf16[256,256]{1,0:T(8,128)(2,1)S(1)}, u32[]{:S(2)}, u32[]{:S(2)}) collective-permute-start(bf16[256,256]{1,0:T(8,128)(2,1)S(1)} %add_convert_fusion.1), channel_id=1, source_target_pairs={{0,4},{1,5},{2,6},{3,7},{4,0},{5,1},{6,2},{7,3},{8,12},{9,13},{10,... | collective-permute-start | bytes 393224 | tf_op jit(solution)/shard_map/ppermute | solution.py:23
  32.9 6.6 %collective-permute-done.6 = bf16[256,256]{1,0:T(8,128)(2,1)S(1)} collective-permute-done((bf16[256,256]{1,0:T(8,128)(2,1)S(1)}, bf16[256,256]{1,0:T(8,128)(2,1)S(1)}, u32[]{:S(2)}, u32[]{:S(2)}) %collective-permute-start.6) | collective-permute-done | bytes 131104 | tf_op jit(solution)/shard_map/ppermute | solution.py:23
  39.5 0.4 collective-permute-start.7
  39.9 0.0 copy-start
  39.9 3.5 %collective-permute-done.7 = bf16[256,256]{1,0:T(8,128)(2,1)S(1)} collective-permute-done((bf16[256,256]{1,0:T(8,128)(2,1)S(1)}, bf16[256,256]{1,0:T(8,128)(2,1)S(1)}, u32[]{:S(2)}, u32[]{:S(2)}) %collective-permute-start.7) | collective-permute-done | bytes 131104 | tf_op jit(solution)/shard_map/ppermute | solution.py:23
  43.5 2.4 %collective-permute-start.8 = (bf16[512,256]{1,0:T(8,128)(2,1)S(1)}, bf16[512,256]{1,0:T(8,128)(2,1)S(1)}, u32[]{:S(2)}, u32[]{:S(2)}) collective-permute-start(bf16[512,256]{1,0:T(8,128)(2,1)S(1)} %pad_maximum_fusion.2), channel_id=1, source_target_pairs={{0,8},{8,0},{16,24},{24,16},{1,9},{9,1},{17,25},{25,17},{2,10},{10... | collective-permute-start | bytes 786440 | tf_op jit(solution)/shard_map/ppermute | solution.py:23
  45.8 0.0 copy-done
  45.8 1.6 %fields.1 = (bf16[4,32,256]{2,1,0:T(8,128)(2,1)}, bf16[4,32,256]{2,1,0:T(8,128)(2,1)}) custom-call(bf16[2,4,96,256]{3,2,1,0:T(8,128)(2,1)S(1)} %bitcast.10, bf16[128,256]{1,0:T(8,128)(2,1)S(1)} %bitcast.15, bf16[896,256]{1,0:T(8,128)(2,1)S(1)} %collective-permute-done.2.partner, bf16[448,256]{1,0:T(8,128)(2,1)S(1)} %collective-permute-done.3.outer, ...), custom_call_target="tpu_custom_call" | custom-call | flops 400000000 | bytes 1000000 | tf_op jit(solution)/shard_map/fields/pallas_call | solution.py:223
  47.5 0.0 collective-permute-done.8
  47.5 0.1 broadcast_select_fusion.1
  47.6 1.1 %convert.1 = f32[4,256,256]{2,1,0:T(8,128)} convert(bf16[4,256,256]{2,1,0:T(8,128)(2,1)S(1)} %bitcast.16) | non-fusion elementwise | flops 262144 | bytes 1572864 | tf_op jit(solution)/shard_map/convert_element_type | solution.py:313
  (20 shorter events, 0.3 us)
Async XLA Ops:
  0.6 0.9 %copy-start.1 = (bf16[4,32,256]{2,1,0:T(8,128)(2,1)S(1)}, bf16[4,32,256]{2,1,0:T(8,128)(2,1)}, u32[]{:S(2)}) copy-start(bf16[4,32,256]{2,1,0:T(8,128)(2,1)} %param.7) | copy-start | bytes 196612
  1.5 2.2 %copy-start.3 = (s32[4]{0:T(128)S(1)}, s32[4]{0:T(128)}, u32[]{:S(2)}) copy-start(s32[4]{0:T(128)} %param.10) | copy-start | bytes 52
  1.5 2.2 %copy-start.4 = (s32[4]{0:T(128)S(1)}, s32[4]{0:T(128)}, u32[]{:S(2)}) copy-start(s32[4]{0:T(128)} %param.11) | copy-start | bytes 52
  1.6 6.0 %copy-start.2 = (bf16[4,4,5,64]{3,1,2,0:T(4,128)(2,1)S(1)}, bf16[4,4,5,64]{3,1,2,0:T(4,128)(2,1)}, u32[]{:S(2)}) copy-start(bf16[4,4,5,64]{3,1,2,0:T(4,128)(2,1)} %param.9) | copy-start | bytes 30724
  1.6 8.4 %collective-permute-start = (bf16[8,32,256]{2,1,0:T(8,128)(2,1)S(1)}, bf16[8,32,256]{2,1,0:T(8,128)(2,1)S(1)}, u32[]{:S(2)}, u32[]{:S(2)}) collective-permute-start(bf16[8,32,256]{2,1,0:T(8,128)(2,1)S(1)} %constant_dynamic-update-slice_fusion), channel_id=1, source_target_pairs={{0,1},{1,2},{2,3},{3,4},{4,5},{5,6},{6,7},{7,0},{8,9},{9,10},{10,1... | collective-permute-start | bytes 393224 | tf_op jit(solution)/shard_map/ppermute | solution.py:18
  3.7 6.3 %collective-permute-start.1 = (bf16[8,32,256]{2,1,0:T(8,128)(2,1)S(1)}, bf16[8,32,256]{2,1,0:T(8,128)(2,1)S(1)}, u32[]{:S(2)}, u32[]{:S(2)}) collective-permute-start(bf16[8,32,256]{2,1,0:T(8,128)(2,1)S(1)} %constant_dynamic-update-slice_fusion), channel_id=1, source_target_pairs={{0,7},{1,0},{2,1},{3,2},{4,3},{5,4},{6,5},{7,6},{8,15},{9,8},{10,9... | collective-permute-start | bytes 393224 | tf_op jit(solution)/shard_map/ppermute | solution.py:18
  10.0 5.7 %collective-permute-start.2 = (bf16[896,256]{1,0:T(8,128)(2,1)S(1)}, bf16[896,256]{1,0:T(8,128)(2,1)S(1)}, u32[]{:S(2)}, u32[]{:S(2)}) collective-permute-start(bf16[896,256]{1,0:T(8,128)(2,1)S(1)} %pad_maximum_fusion.1), channel_id=1, source_target_pairs={{0,8},{8,0},{16,24},{24,16},{1,9},{9,1},{17,25},{25,17},{2,10},{10... | collective-permute-start | bytes 1376264 | tf_op jit(solution)/shard_map/ppermute | solution.py:23
  12.6 7.3 %collective-permute-start.3 = (bf16[448,256]{1,0:T(8,128)(2,1)S(1)}, bf16[448,256]{1,0:T(8,128)(2,1)S(1)}, u32[]{:S(2)}, u32[]{:S(2)}) collective-permute-start(bf16[448,256]{1,0:T(8,128)(2,1)S(1)} %pad_maximum_fusion.3), channel_id=1, source_target_pairs={{8,16},{16,8},{9,17},{17,9},{10,18},{18,10},{11,19},{19,11},{12,20... | collective-permute-start | bytes 688136 | tf_op jit(solution)/shard_map/ppermute | solution.py:29
  20.6 5.5 %collective-permute-start.4 = (bf16[256,256]{1,0:T(8,128)(2,1)S(1)}, bf16[256,256]{1,0:T(8,128)(2,1)S(1)}, u32[]{:S(2)}, u32[]{:S(2)}) collective-permute-start(bf16[256,256]{1,0:T(8,128)(2,1)S(1)} %weight_outer.1), channel_id=1, source_target_pairs={{0,16},{8,24},{16,0},{24,8},{1,17},{9,25},{17,1},{25,9},{2,18},{10... | collective-permute-start | bytes 393224 | tf_op jit(solution)/shard_map/ppermute | solution.py:23
  26.2 4.7 %collective-permute-start.5 = (bf16[256,256]{1,0:T(8,128)(2,1)S(1)}, bf16[256,256]{1,0:T(8,128)(2,1)S(1)}, u32[]{:S(2)}, u32[]{:S(2)}) collective-permute-start(bf16[256,256]{1,0:T(8,128)(2,1)S(1)} %add_convert_fusion.2), channel_id=1, source_target_pairs={{0,2},{1,3},{2,0},{3,1},{4,6},{5,7},{6,4},{7,5},{8,10},{9,11},{10,... | collective-permute-start | bytes 393224 | tf_op jit(solution)/shard_map/ppermute | solution.py:23
  31.0 8.5 %collective-permute-start.6 = (bf16[256,256]{1,0:T(8,128)(2,1)S(1)}, bf16[256,256]{1,0:T(8,128)(2,1)S(1)}, u32[]{:S(2)}, u32[]{:S(2)}) collective-permute-start(bf16[256,256]{1,0:T(8,128)(2,1)S(1)} %add_convert_fusion.1), channel_id=1, source_target_pairs={{0,4},{1,5},{2,6},{3,7},{4,0},{5,1},{6,2},{7,3},{8,12},{9,13},{10,... | collective-permute-start | bytes 393224 | tf_op jit(solution)/shard_map/ppermute | solution.py:23
  39.5 3.9 %collective-permute-start.7 = (bf16[256,256]{1,0:T(8,128)(2,1)S(1)}, bf16[256,256]{1,0:T(8,128)(2,1)S(1)}, u32[]{:S(2)}, u32[]{:S(2)}) collective-permute-start(bf16[256,256]{1,0:T(8,128)(2,1)S(1)} %add_convert_fusion), channel_id=1, source_target_pairs={{0,1},{1,0},{2,3},{3,2},{4,5},{5,4},{6,7},{7,6},{8,9},{9,8},{10,11... | collective-permute-start | bytes 393224 | tf_op jit(solution)/shard_map/ppermute | solution.py:23
  39.9 5.9 %copy-start = (bf16[4,256,256]{2,1,0:T(8,128)(2,1)S(1)}, bf16[4,256,256]{2,1,0:T(8,128)(2,1)}, u32[]{:S(2)}) copy-start(bf16[4,256,256]{2,1,0:T(8,128)(2,1)} %weight.1) | copy-start | bytes 1572868
  43.5 4.0 %collective-permute-start.8 = (bf16[512,256]{1,0:T(8,128)(2,1)S(1)}, bf16[512,256]{1,0:T(8,128)(2,1)S(1)}, u32[]{:S(2)}, u32[]{:S(2)}) collective-permute-start(bf16[512,256]{1,0:T(8,128)(2,1)S(1)} %pad_maximum_fusion.2), channel_id=1, source_target_pairs={{0,8},{8,0},{16,24},{24,16},{1,9},{9,1},{17,25},{25,17},{2,10},{10... | collective-permute-start | bytes 786440 | tf_op jit(solution)/shard_map/ppermute | solution.py:23

commit v4 on v3

--- a/solution.py
+++ b/solution.py
@@ -10,6 +10,7 @@
 
 LANES = 128
 INNER_FLOPS = 300_000_000
+MIDDLE_FLOPS = 100_000_000
 TAP_ROWS = 8
 
 
@@ -99,7 +100,7 @@
     return lax.dot_general(left, right, (dims, ((), ())), preferred_element_type=jnp.float32)
 
 
-def inner_kernel(lay, strip, filters, partner, grad, window, taps, basis_out):
+def inner_kernel(lay, scale, strip, filters, partner, grad, window, taps, basis_out):
     rows, reach = lay.rows, lay.reach
     even = lax.axis_index("lat") % 2 == 0
     at_own, at_partner = jnp.where(even, 0, rows), jnp.where(even, rows, 0)
@@ -122,22 +123,11 @@
         result = product(jnp.concatenate(bands, axis=1), source, ((1,), (0,)))
         basis_out[row * lay.strip : (row + 1) * lay.strip] = result.astype(jnp.bfloat16)
     cot = window[1, :, : lay.strip].reshape(2 * rows * lay.strip, lay.channels)
-    grad[...] = product(basis_out[...], cot, ((0,), (0,)))
-
-
-def outer_kernel(lay, scale, strip, filters, outer, inner, grad, window, taps, basis_out):
-    rows, reach = lay.rows, lay.reach
-    even = lax.axis_index("lat") % 2 == 0
-    at_outer, at_own = jnp.where(even, 0, reach), jnp.where(even, reach, 0)
-    first = jnp.where(even, 0, rows - reach)
-    for row in range(reach):
-        for field in range(2):
-            put_row(lay, window, field, at_own + row, strip[field, first + row])
-            put_row(lay, window, field, at_outer + row, message_row(lay, outer, reach, field, row))
-        taps[at_outer + row] = message_taps(lay, outer, reach, row)
-        taps[at_own + row] = jnp.where(
-            even, own_taps(lay, filters, row), own_taps(lay, filters, rows - reach + row)
-        )
+    grad[...] = (product(basis_out[...], cot, ((0,), (0,))) * scale).astype(jnp.bfloat16)
+
+
+def across(lay, scale, window, taps, basis_out):
+    reach = lay.reach
     keep_west, keep_east = keep_lanes(lay)
     at_mine = pl.multiple_of(my_basis() * TAP_ROWS, TAP_ROWS)
     nothing = jnp.zeros((lay.strip, LANES), jnp.bfloat16)
@@ -162,8 +152,36 @@
         start = side * reach * lay.strip
         basis_out[start : start + reach * lay.strip] = result.astype(jnp.bfloat16)
     cot = window[1, :, : lay.strip].reshape(2 * reach * lay.strip, lay.channels)
-    total = inner[...] + product(basis_out[...], cot, ((0,), (0,)))
-    grad[...] = (total * scale).astype(jnp.bfloat16)
+    return product(basis_out[...], cot, ((0,), (0,))) * scale
+
+
+def outer_kernel(lay, scale, strip, filters, outer, inner, grad, window, taps, basis_out):
+    rows, reach = lay.rows, lay.reach
+    even = lax.axis_index("lat") % 2 == 0
+    at_outer, at_own = jnp.where(even, 0, reach), jnp.where(even, reach, 0)
+    first = jnp.where(even, 0, rows - reach)
+    for row in range(reach):
+        for field in range(2):
+            put_row(lay, window, field, at_own + row, strip[field, first + row])
+            put_row(lay, window, field, at_outer + row, message_row(lay, outer, reach, field, row))
+        taps[at_outer + row] = message_taps(lay, outer, reach, row)
+        taps[at_own + row] = jnp.where(
+            even, own_taps(lay, filters, row), own_taps(lay, filters, rows - reach + row)
+        )
+    total = inner[...].astype(jnp.float32) + across(lay, scale, window, taps, basis_out)
+    grad[...] = total.astype(jnp.bfloat16)
+
+
+def middle_kernel(lay, scale, near, far, grad, window, taps, basis_out):
+    reach = lay.reach
+    upper = (lax.axis_index("lat") // 2) % 2 == 0
+    at_near, at_far = jnp.where(upper, 0, reach), jnp.where(upper, reach, 0)
+    for at, message in ((at_near, near), (at_far, far)):
+        for row in range(reach):
+            for field in range(2):
+                put_row(lay, window, field, at + row, message_row(lay, message, reach, field, row))
+            taps[at + row] = message_taps(lay, message, reach, row)
+    grad[...] = across(lay, scale, window, taps, basis_out)
 
 
 def field_kernel(lay, strip, filters, partner, outer, weight, output, field_grad, window, taps, mixed):
@@ -244,9 +262,10 @@
 
     own = jnp.concatenate([features, cotangent], axis=0)
     west = shift(own, "lon", 1)
+    own, lat_ext = lax.optimization_barrier((own, lat_ext))
+    east = shift(own, "lon", -1)
     support_size = ((2 * lat_ext - 1) * (2 * lon_count - 1)).astype(jnp.float32)
-    own, row_scale = lax.optimization_barrier((own, lax.rsqrt(support_size)))
-    east = shift(own, "lon", -1)
+    row_scale = lax.rsqrt(support_size)
     filters = make_filters(filter_taps, lat_ext, lon_count, row_scale)
     gap = jnp.zeros(filters.shape[:-1] + (LANES - filters.shape[-1],), filters.dtype)
     filters = jnp.concatenate([filters, gap, filters[..., ::-1], gap], axis=-1)
@@ -256,19 +275,20 @@
 
     strip = jnp.concatenate([west, own, east], axis=1).reshape(2, rows, lay.strip, channels)
 
-    def edge(array, axis, size, bottom):
-        start = jnp.where(bottom, array.shape[axis] - size, 0)
-        return lax.dynamic_slice_in_dim(array, start, size, axis)
-
-    outward = jnp.concatenate(
-        [
-            edge(strip, 1, lay.reach, jnp.logical_not(even)).reshape(-1, channels),
-            edge(filters, 0, lay.reach * per_row, jnp.logical_not(even)),
-        ],
-        axis=0,
-    )
-    outer = outer_swap(outward, "lat")
     partner = flip(jnp.concatenate([strip.reshape(-1, channels), filters], axis=0), "lat", 1)
+
+    def edge(cells, taps, bottom):
+        start = jnp.where(bottom, rows - lay.reach, 0)
+        cells = lax.dynamic_slice_in_dim(cells.reshape(strip.shape), start, lay.reach, 1)
+        taps = lax.dynamic_slice_in_dim(taps, start * per_row, lay.reach * per_row, 0)
+        return jnp.concatenate([cells.reshape(-1, channels), taps], axis=0)
+
+    upper = (lat // 2) % 2 == 0
+    beside = (lat % 2 == 1) == upper
+    near = jnp.where(
+        beside, edge(strip, filters, upper), edge(partner[: lay.cells], partner[lay.cells :], upper)
+    )
+    far = flip(near, "lat", 2)
 
     def scratch(window_rows, basis_rows):
         return [
@@ -277,21 +297,33 @@
             pltpu.VMEM((basis_rows, channels), jnp.bfloat16),
         ]
 
-    total_cells = rows * lax.axis_size("lat") * width * lax.axis_size("lon")
-    (inner,) = call(
-        functools.partial(inner_kernel, lay),
-        [jax.ShapeDtypeStruct((channels, channels), jnp.float32)],
+    scale = 1.0 / math.sqrt(rows * lax.axis_size("lat") * width * lax.axis_size("lon"))
+    share = jax.ShapeDtypeStruct((channels, channels), jnp.bfloat16)
+    edges = scratch(2 * lay.reach, 2 * lay.reach * lay.strip)
+    (grad,) = call(
+        functools.partial(inner_kernel, lay, scale),
+        [share],
         scratch(2 * rows, 2 * rows * lay.strip),
         INNER_FLOPS,
         "weight_inner",
     )(strip, filters, partner)
-    (grad,) = call(
-        functools.partial(outer_kernel, lay, 1.0 / math.sqrt(total_cells)),
-        [jax.ShapeDtypeStruct((channels, channels), jnp.bfloat16)],
-        scratch(2 * lay.reach, 2 * lay.reach * lay.strip),
-        100_000_000,
-        "weight_outer",
-    )(strip, filters, outer, inner)
+    outer = jnp.zeros_like(far)
+    if lax.axis_size("lat") > 4:
+        outer = outer_swap(edge(strip, filters, jnp.logical_not(even)), "lat")
+        outer = jnp.where(beside, jnp.zeros_like(outer), outer)
+        (grad,) = call(functools.partial(outer_kernel, lay, scale), [share], edges, MIDDLE_FLOPS, "weight_outer")(
+            strip, filters, outer, grad
+        )
+    got = flip(grad, "lat", 2)
+    (middle,) = call(
+        functools.partial(middle_kernel, lay, scale),
+        [jax.ShapeDtypeStruct((channels, channels), jnp.float32)],
+        edges,
+        MIDDLE_FLOPS,
+        "weight_middle",
+    )(near, far)
+    grad = (grad.astype(jnp.float32) + got.astype(jnp.float32) + middle).astype(jnp.bfloat16)
+    outer = jnp.where(beside, far, outer)
     output, field_grad = call(
         functools.partial(field_kernel, lay),
         [jax.ShapeDtypeStruct(features.shape, jnp.bfloat16)] * 2,
@@ -301,9 +333,11 @@
         "fields",
     )(strip, filters, partner, outer, weight)
 
-    others = [("lat", 1 << b) for b in range(1, lax.axis_size("lat").bit_length() - 1)]
+    others = [("lat", 1 << b) for b in range(2, lax.axis_size("lat").bit_length() - 1)]
     others += [("lon", 1 << b) for b in range(1, lax.axis_size("lon").bit_length() - 1)]
-    for axis, bit in others:
+    for step, (axis, bit) in enumerate(others):
+        if step == 1:
+            grad, output, field_grad = lax.optimization_barrier((grad, output, field_grad))
         total = grad.astype(jnp.float32) + flip(grad, axis, bit).astype(jnp.float32)
         grad = total.astype(jnp.bfloat16)
     for axis, index in (("lon", lon), ("lat", lat)):

time: 48.9 us -> 45.5 us (0.930)
  the two profiles are of different devices: /device:TPU:1 before, /device:TPU:0 now
where the time goes in v4:
time: 45.5 us; the launch traced here: 45.4 us
  waiting for transfers between devices  25.6 us (56%)
  starting transfers between devices  12.4 us (27%)
  Pallas kernels  3.42 us (8%)
  other arithmetic  1.89 us (4%)
  local copies, waits for them, and re-layouts  1.2 us (3%)
  between operations  0.92 us (2%)
    ppermute x7, waiting for transfers between devices, flip(): return lax.ppermute(block, axis, [(i, i ^ bit) for i in range(count)])  21.5 us
    ppermute x7, starting transfers between devices, flip(): return lax.ppermute(block, axis, [(i, i ^ bit) for i in range(count)])  6.27 us
    ppermute x2, starting transfers between devices, shift(): lax.ppermute(block, axis, [(i, (i + by) % count) for i in range(count)])  6.12 us
    ppermute x2, waiting for transfers between devices, shift(): lax.ppermute(block, axis, [(i, (i + by) % count) for i in range(count)])  4.01 us
    pallas_call x3, Pallas kernels, run(): pl.pallas_call(kernel, out_shape=outs, in_specs=[vmem] * len(operands), o...  3.42 us
    convert_element_type x1, other arithmetic, per_device(): weight_grad = grad.astype(jnp.float32).reshape(basis, channels, channels)  1.06 us
    unnamed x14, local copies, waits for them, and re-layouts  0.93 us
  transfers between devices with their start and end apart: 9, of which 9 were waited for; matrix products, arithmetic and copies ran while one was open for 1% of the time, Pallas kernels for 8%

profile of v4, /device:TPU:0, one launch (start us, length us, event | category | flops | bytes accessed | tf_op | source)
XLA Modules:
  0.0 45.4 jit_solution(7822217565143166295)
XLA Ops:
  0.6 0.0 copy-start.1
  0.6 0.9 %constant_dynamic-update-slice_fusion.1 = bf16[8,32,256]{2,1,0:T(8,128)(2,1)S(1)} fusion(bf16[4,32,256]{2,1,0:T(8,128)(2,1)} %param.6), kind=kLoop, calls=%fused_computation.16 | loop fusion | bytes 131072
  1.5 0.0 copy-done.1
  1.5 0.0 copy-start.3
  1.5 0.0 copy-start.4
  1.6 0.0 copy-start.2
  1.6 3.0 %collective-permute-start = (bf16[8,32,256]{2,1,0:T(8,128)(2,1)S(1)}, bf16[8,32,256]{2,1,0:T(8,128)(2,1)S(1)}, u32[]{:S(2)}, u32[]{:S(2)}) collective-permute-start(bf16[8,32,256]{2,1,0:T(8,128)(2,1)S(1)} %constant_dynamic-update-slice_fusion), channel_id=1, source_target_pairs={{0,1},{1,2},{2,3},{3,4},{4,5},{5,6},{6,7},{7,0},{8,9},{9,10},{10,1... | collective-permute-start | bytes 393224 | tf_op jit(solution)/shard_map/ppermute | solution.py:19
  4.6 3.1 %collective-permute-start.1 = (bf16[8,32,256]{2,1,0:T(8,128)(2,1)S(1)}, bf16[8,32,256]{2,1,0:T(8,128)(2,1)S(1)}, u32[]{:S(2)}, u32[]{:S(2)}) collective-permute-start(bf16[8,32,256]{2,1,0:T(8,128)(2,1)S(1)} %constant_dynamic-update-slice_fusion), channel_id=1, source_target_pairs={{0,7},{1,0},{2,1},{3,2},{4,3},{5,4},{6,5},{7,6},{8,15},{9,8},{10,9... | collective-permute-start | bytes 393224 | tf_op jit(solution)/shard_map/ppermute | solution.py:19
  7.7 0.0 copy-done.3
  7.7 0.1 broadcast_compare_fusion.1
  7.8 0.0 copy-done.4
  7.8 0.1 broadcast_compare_fusion
  7.9 0.1 and_convert_fusion
  7.9 0.0 copy-done.2
  7.9 0.1 multiply_convert_fusion
  8.0 0.1 rev.3
  8.2 0.1 pad_maximum_fusion.3
  8.3 2.9 %collective-permute-done = bf16[8,32,256]{2,1,0:T(8,128)(2,1)S(1)} collective-permute-done((bf16[8,32,256]{2,1,0:T(8,128)(2,1)S(1)}, bf16[8,32,256]{2,1,0:T(8,128)(2,1)S(1)}, u32[]{:S(2)}, u32[]{:S(2)}) %collective-permute-start) | collective-permute-done | bytes 131104 | tf_op jit(solution)/shard_map/ppermute | solution.py:19
  11.3 1.1 %collective-permute-done.1 = bf16[8,32,256]{2,1,0:T(8,128)(2,1)S(1)} collective-permute-done((bf16[8,32,256]{2,1,0:T(8,128)(2,1)S(1)}, bf16[8,32,256]{2,1,0:T(8,128)(2,1)S(1)}, u32[]{:S(2)}, u32[]{:S(2)}) %collective-permute-start.1) | collective-permute-done | bytes 131104 | tf_op jit(solution)/shard_map/ppermute | solution.py:19
  12.4 0.1 collective-permute-start.2
  12.6 1.7 %collective-permute-done.2.partner = bf16[896,256]{1,0:T(8,128)(2,1)S(1)} collective-permute-done((bf16[896,256]{1,0:T(8,128)(2,1)S(1)}, bf16[896,256]{1,0:T(8,128)(2,1)S(1)}, u32[]{:S(2)}, u32[]{:S(2)}) %collective-permute-start.2) | collective-permute-done | bytes 458784 | tf_op jit(solution)/shard_map/ppermute | solution.py:24
  14.4 0.1 maximum_select_fusion.near
  14.5 1.6 %collective-permute-start.4 = (bf16[448,256]{1,0:T(8,128)(2,1)S(1)}, bf16[448,256]{1,0:T(8,128)(2,1)S(1)}, u32[]{:S(2)}, u32[]{:S(2)}) collective-permute-start(bf16[448,256]{1,0:T(8,128)(2,1)S(1)} %maximum_select_fusion.near), channel_id=1, source_target_pairs={{0,16},{8,24},{16,0},{24,8},{1,17},{9,25},{17,1},{25,9},{2,18},{10... | collective-permute-start | bytes 688136 | tf_op jit(solution)/shard_map/ppermute | solution.py:24
  16.0 1.2 %weight_inner.1 = bf16[256,256]{1,0:T(8,128)(2,1)S(1)} custom-call(bf16[2,4,96,256]{3,2,1,0:T(8,128)(2,1)S(1)} %bitcast.10, bf16[128,256]{1,0:T(8,128)(2,1)S(1)} %bitcast.14, bf16[896,256]{1,0:T(8,128)(2,1)S(1)} %collective-permute-done.2.partner), custom_call_target="tpu_custom_call" | custom-call | flops 300000000 | bytes 1000000 | tf_op jit(solution)/shard_map/weight_inner/pallas_call | solution.py:241
  17.2 0.6 %collective-permute-start.3 = (bf16[256,256]{1,0:T(8,128)(2,1)S(1)}, bf16[256,256]{1,0:T(8,128)(2,1)S(1)}, u32[]{:S(2)}, u32[]{:S(2)}) collective-permute-start(bf16[256,256]{1,0:T(8,128)(2,1)S(1)} %weight_inner.1), channel_id=1, source_target_pairs={{0,16},{8,24},{16,0},{24,8},{1,17},{9,25},{17,1},{25,9},{2,18},{10... | collective-permute-start | bytes 393224 | tf_op jit(solution)/shard_map/ppermute | solution.py:24
  17.8 5.2 %collective-permute-done.4.far = bf16[448,256]{1,0:T(8,128)(2,1)S(1)} collective-permute-done((bf16[448,256]{1,0:T(8,128)(2,1)S(1)}, bf16[448,256]{1,0:T(8,128)(2,1)S(1)}, u32[]{:S(2)}, u32[]{:S(2)}) %collective-permute-start.4) | collective-permute-done | bytes 229408 | tf_op jit(solution)/shard_map/ppermute | solution.py:24
  23.0 0.6 %weight_middle.1 = f32[256,256]{1,0:T(8,128)S(1)} custom-call(bf16[448,256]{1,0:T(8,128)(2,1)S(1)} %maximum_select_fusion.near, bf16[448,256]{1,0:T(8,128)(2,1)S(1)} %collective-permute-done.4.far), custom_call_target="tpu_custom_call" | custom-call | flops 100000000 | bytes 1000000 | tf_op jit(solution)/shard_map/weight_middle/pallas_call | solution.py:241
  23.6 0.0 copy-start
  23.6 1.4 %collective-permute-done.3 = bf16[256,256]{1,0:T(8,128)(2,1)S(1)} collective-permute-done((bf16[256,256]{1,0:T(8,128)(2,1)S(1)}, bf16[256,256]{1,0:T(8,128)(2,1)S(1)}, u32[]{:S(2)}, u32[]{:S(2)}) %collective-permute-start.3) | collective-permute-done | bytes 131104 | tf_op jit(solution)/shard_map/ppermute | solution.py:24
  25.0 1.3 %collective-permute-start.5 = (bf16[256,256]{1,0:T(8,128)(2,1)S(1)}, bf16[256,256]{1,0:T(8,128)(2,1)S(1)}, u32[]{:S(2)}, u32[]{:S(2)}) collective-permute-start(bf16[256,256]{1,0:T(8,128)(2,1)S(1)} %add_convert_fusion.2), channel_id=1, source_target_pairs={{0,2},{1,3},{2,0},{3,1},{4,6},{5,7},{6,4},{7,5},{8,10},{9,11},{10,... | collective-permute-start | bytes 393224 | tf_op jit(solution)/shard_map/ppermute | solution.py:24
  26.3 0.0 copy-done
  26.3 1.6 %fields.1 = (bf16[4,32,256]{2,1,0:T(8,128)(2,1)}, bf16[4,32,256]{2,1,0:T(8,128)(2,1)}) custom-call(bf16[2,4,96,256]{3,2,1,0:T(8,128)(2,1)S(1)} %bitcast.11, bf16[128,256]{1,0:T(8,128)(2,1)S(1)} %bitcast.15, bf16[896,256]{1,0:T(8,128)(2,1)S(1)} %collective-permute-done.2.partner, bf16[448,256]{1,0:T(8,128)(2,1)S(1)} %broadcast_select_fusion.2.outer, ...), custom_call_target="tpu_custom_call" | custom-call | flops 400000000 | bytes 1000000 | tf_op jit(solution)/shard_map/fields/pallas_call | solution.py:241
  28.0 2.1 %collective-permute-done.5 = bf16[256,256]{1,0:T(8,128)(2,1)S(1)} collective-permute-done((bf16[256,256]{1,0:T(8,128)(2,1)S(1)}, bf16[256,256]{1,0:T(8,128)(2,1)S(1)}, u32[]{:S(2)}, u32[]{:S(2)}) %collective-permute-start.5) | collective-permute-done | bytes 131104 | tf_op jit(solution)/shard_map/ppermute | solution.py:24
  30.1 2.3 %collective-permute-start.6 = (bf16[256,256]{1,0:T(8,128)(2,1)S(1)}, bf16[256,256]{1,0:T(8,128)(2,1)S(1)}, u32[]{:S(2)}, u32[]{:S(2)}) collective-permute-start(bf16[256,256]{1,0:T(8,128)(2,1)S(1)} %add_convert_fusion.1), channel_id=1, source_target_pairs={{0,4},{1,5},{2,6},{3,7},{4,0},{5,1},{6,2},{7,3},{8,12},{9,13},{10,... | collective-permute-start | bytes 393224 | tf_op jit(solution)/shard_map/ppermute | solution.py:24
  32.4 5.0 %collective-permute-done.6 = bf16[256,256]{1,0:T(8,128)(2,1)S(1)} collective-permute-done((bf16[256,256]{1,0:T(8,128)(2,1)S(1)}, bf16[256,256]{1,0:T(8,128)(2,1)S(1)}, u32[]{:S(2)}, u32[]{:S(2)}) %collective-permute-start.6) | collective-permute-done | bytes 131104 | tf_op jit(solution)/shard_map/ppermute | solution.py:24
  37.5 0.4 collective-permute-start.7
  37.8 4.7 %collective-permute-done.7 = bf16[256,256]{1,0:T(8,128)(2,1)S(1)} collective-permute-done((bf16[256,256]{1,0:T(8,128)(2,1)S(1)}, bf16[256,256]{1,0:T(8,128)(2,1)S(1)}, u32[]{:S(2)}, u32[]{:S(2)}) %collective-permute-start.7) | collective-permute-done | bytes 131104 | tf_op jit(solution)/shard_map/ppermute | solution.py:24
  42.6 0.1 collective-permute-start.8
  42.6 1.5 %collective-permute-done.8 = bf16[512,256]{1,0:T(8,128)(2,1)S(1)} collective-permute-done((bf16[512,256]{1,0:T(8,128)(2,1)S(1)}, bf16[512,256]{1,0:T(8,128)(2,1)S(1)}, u32[]{:S(2)}, u32[]{:S(2)}) %collective-permute-start.8) | collective-permute-done | bytes 262176 | tf_op jit(solution)/shard_map/ppermute | solution.py:24
  44.2 0.1 broadcast_select_fusion.1
  44.3 1.1 %convert.1 = f32[4,256,256]{2,1,0:T(8,128)} convert(bf16[4,256,256]{2,1,0:T(8,128)(2,1)S(1)} %bitcast.16) | non-fusion elementwise | flops 262144 | bytes 1572864 | tf_op jit(solution)/shard_map/convert_element_type | solution.py:347
  (24 shorter events, 0.4 us)
Async XLA Ops:
  0.6 0.9 %copy-start.1 = (bf16[4,32,256]{2,1,0:T(8,128)(2,1)S(1)}, bf16[4,32,256]{2,1,0:T(8,128)(2,1)}, u32[]{:S(2)}) copy-start(bf16[4,32,256]{2,1,0:T(8,128)(2,1)} %param.7) | copy-start | bytes 196612
  1.5 6.2 %copy-start.3 = (s32[4]{0:T(128)S(1)}, s32[4]{0:T(128)}, u32[]{:S(2)}) copy-start(s32[4]{0:T(128)} %param.10) | copy-start | bytes 52
  1.5 6.3 %copy-start.4 = (s32[4]{0:T(128)S(1)}, s32[4]{0:T(128)}, u32[]{:S(2)}) copy-start(s32[4]{0:T(128)} %param.11) | copy-start | bytes 52
  1.6 6.4 %copy-start.2 = (bf16[4,4,5,64]{3,1,2,0:T(4,128)(2,1)S(1)}, bf16[4,4,5,64]{3,1,2,0:T(4,128)(2,1)}, u32[]{:S(2)}) copy-start(bf16[4,4,5,64]{3,1,2,0:T(4,128)(2,1)} %param.9) | copy-start | bytes 30724
  1.6 9.7 %collective-permute-start = (bf16[8,32,256]{2,1,0:T(8,128)(2,1)S(1)}, bf16[8,32,256]{2,1,0:T(8,128)(2,1)S(1)}, u32[]{:S(2)}, u32[]{:S(2)}) collective-permute-start(bf16[8,32,256]{2,1,0:T(8,128)(2,1)S(1)} %constant_dynamic-update-slice_fusion), channel_id=1, source_target_pairs={{0,1},{1,2},{2,3},{3,4},{4,5},{5,6},{6,7},{7,0},{8,9},{9,10},{10,1... | collective-permute-start | bytes 393224 | tf_op jit(solution)/shard_map/ppermute | solution.py:19
  4.6 7.8 %collective-permute-start.1 = (bf16[8,32,256]{2,1,0:T(8,128)(2,1)S(1)}, bf16[8,32,256]{2,1,0:T(8,128)(2,1)S(1)}, u32[]{:S(2)}, u32[]{:S(2)}) collective-permute-start(bf16[8,32,256]{2,1,0:T(8,128)(2,1)S(1)} %constant_dynamic-update-slice_fusion), channel_id=1, source_target_pairs={{0,7},{1,0},{2,1},{3,2},{4,3},{5,4},{6,5},{7,6},{8,15},{9,8},{10,9... | collective-permute-start | bytes 393224 | tf_op jit(solution)/shard_map/ppermute | solution.py:19
  12.4 1.9 %collective-permute-start.2 = (bf16[896,256]{1,0:T(8,128)(2,1)S(1)}, bf16[896,256]{1,0:T(8,128)(2,1)S(1)}, u32[]{:S(2)}, u32[]{:S(2)}) collective-permute-start(bf16[896,256]{1,0:T(8,128)(2,1)S(1)} %pad_maximum_fusion.1), channel_id=1, source_target_pairs={{0,8},{8,0},{16,24},{24,16},{1,9},{9,1},{17,25},{25,17},{2,10},{10... | collective-permute-start | bytes 1376264 | tf_op jit(solution)/shard_map/ppermute | solution.py:24
  14.5 8.5 %collective-permute-start.4 = (bf16[448,256]{1,0:T(8,128)(2,1)S(1)}, bf16[448,256]{1,0:T(8,128)(2,1)S(1)}, u32[]{:S(2)}, u32[]{:S(2)}) collective-permute-start(bf16[448,256]{1,0:T(8,128)(2,1)S(1)} %maximum_select_fusion.near), channel_id=1, source_target_pairs={{0,16},{8,24},{16,0},{24,8},{1,17},{9,25},{17,1},{25,9},{2,18},{10... | collective-permute-start | bytes 688136 | tf_op jit(solution)/shard_map/ppermute | solution.py:24
  17.2 7.8 %collective-permute-start.3 = (bf16[256,256]{1,0:T(8,128)(2,1)S(1)}, bf16[256,256]{1,0:T(8,128)(2,1)S(1)}, u32[]{:S(2)}, u32[]{:S(2)}) collective-permute-start(bf16[256,256]{1,0:T(8,128)(2,1)S(1)} %weight_inner.1), channel_id=1, source_target_pairs={{0,16},{8,24},{16,0},{24,8},{1,17},{9,25},{17,1},{25,9},{2,18},{10... | collective-permute-start | bytes 393224 | tf_op jit(solution)/shard_map/ppermute | solution.py:24
  23.6 2.8 %copy-start = (bf16[4,256,256]{2,1,0:T(8,128)(2,1)S(1)}, bf16[4,256,256]{2,1,0:T(8,128)(2,1)}, u32[]{:S(2)}) copy-start(bf16[4,256,256]{2,1,0:T(8,128)(2,1)} %weight.1) | copy-start | bytes 1572868
  25.0 5.0 %collective-permute-start.5 = (bf16[256,256]{1,0:T(8,128)(2,1)S(1)}, bf16[256,256]{1,0:T(8,128)(2,1)S(1)}, u32[]{:S(2)}, u32[]{:S(2)}) collective-permute-start(bf16[256,256]{1,0:T(8,128)(2,1)S(1)} %add_convert_fusion.2), channel_id=1, source_target_pairs={{0,2},{1,3},{2,0},{3,1},{4,6},{5,7},{6,4},{7,5},{8,10},{9,11},{10,... | collective-permute-start | bytes 393224 | tf_op jit(solution)/shard_map/ppermute | solution.py:24
  30.1 7.3 %collective-permute-start.6 = (bf16[256,256]{1,0:T(8,128)(2,1)S(1)}, bf16[256,256]{1,0:T(8,128)(2,1)S(1)}, u32[]{:S(2)}, u32[]{:S(2)}) collective-permute-start(bf16[256,256]{1,0:T(8,128)(2,1)S(1)} %add_convert_fusion.1), channel_id=1, source_target_pairs={{0,4},{1,5},{2,6},{3,7},{4,0},{5,1},{6,2},{7,3},{8,12},{9,13},{10,... | collective-permute-start | bytes 393224 | tf_op jit(solution)/shard_map/ppermute | solution.py:24
  37.5 5.0 %collective-permute-start.7 = (bf16[256,256]{1,0:T(8,128)(2,1)S(1)}, bf16[256,256]{1,0:T(8,128)(2,1)S(1)}, u32[]{:S(2)}, u32[]{:S(2)}) collective-permute-start(bf16[256,256]{1,0:T(8,128)(2,1)S(1)} %add_convert_fusion), channel_id=1, source_target_pairs={{0,1},{1,0},{2,3},{3,2},{4,5},{5,4},{6,7},{7,6},{8,9},{9,8},{10,11... | collective-permute-start | bytes 393224 | tf_op jit(solution)/shard_map/ppermute | solution.py:24
  42.6 1.6 %collective-permute-start.8 = (bf16[512,256]{1,0:T(8,128)(2,1)S(1)}, bf16[512,256]{1,0:T(8,128)(2,1)S(1)}, u32[]{:S(2)}, u32[]{:S(2)}) collective-permute-start(bf16[512,256]{1,0:T(8,128)(2,1)S(1)} %pad_maximum_fusion.2), channel_id=1, source_target_pairs={{0,8},{8,0},{16,24},{24,16},{1,9},{9,1},{17,25},{25,17},{2,10},{10... | collective-permute-start | bytes 786440 | tf_op jit(solution)/shard_map/ppermute | solution.py:24

commit v5 on v4

v5 whole, which is shorter than its diff:
```python
import functools
import math

import jax
import jax.numpy as jnp
from jax import lax
from jax.experimental import pallas as pl
from jax.experimental.pallas import tpu as pltpu
from jax.sharding import PartitionSpec as P

LANES = 128
TAP_ROWS = 8
INNER_FLOPS = 300_000_000
MIDDLE_FLOPS = 100_000_000
FIELD_FLOPS = 400_000_000


def shift(block, axis, by):
    count = lax.axis_size(axis)
    return lax.ppermute(block, axis, [(i, (i + by) % count) for i in range(count)])


def flip(block, axis, bit):
    count = lax.axis_size(axis)
    return lax.ppermute(block, axis, [(i, i ^ bit) for i in range(count)])


def outer_swap(block, axis):
    pairs = [(i, i + 1) for i in range(3, lax.axis_size(axis) - 1, 4)]
    return lax.ppermute(block, axis, pairs + [(b, a) for a, b in pairs])


def make_filters(filter_taps, lat_ext, lon_count):
    lat_reach = filter_taps.shape[2] // 2
    half_width = filter_taps.shape[3] // 2
    lat_dist = jnp.abs(jnp.arange(filter_taps.shape[2], dtype=jnp.int32) - lat_reach)
    lon_dist = jnp.abs(jnp.arange(filter_taps.shape[3], dtype=jnp.int32) - half_width)
    support = (lat_dist[None, :, None] < lat_ext[:, None, None]) & (
        lon_dist[None, None, :] < lon_count[:, None, None]
    )
    support_size = ((2 * lat_ext - 1) * (2 * lon_count - 1)).astype(jnp.float32)
    row_scale = lax.rsqrt(support_size)
    masked = (
        filter_taps.astype(jnp.float32)
        * support[:, None].astype(jnp.float32)
        * row_scale[:, None, None, None]
    )
    return masked.astype(jnp.bfloat16)


class Layout:
    def __init__(self, rows, reach, width, basis, channels):
        self.rows, self.reach, self.width = rows, reach, width
        self.basis, self.channels = basis, channels
        self.taps = 2 * reach + 1
        self.strip = 3 * width
        self.cells = 2 * rows * self.strip
        self.side = reach * self.strip


def put_row(lay, window, field, at, cells):
    window[field, at, : lay.strip] = cells
    window[field, at, lay.strip :] = jnp.zeros((LANES - lay.strip, lay.channels), jnp.bfloat16)


def tile(message, start, row):
    return message[start + row * TAP_ROWS : start + (row + 1) * TAP_ROWS]


def put_taps(taps, at, count, message, start):
    for row in range(0, count, 2):
        both = message[start + row * TAP_ROWS : start + (row + 2) * TAP_ROWS].astype(jnp.float32)
        taps[at + row] = both[:TAP_ROWS]
        taps[at + row + 1] = both[TAP_ROWS:]


def lines(lay, rows_taps, block):
    width = 2 * lay.width
    lanes = rows_taps.shape[1]
    moved = pltpu.roll(rows_taps, lax.rem(lanes - block * width, lanes), 1)[:, :LANES]
    lane = lax.broadcasted_iota(jnp.int32, (1, LANES), 1)
    return jnp.where(lane < width, moved, 0.0)


def my_basis():
    return (lax.axis_index("lat") % 2) * 2 + lax.axis_index("lon") % 2


def strip_band(lay, line, keep_west, keep_east):
    width = lay.width
    middle = pltpu.roll(jnp.broadcast_to(line, (width, LANES)), 0, 1, stride=1, stride_axis=0)
    west = pltpu.roll(middle, LANES - width, 1) * keep_west
    east = pltpu.roll(middle, width, 1) * keep_east
    return jnp.concatenate([west, middle, east], axis=0).astype(jnp.bfloat16)


def keep_lanes(lay):
    even = lax.axis_index("lon") % 2 == 0
    lane = lax.broadcasted_iota(jnp.int32, (1, LANES), 1)
    west = jnp.where((lane < lay.width) & even, 0.0, 1.0)
    east = jnp.where((lane >= 2 * lay.width) & jnp.logical_not(even), 0.0, 1.0)
    return west, east


def product(left, right, dims):
    return lax.dot_general(left, right, (dims, ((), ())), preferred_element_type=jnp.float32)


def inner_kernel(lay, scale, strip, filters, partner, grad, window, taps, basis_out):
    rows, reach = lay.rows, lay.reach
    even = lax.axis_index("lat") % 2 == 0
    at_own, at_partner = jnp.where(even, 0, rows), jnp.where(even, rows, 0)
    for row in range(rows):
        for field in range(2):
            start = (field * rows + row) * lay.strip
            put_row(lay, window, field, at_own + row, strip[field, row])
            put_row(lay, window, field, at_partner + row, partner[start : start + lay.strip])
    put_taps(taps, at_own, rows, filters, 0)
    put_taps(taps, at_partner, rows, partner, lay.cells)
    keep_west, keep_east = keep_lanes(lay)
    mine = my_basis()
    for row in range(2 * rows):
        line = lines(lay, taps[row], mine)
        low, high = max(0, row - reach), min(2 * rows, row + reach + 1)
        bands = [
            strip_band(lay, line[e : e + 1], keep_west, keep_east)
            for e in range(low - row + reach, high - row + reach)
        ]
        source = window[0, low:high].reshape((high - low) * LANES, lay.channels)
        result = product(jnp.concatenate(bands, axis=1), source, ((1,), (0,)))
        basis_out[row * lay.strip : (row + 1) * lay.strip] = result.astype(jnp.bfloat16)
    cot = window[1, :, : lay.strip].reshape(2 * rows * lay.strip, lay.channels)
    grad[...] = (product(basis_out[...], cot, ((0,), (0,))) * scale).astype(jnp.bfloat16)


def across(lay, scale, window, taps, basis_out):
    reach = lay.reach
    keep_west, keep_east = keep_lanes(lay)
    mine = my_basis()
    nothing = jnp.zeros((lay.strip, LANES), jnp.bfloat16)
    for side in range(2):
        rows_of_bands = []
        for row in range(side * reach, (side + 1) * reach):
            line = lines(lay, taps[row], mine)
            blocks = []
            for other in range((1 - side) * reach, (2 - side) * reach):
                e = other - row + reach
                inside = 0 <= e < lay.taps
                blocks.append(strip_band(lay, line[e : e + 1], keep_west, keep_east) if inside else nothing)
            rows_of_bands.append(jnp.concatenate(blocks, axis=1))
        source = window[0, (1 - side) * reach : (2 - side) * reach]
        result = product(
            jnp.concatenate(rows_of_bands, axis=0),
            source.reshape(reach * LANES, lay.channels),
            ((1,), (0,)),
        )
        basis_out[side * lay.side : (side + 1) * lay.side] = result.astype(jnp.bfloat16)
    cot = window[1, :, : lay.strip].reshape(2 * lay.side, lay.channels)
    return product(basis_out[...], cot, ((0,), (0,))) * scale


def outer_kernel(lay, scale, near, outer, inner, grad, window, taps, basis_out):
    reach = lay.reach
    even = lax.axis_index("lat") % 2 == 0
    at_outer, at_near = jnp.where(even, 0, reach), jnp.where(even, reach, 0)
    for at, message in ((at_near, near), (at_outer, outer)):
        for row in range(reach):
            for field in range(2):
                start = field * lay.side + row * lay.strip
                put_row(lay, window, field, at + row, message[start : start + lay.strip])
        put_taps(taps, at, reach, message, 2 * lay.side)
    total = inner[...].astype(jnp.float32) + across(lay, scale, window, taps, basis_out)
    grad[...] = total.astype(jnp.bfloat16)


def middle_kernel(lay, scale, near, far, passed, grad, window, taps, basis_out):
    reach = lay.reach
    lat = lax.axis_index("lat")
    upper = (lat // 2) % 2 == 0
    first = lat % 2 == 0
    at_near, at_far = jnp.where(upper, 0, reach), jnp.where(upper, reach, 0)
    for row in range(reach):
        cells = slice(row * lay.strip, (row + 1) * lay.strip)
        put_row(lay, window, 0, at_far + row, jnp.where(first, far[cells], passed[cells]))
        put_row(lay, window, 1, at_far + row, jnp.where(first, passed[cells], far[cells]))
        for field in range(2):
            start = field * lay.side + row * lay.strip
            put_row(lay, window, field, at_near + row, near[start : start + lay.strip])
    put_taps(taps, at_near, reach, near, 2 * lay.side)
    put_taps(taps, at_far, reach, far, lay.side)
    grad[...] = across(lay, scale, window, taps, basis_out)


def field_kernel(
    lay, strip, filters, partner, outer, turned, turned_partner, turned_outer, weight,
    output, field_grad, window, taps, mixed,
):
    rows, reach, width, basis = lay.rows, lay.reach, lay.width, lay.basis
    even = lax.axis_index("lat") % 2 == 0
    at_outer, at_partner = jnp.where(even, 0, rows + reach), jnp.where(even, rows + reach, 0)
    for field in range(2):
        for row in range(rows):
            put_row(lay, window, field, reach + row, strip[field, row])
        for row in range(reach):
            start = (field * rows + row) * lay.strip
            last = start + (rows - reach) * lay.strip
            near = jnp.where(even, partner[start : start + lay.strip], partner[last : last + lay.strip])
            put_row(lay, window, field, at_partner + row, near)
            start = field * lay.side + row * lay.strip
            put_row(lay, window, field, at_outer + row, outer[start : start + lay.strip])

    def bands(row, is_turned):
        blocks = []
        for n in range(lay.taps):
            at, e = (row + n, lay.taps - 1 - n) if is_turned else (reach + row, n)
            parts = []
            for k in range(basis):
                spread = jnp.broadcast_to(taps[at, k, e : e + 1], (width, LANES))
                parts.append(pltpu.roll(spread, int(is_turned), 1, stride=1, stride_axis=0))
            blocks.append(jnp.concatenate(parts, axis=0).astype(jnp.bfloat16))
        return jnp.concatenate(blocks, axis=1)

    def put(at, message, start, count, is_turned):
        both = message[start : start + count * TAP_ROWS].astype(jnp.float32)
        for row in range(count):
            for k in range(basis):
                block = basis - 1 - k if is_turned else k
                taps[at + row, k] = lines(lay, both[row * TAP_ROWS : (row + 1) * TAP_ROWS], block)

    for field, is_turned, out in ((0, False, output), (1, True, field_grad)):
        if is_turned:
            put(reach, turned, 0, rows, True)
            put(at_partner, turned_partner, 0, reach, True)
            put(at_outer, turned_outer, 0, reach, True)
        else:
            put(reach, filters, 0, rows, False)
        for row in range(rows):
            source = window[field, row : row + lay.taps].reshape(lay.taps * LANES, lay.channels)
            result = product(bands(row, is_turned), source, ((1,), (0,))).astype(jnp.bfloat16)
            for k in range(basis):
                mixed[k, row * width : (row + 1) * width] = result[k * width : (k + 1) * width]
        total = jnp.zeros((rows * width, lay.channels), jnp.float32)
        for k in range(basis):
            total += product(mixed[k], weight[k], ((1,), (1 if is_turned else 0,)))
        out[...] = total.astype(jnp.bfloat16).reshape(out.shape)


def call(kernel, outs, scratch, flops, name):
    vmem = pl.BlockSpec(memory_space=pltpu.VMEM)

    def run(*operands):
        return pl.pallas_call(
            kernel,
            out_shape=outs,
            in_specs=[vmem] * len(operands),
            out_specs=[vmem] * len(outs),
            scratch_shapes=scratch,
            compiler_params=pltpu.CompilerParams(vmem_limit_bytes=32 * 1024 * 1024),
            cost_estimate=pl.CostEstimate(flops=flops, bytes_accessed=1_000_000, transcendentals=0),
            name=name,
        )(*operands)

    return run


def per_device(features, cotangent, weight, filter_taps, lat_ext, lon_count):
    rows, width, channels = features.shape
    basis = weight.shape[0]
    lat_taps = filter_taps.shape[2]
    lay = Layout(rows, lat_taps // 2, width, basis, channels)
    reach = lay.reach
    lat, lon = lax.axis_index("lat"), lax.axis_index("lon")
    even = lat % 2 == 0

    own = jnp.concatenate([features, cotangent], axis=0)
    west = shift(own, "lon", 1)
    own, lat_ext = lax.optimization_barrier((own, lat_ext))
    east = shift(own, "lon", -1)
    filters = make_filters(filter_taps, lat_ext, lon_count)
    filters = jnp.pad(jnp.swapaxes(filters, 1, 2), ((0, 0), (0, TAP_ROWS - lat_taps), (0, 0), (0, 0)))
    filters = filters.reshape(rows * TAP_ROWS, channels)

    strip = jnp.concatenate([west, own, east], axis=1).reshape(2, rows, lay.strip, channels)
    partner = flip(jnp.concatenate([strip.reshape(-1, channels), filters], axis=0), "lat", 1)
    partner_taps = partner[lay.cells :]

    def edge(cells, taps, bottom):
        start = jnp.where(bottom, rows - reach, 0)
        cells = lax.dynamic_slice_in_dim(cells.reshape(strip.shape), start, reach, 1)
        taps = lax.dynamic_slice_in_dim(taps, start * TAP_ROWS, reach * TAP_ROWS, 0)
        return jnp.concatenate([cells.reshape(-1, channels), taps], axis=0)

    upper = (lat // 2) % 2 == 0
    beside = (lat % 2 == 1) == upper
    near = jnp.where(beside, edge(strip, filters, upper), edge(partner[: lay.cells], partner_taps, upper))
    piece = lax.dynamic_slice_in_dim(near, (lat % 2) * lay.side, lay.side, 0)
    far = flip(jnp.concatenate([piece, near[2 * lay.side :]], axis=0), "lat", 2)

    def scratch(window_rows, basis_rows):
        return [
            pltpu.VMEM((2, window_rows, LANES, channels), jnp.bfloat16),
            pltpu.VMEM((window_rows, TAP_ROWS, channels), jnp.float32),
            pltpu.VMEM((basis_rows, channels), jnp.bfloat16),
        ]

    scale = 1.0 / math.sqrt(rows * lax.axis_size("lat") * width * lax.axis_size("lon"))
    share = jax.ShapeDtypeStruct((channels, channels), jnp.bfloat16)
    edges = scratch(2 * reach, 2 * lay.side)
    (grad,) = call(
        functools.partial(inner_kernel, lay, scale),
        [share],
        scratch(2 * rows, 2 * rows * lay.strip),
        INNER_FLOPS,
        "weight_inner",
    )(strip, filters, partner)
    outer = None
    if lax.axis_size("lat") > 4:
        bottom = jnp.logical_not(even)
        outward = edge(strip, filters, bottom)
        outer = outer_swap(outward, "lat")
        (grad,) = call(functools.partial(outer_kernel, lay, scale), [share], edges, MIDDLE_FLOPS, "weight_outer")(
            outward, outer, grad
        )
    got = flip(grad, "lat", 2)
    far, grad = lax.optimization_barrier((far, grad))
    passed = flip(far[: lay.side], "lat", 1)
    (middle,) = call(
        functools.partial(middle_kernel, lay, scale),
        [jax.ShapeDtypeStruct((channels, channels), jnp.float32)],
        edges,
        MIDDLE_FLOPS,
        "weight_middle",
    )(near, far, passed)
    grad = (grad.astype(jnp.float32) + got.astype(jnp.float32) + middle).astype(jnp.bfloat16)

    beyond = jnp.concatenate(
        [jnp.where(even, far[: lay.side], passed), jnp.where(even, passed, far[: lay.side]), far[lay.side :]], axis=0
    )
    outer = jnp.where(beside, beyond, jnp.zeros_like(beyond) if outer is None else outer)
    output, field_grad = call(
        functools.partial(field_kernel, lay),
        [jax.ShapeDtypeStruct(features.shape, jnp.bfloat16)] * 2,
        [
            pltpu.VMEM((2, rows + 2 * reach, LANES, channels), jnp.bfloat16),
            pltpu.VMEM((rows + 2 * reach, basis, TAP_ROWS, LANES), jnp.float32),
            pltpu.VMEM((basis, rows * width, channels), jnp.bfloat16),
        ],
        FIELD_FLOPS,
        "fields",
    )(
        strip,
        filters,
        partner,
        outer,
        filters[:, ::-1],
        edge(partner[: lay.cells], partner_taps, jnp.logical_not(even))[2 * lay.side :, ::-1],
        outer[2 * lay.side :, ::-1],
        weight,
    )

    others = [("lat", 1 << b) for b in range(2, lax.axis_size("lat").bit_length() - 1)]
    others += [("lon", 1 << b) for b in range(1, lax.axis_size("lon").bit_length() - 1)]
    for step, (axis, bit) in enumerate(others):
        if step == 1:
            grad, output, field_grad = lax.optimization_barrier((grad, output, field_grad))
        total = grad.astype(jnp.float32) + flip(grad, axis, bit).astype(jnp.float32)
        grad = total.astype(jnp.bfloat16)
    for axis, index in (("lon", lon), ("lat", lat)):
        got = flip(grad, axis, 1)
        second = index % 2 == 1
        grad = jnp.concatenate([jnp.where(second, got, grad), jnp.where(second, grad, got)], axis=0)
    weight_grad = grad.astype(jnp.float32).reshape(basis, channels, channels)
    return (output, field_grad, weight_grad)


def solution(mesh):
    in_specs = (
        P("lat", "lon", None),
        P("lat", "lon", None),
        P(),
        P("lat", None, None, None),
        P("lat"),
        P("lat"),
    )
    out_specs = (P("lat", "lon", None), P("lat", "lon", None), P())
    return jax.shard_map(
        per_device, mesh=mesh, in_specs=in_specs, out_specs=out_specs, check_vma=False
    )
```

time: 45.5 us -> 43.5 us (0.956)
  the two profiles are of different devices: /device:TPU:0 before, /device:TPU:3 now
where the time goes in v5:
time: 43.5 us; the launch traced here: 43.4 us
  waiting for transfers between devices  19.1 us (44%)
  starting transfers between devices  16.3 us (37%)
  Pallas kernels  3.63 us (8%)
  other arithmetic  1.82 us (4%)
  local copies, waits for them, and re-layouts  1.69 us (4%)
  between operations  0.91 us (2%)
    ppermute x8, waiting for transfers between devices, flip(): return lax.ppermute(block, axis, [(i, i ^ bit) for i in range(count)])  16.6 us
    ppermute x8, starting transfers between devices, flip(): return lax.ppermute(block, axis, [(i, i ^ bit) for i in range(count)])  11.9 us
    ppermute x2, starting transfers between devices, shift(): lax.ppermute(block, axis, [(i, (i + by) % count) for i in range(count)])  4.4 us
    pallas_call x3, Pallas kernels, run(): pl.pallas_call(kernel, out_shape=outs, in_specs=[vmem] * len(operands), o...  3.63 us
    ppermute x2, waiting for transfers between devices, shift(): lax.ppermute(block, axis, [(i, (i + by) % count) for i in range(count)])  2.51 us
    convert_element_type x1, other arithmetic, per_device(): weight_grad = grad.astype(jnp.float32).reshape(basis, channels, channels)  1.06 us
    unnamed x13, local copies, waits for them, and re-layouts  0.92 us
  transfers between devices with their start and end apart: 10, of which 8 were waited for; matrix products, arithmetic and copies ran while one was open for 2% of the time, Pallas kernels for 8%

profile of v5, /device:TPU:3, one launch (start us, length us, event | category | flops | bytes accessed | tf_op | source)
XLA Modules:
  0.0 43.4 jit_solution(12578753747514356005)
XLA Ops:
  0.6 0.0 copy-start.1
  0.6 0.9 %constant_dynamic-update-slice_fusion.1 = bf16[8,32,256]{2,1,0:T(8,128)(2,1)S(1)} fusion(bf16[4,32,256]{2,1,0:T(8,128)(2,1)} %param.6), kind=kLoop, calls=%fused_computation.19 | loop fusion | bytes 131072
  1.5 0.0 copy-done.1
  1.5 0.0 copy-start.3
  1.5 0.0 copy-start.4
  1.6 0.0 copy-start.2
  1.6 1.3 %collective-permute-start = (bf16[8,32,256]{2,1,0:T(8,128)(2,1)S(1)}, bf16[8,32,256]{2,1,0:T(8,128)(2,1)S(1)}, u32[]{:S(2)}, u32[]{:S(2)}) collective-permute-start(bf16[8,32,256]{2,1,0:T(8,128)(2,1)S(1)} %constant_dynamic-update-slice_fusion), channel_id=1, source_target_pairs={{0,1},{1,2},{2,3},{3,4},{4,5},{5,6},{6,7},{7,0},{8,9},{9,10},{10,1... | collective-permute-start | bytes 393224 | tf_op jit(solution)/shard_map/ppermute | solution.py:20
  2.9 3.1 %collective-permute-start.1 = (bf16[8,32,256]{2,1,0:T(8,128)(2,1)S(1)}, bf16[8,32,256]{2,1,0:T(8,128)(2,1)S(1)}, u32[]{:S(2)}, u32[]{:S(2)}) collective-permute-start(bf16[8,32,256]{2,1,0:T(8,128)(2,1)S(1)} %constant_dynamic-update-slice_fusion), channel_id=1, source_target_pairs={{0,7},{1,0},{2,1},{3,2},{4,3},{5,4},{6,5},{7,6},{8,15},{9,8},{10,9... | collective-permute-start | bytes 393224 | tf_op jit(solution)/shard_map/ppermute | solution.py:20
  6.0 0.0 copy-done.3
  6.0 0.0 copy-done.4
  6.0 0.1 broadcast_compare_fusion
  6.1 0.1 broadcast_compare_fusion.1
  6.1 0.1 and_convert_fusion
  6.2 0.0 copy-done.2
  6.2 0.1 fusion
  6.3 0.1 reshape.103.filters
  6.4 2.5 %collective-permute-done = bf16[8,32,256]{2,1,0:T(8,128)(2,1)S(1)} collective-permute-done((bf16[8,32,256]{2,1,0:T(8,128)(2,1)S(1)}, bf16[8,32,256]{2,1,0:T(8,128)(2,1)S(1)}, u32[]{:S(2)}, u32[]{:S(2)}) %collective-permute-start) | collective-permute-done | bytes 131104 | tf_op jit(solution)/shard_map/ppermute | solution.py:20
  9.0 0.0 collective-permute-done.1
  9.0 2.7 %collective-permute-start.2 = (bf16[800,256]{1,0:T(8,128)(2,1)S(1)}, bf16[800,256]{1,0:T(8,128)(2,1)S(1)}, u32[]{:S(2)}, u32[]{:S(2)}) collective-permute-start(bf16[800,256]{1,0:T(8,128)(2,1)S(1)} %pad_maximum_fusion.1), channel_id=1, source_target_pairs={{0,8},{8,0},{16,24},{24,16},{1,9},{9,1},{17,25},{25,17},{2,10},{10... | collective-permute-start | bytes 1228808 | tf_op jit(solution)/shard_map/ppermute | solution.py:25
  11.7 1.4 %collective-permute-done.2.partner = bf16[800,256]{1,0:T(8,128)(2,1)S(1)} collective-permute-done((bf16[800,256]{1,0:T(8,128)(2,1)S(1)}, bf16[800,256]{1,0:T(8,128)(2,1)S(1)}, u32[]{:S(2)}, u32[]{:S(2)}) %collective-permute-start.2) | collective-permute-done | bytes 409632 | tf_op jit(solution)/shard_map/ppermute | solution.py:25
  13.2 0.1 maximum_select_fusion.near
  13.3 0.3 collective-permute-start.3
  13.6 1.2 %weight_inner.1 = bf16[256,256]{1,0:T(8,128)(2,1)S(1)} custom-call(bf16[2,4,96,256]{3,2,1,0:T(8,128)(2,1)S(1)} %bitcast.11, bf16[32,256]{1,0:T(8,128)(2,1)S(1)} %reshape.103.filters, bf16[800,256]{1,0:T(8,128)(2,1)S(1)} %collective-permute-done.2.partner), custom_call_target="tpu_custom_call" | custom-call | flops 300000000 | bytes 1000000 | tf_op jit(solution)/shard_map/weight_inner/pallas_call | solution.py:252
  14.8 1.3 %collective-permute-start.4 = (bf16[256,256]{1,0:T(8,128)(2,1)S(1)}, bf16[256,256]{1,0:T(8,128)(2,1)S(1)}, u32[]{:S(2)}, u32[]{:S(2)}) collective-permute-start(bf16[256,256]{1,0:T(8,128)(2,1)S(1)} %weight_inner.1), channel_id=1, source_target_pairs={{0,16},{8,24},{16,0},{24,8},{1,17},{9,25},{17,1},{25,9},{2,18},{10... | collective-permute-start | bytes 393224 | tf_op jit(solution)/shard_map/ppermute | solution.py:25
  16.0 1.5 %collective-permute-done.3.far = bf16[208,256]{1,0:T(8,128)(2,1)S(1)} collective-permute-done((bf16[208,256]{1,0:T(8,128)(2,1)S(1)}, bf16[208,256]{1,0:T(8,128)(2,1)S(1)}, u32[]{:S(2)}, u32[]{:S(2)}) %collective-permute-start.3) | collective-permute-done | bytes 106528 | tf_op jit(solution)/shard_map/ppermute | solution.py:25
  17.5 2.1 %collective-permute-start.5 = (bf16[192,256]{1,0:T(8,128)(2,1)S(1)}, bf16[192,256]{1,0:T(8,128)(2,1)S(1)}, u32[]{:S(2)}, u32[]{:S(2)}) collective-permute-start(bf16[192,256]{1,0:T(8,128)(2,1)S(1)} %slice.23), channel_id=1, source_target_pairs={{0,8},{8,0},{16,24},{24,16},{1,9},{9,1},{17,25},{25,17},{2,10},{10... | collective-permute-start | bytes 294920 | tf_op jit(solution)/shard_map/ppermute | solution.py:25
  19.6 0.2 rev.9.turned
  19.8 0.2 rev.10.turned_partner
  19.9 0.6 %collective-permute-done.5.passed = bf16[192,256]{1,0:T(8,128)(2,1)S(1)} collective-permute-done((bf16[192,256]{1,0:T(8,128)(2,1)S(1)}, bf16[192,256]{1,0:T(8,128)(2,1)S(1)}, u32[]{:S(2)}, u32[]{:S(2)}) %collective-permute-start.5) | collective-permute-done | bytes 98336 | tf_op jit(solution)/shard_map/ppermute | solution.py:25
  20.5 0.7 %weight_middle.1 = f32[256,256]{1,0:T(8,128)S(1)} custom-call(bf16[400,256]{1,0:T(8,128)(2,1)S(1)} %maximum_select_fusion.near, bf16[208,256]{1,0:T(8,128)(2,1)S(1)} %collective-permute-done.3.far, bf16[192,256]{1,0:T(8,128)(2,1)S(1)} %collective-permute-done.5.passed), custom_call_target="tpu_custom_call" | custom-call | flops 100000000 | bytes 1000000 | tf_op jit(solution)/shard_map/weight_middle/pallas_call | solution.py:252
  21.2 0.0 collective-permute-done.4
  21.3 0.0 copy-start
  21.3 1.0 %collective-permute-start.6 = (bf16[256,256]{1,0:T(8,128)(2,1)S(1)}, bf16[256,256]{1,0:T(8,128)(2,1)S(1)}, u32[]{:S(2)}, u32[]{:S(2)}) collective-permute-start(bf16[256,256]{1,0:T(8,128)(2,1)S(1)} %add_convert_fusion.2), channel_id=1, source_target_pairs={{0,2},{1,3},{2,0},{3,1},{4,6},{5,7},{6,4},{7,5},{8,10},{9,11},{10,... | collective-permute-start | bytes 393224 | tf_op jit(solution)/shard_map/ppermute | solution.py:25
  22.4 0.2 rev.11.turned_outer
  22.6 0.0 copy-done
  22.6 1.8 %fields.1 = (bf16[4,32,256]{2,1,0:T(8,128)(2,1)}, bf16[4,32,256]{2,1,0:T(8,128)(2,1)}) custom-call(bf16[2,4,96,256]{3,2,1,0:T(8,128)(2,1)S(1)} %bitcast.12, bf16[32,256]{1,0:T(8,128)(2,1)S(1)} %reshape.103.filters, bf16[800,256]{1,0:T(8,128)(2,1)S(1)} %collective-permute-done.2.partner, bf16[400,256]{1,0:T(8,128)(2,1)S(1)} %maximum_select_fusion.1.outer, ...), custom_call_target="tpu_custom_call" | custom-call | flops 400000000 | bytes 1000000 | tf_op jit(solution)/shard_map/fields/pallas_call | solution.py:252
  24.4 1.7 %collective-permute-done.6 = bf16[256,256]{1,0:T(8,128)(2,1)S(1)} collective-permute-done((bf16[256,256]{1,0:T(8,128)(2,1)S(1)}, bf16[256,256]{1,0:T(8,128)(2,1)S(1)}, u32[]{:S(2)}, u32[]{:S(2)}) %collective-permute-start.6) | collective-permute-done | bytes 131104 | tf_op jit(solution)/shard_map/ppermute | solution.py:25
  26.1 2.0 %collective-permute-start.7 = (bf16[256,256]{1,0:T(8,128)(2,1)S(1)}, bf16[256,256]{1,0:T(8,128)(2,1)S(1)}, u32[]{:S(2)}, u32[]{:S(2)}) collective-permute-start(bf16[256,256]{1,0:T(8,128)(2,1)S(1)} %add_convert_fusion.1), channel_id=1, source_target_pairs={{0,4},{1,5},{2,6},{3,7},{4,0},{5,1},{6,2},{7,3},{8,12},{9,13},{10,... | collective-permute-start | bytes 393224 | tf_op jit(solution)/shard_map/ppermute | solution.py:25
  28.2 6.4 %collective-permute-done.7 = bf16[256,256]{1,0:T(8,128)(2,1)S(1)} collective-permute-done((bf16[256,256]{1,0:T(8,128)(2,1)S(1)}, bf16[256,256]{1,0:T(8,128)(2,1)S(1)}, u32[]{:S(2)}, u32[]{:S(2)}) %collective-permute-start.7) | collective-permute-done | bytes 131104 | tf_op jit(solution)/shard_map/ppermute | solution.py:25
  34.6 0.1 collective-permute-start.8
  34.7 3.8 %collective-permute-done.8 = bf16[256,256]{1,0:T(8,128)(2,1)S(1)} collective-permute-done((bf16[256,256]{1,0:T(8,128)(2,1)S(1)}, bf16[256,256]{1,0:T(8,128)(2,1)S(1)}, u32[]{:S(2)}, u32[]{:S(2)}) %collective-permute-start.8) | collective-permute-done | bytes 131104 | tf_op jit(solution)/shard_map/ppermute | solution.py:25
  38.6 2.4 %collective-permute-start.9 = (bf16[512,256]{1,0:T(8,128)(2,1)S(1)}, bf16[512,256]{1,0:T(8,128)(2,1)S(1)}, u32[]{:S(2)}, u32[]{:S(2)}) collective-permute-start(bf16[512,256]{1,0:T(8,128)(2,1)S(1)} %pad_maximum_fusion.2), channel_id=1, source_target_pairs={{0,8},{8,0},{16,24},{24,16},{1,9},{9,1},{17,25},{25,17},{2,10},{10... | collective-permute-start | bytes 786440 | tf_op jit(solution)/shard_map/ppermute | solution.py:25
  41.0 1.2 %collective-permute-done.9 = bf16[512,256]{1,0:T(8,128)(2,1)S(1)} collective-permute-done((bf16[512,256]{1,0:T(8,128)(2,1)S(1)}, bf16[512,256]{1,0:T(8,128)(2,1)S(1)}, u32[]{:S(2)}, u32[]{:S(2)}) %collective-permute-start.9) | collective-permute-done | bytes 262176 | tf_op jit(solution)/shard_map/ppermute | solution.py:25
  42.2 0.1 broadcast_select_fusion.1
  42.3 1.1 %convert.1 = f32[4,256,256]{2,1,0:T(8,128)} convert(bf16[4,256,256]{2,1,0:T(8,128)(2,1)S(1)} %bitcast.13) | non-fusion elementwise | flops 262144 | bytes 1572864 | tf_op jit(solution)/shard_map/convert_element_type | solution.py:372
  (29 shorter events, 0.5 us)
Async XLA Ops:
  0.6 0.9 %copy-start.1 = (bf16[4,32,256]{2,1,0:T(8,128)(2,1)S(1)}, bf16[4,32,256]{2,1,0:T(8,128)(2,1)}, u32[]{:S(2)}) copy-start(bf16[4,32,256]{2,1,0:T(8,128)(2,1)} %param.7) | copy-start | bytes 196612
  1.5 4.5 %copy-start.3 = (s32[4]{0:T(128)S(1)}, s32[4]{0:T(128)}, u32[]{:S(2)}) copy-start(s32[4]{0:T(128)} %param.11) | copy-start | bytes 52
  1.5 4.5 %copy-start.4 = (s32[4]{0:T(128)S(1)}, s32[4]{0:T(128)}, u32[]{:S(2)}) copy-start(s32[4]{0:T(128)} %param.10) | copy-start | bytes 52
  1.6 4.7 %copy-start.2 = (bf16[4,4,5,64]{3,1,2,0:T(4,128)(2,1)S(1)}, bf16[4,4,5,64]{3,1,2,0:T(4,128)(2,1)}, u32[]{:S(2)}) copy-start(bf16[4,4,5,64]{3,1,2,0:T(4,128)(2,1)} %param.9) | copy-start | bytes 30724
  1.6 7.4 %collective-permute-start = (bf16[8,32,256]{2,1,0:T(8,128)(2,1)S(1)}, bf16[8,32,256]{2,1,0:T(8,128)(2,1)S(1)}, u32[]{:S(2)}, u32[]{:S(2)}) collective-permute-start(bf16[8,32,256]{2,1,0:T(8,128)(2,1)S(1)} %constant_dynamic-update-slice_fusion), channel_id=1, source_target_pairs={{0,1},{1,2},{2,3},{3,4},{4,5},{5,6},{6,7},{7,0},{8,9},{9,10},{10,1... | collective-permute-start | bytes 393224 | tf_op jit(solution)/shard_map/ppermute | solution.py:20
  2.9 6.1 %collective-permute-start.1 = (bf16[8,32,256]{2,1,0:T(8,128)(2,1)S(1)}, bf16[8,32,256]{2,1,0:T(8,128)(2,1)S(1)}, u32[]{:S(2)}, u32[]{:S(2)}) collective-permute-start(bf16[8,32,256]{2,1,0:T(8,128)(2,1)S(1)} %constant_dynamic-update-slice_fusion), channel_id=1, source_target_pairs={{0,7},{1,0},{2,1},{3,2},{4,3},{5,4},{6,5},{7,6},{8,15},{9,8},{10,9... | collective-permute-start | bytes 393224 | tf_op jit(solution)/shard_map/ppermute | solution.py:20
  9.0 4.0 %collective-permute-start.2 = (bf16[800,256]{1,0:T(8,128)(2,1)S(1)}, bf16[800,256]{1,0:T(8,128)(2,1)S(1)}, u32[]{:S(2)}, u32[]{:S(2)}) collective-permute-start(bf16[800,256]{1,0:T(8,128)(2,1)S(1)} %pad_maximum_fusion.1), channel_id=1, source_target_pairs={{0,8},{8,0},{16,24},{24,16},{1,9},{9,1},{17,25},{25,17},{2,10},{10... | collective-permute-start | bytes 1228808 | tf_op jit(solution)/shard_map/ppermute | solution.py:25
  13.3 4.2 %collective-permute-start.3 = (bf16[208,256]{1,0:T(8,128)(2,1)S(1)}, bf16[208,256]{1,0:T(8,128)(2,1)S(1)}, u32[]{:S(2)}, u32[]{:S(2)}) collective-permute-start(bf16[208,256]{1,0:T(8,128)(2,1)S(1)} %pad_maximum_fusion.3), channel_id=1, source_target_pairs={{0,16},{8,24},{16,0},{24,8},{1,17},{9,25},{17,1},{25,9},{2,18},{10... | collective-permute-start | bytes 319496 | tf_op jit(solution)/shard_map/ppermute | solution.py:25
  14.8 6.5 %collective-permute-start.4 = (bf16[256,256]{1,0:T(8,128)(2,1)S(1)}, bf16[256,256]{1,0:T(8,128)(2,1)S(1)}, u32[]{:S(2)}, u32[]{:S(2)}) collective-permute-start(bf16[256,256]{1,0:T(8,128)(2,1)S(1)} %weight_inner.1), channel_id=1, source_target_pairs={{0,16},{8,24},{16,0},{24,8},{1,17},{9,25},{17,1},{25,9},{2,18},{10... | collective-permute-start | bytes 393224 | tf_op jit(solution)/shard_map/ppermute | solution.py:25
  17.5 3.0 %collective-permute-start.5 = (bf16[192,256]{1,0:T(8,128)(2,1)S(1)}, bf16[192,256]{1,0:T(8,128)(2,1)S(1)}, u32[]{:S(2)}, u32[]{:S(2)}) collective-permute-start(bf16[192,256]{1,0:T(8,128)(2,1)S(1)} %slice.23), channel_id=1, source_target_pairs={{0,8},{8,0},{16,24},{24,16},{1,9},{9,1},{17,25},{25,17},{2,10},{10... | collective-permute-start | bytes 294920 | tf_op jit(solution)/shard_map/ppermute | solution.py:25
  21.3 1.3 %copy-start = (bf16[4,256,256]{2,1,0:T(8,128)(2,1)S(1)}, bf16[4,256,256]{2,1,0:T(8,128)(2,1)}, u32[]{:S(2)}) copy-start(bf16[4,256,256]{2,1,0:T(8,128)(2,1)} %weight.1) | copy-start | bytes 1572868
  21.3 4.8 %collective-permute-start.6 = (bf16[256,256]{1,0:T(8,128)(2,1)S(1)}, bf16[256,256]{1,0:T(8,128)(2,1)S(1)}, u32[]{:S(2)}, u32[]{:S(2)}) collective-permute-start(bf16[256,256]{1,0:T(8,128)(2,1)S(1)} %add_convert_fusion.2), channel_id=1, source_target_pairs={{0,2},{1,3},{2,0},{3,1},{4,6},{5,7},{6,4},{7,5},{8,10},{9,11},{10,... | collective-permute-start | bytes 393224 | tf_op jit(solution)/shard_map/ppermute | solution.py:25
  26.1 8.5 %collective-permute-start.7 = (bf16[256,256]{1,0:T(8,128)(2,1)S(1)}, bf16[256,256]{1,0:T(8,128)(2,1)S(1)}, u32[]{:S(2)}, u32[]{:S(2)}) collective-permute-start(bf16[256,256]{1,0:T(8,128)(2,1)S(1)} %add_convert_fusion.1), channel_id=1, source_target_pairs={{0,4},{1,5},{2,6},{3,7},{4,0},{5,1},{6,2},{7,3},{8,12},{9,13},{10,... | collective-permute-start | bytes 393224 | tf_op jit(solution)/shard_map/ppermute | solution.py:25
  34.6 3.9 %collective-permute-start.8 = (bf16[256,256]{1,0:T(8,128)(2,1)S(1)}, bf16[256,256]{1,0:T(8,128)(2,1)S(1)}, u32[]{:S(2)}, u32[]{:S(2)}) collective-permute-start(bf16[256,256]{1,0:T(8,128)(2,1)S(1)} %add_convert_fusion), channel_id=1, source_target_pairs={{0,1},{1,0},{2,3},{3,2},{4,5},{5,4},{6,7},{7,6},{8,9},{9,8},{10,11... | collective-permute-start | bytes 393224 | tf_op jit(solution)/shard_map/ppermute | solution.py:25
  38.6 3.6 %collective-permute-start.9 = (bf16[512,256]{1,0:T(8,128)(2,1)S(1)}, bf16[512,256]{1,0:T(8,128)(2,1)S(1)}, u32[]{:S(2)}, u32[]{:S(2)}) collective-permute-start(bf16[512,256]{1,0:T(8,128)(2,1)S(1)} %pad_maximum_fusion.2), channel_id=1, source_target_pairs={{0,8},{8,0},{16,24},{24,16},{1,9},{9,1},{17,25},{25,17},{2,10},{10... | collective-permute-start | bytes 786440 | tf_op jit(solution)/shard_map/ppermute | solution.py:25

commit v6 on v5

--- a/solution.py
+++ b/solution.py
@@ -358,13 +358,21 @@
         weight,
     )
 
-    others = [("lat", 1 << b) for b in range(2, lax.axis_size("lat").bit_length() - 1)]
-    others += [("lon", 1 << b) for b in range(1, lax.axis_size("lon").bit_length() - 1)]
-    for step, (axis, bit) in enumerate(others):
+    lat_count, lon_count_devices = lax.axis_size("lat"), lax.axis_size("lon")
+    lat_bits = [1 << b for b in range(2, lat_count.bit_length() - 1)]
+    lon_bits = [1 << b for b in range(1, lon_count_devices.bit_length() - 1)]
+    rounds = [(bit, bit, 0, 0) for bit in lat_bits]
+    rounds += [(0, 0, up, down) for up, down in zip(lon_bits, lon_bits[::-1], strict=True)]
+    for step, (lat_even, lat_odd, lon_even, lon_odd) in enumerate(rounds):
         if step == 1:
             grad, output, field_grad = lax.optimization_barrier((grad, output, field_grad))
-        total = grad.astype(jnp.float32) + flip(grad, axis, bit).astype(jnp.float32)
-        grad = total.astype(jnp.bfloat16)
+        pairs = []
+        for a in range(lat_count):
+            lat_bit, lon_bit = (lat_odd, lon_odd) if a % 2 else (lat_even, lon_even)
+            for o in range(lon_count_devices):
+                pairs.append((a * lon_count_devices + o, (a ^ lat_bit) * lon_count_devices + (o ^ lon_bit)))
+        got = lax.ppermute(grad, ("lat", "lon"), pairs)
+        grad = (grad.astype(jnp.float32) + got.astype(jnp.float32)).astype(jnp.bfloat16)
     for axis, index in (("lon", lon), ("lat", lat)):
         got = flip(grad, axis, 1)
         second = index % 2 == 1

time: 43.5 us -> 42.8 us (0.984)
  waiting for transfers between devices: 19.1 us -> 16.6 us
  starting transfers between devices: 16.3 us -> 18 us
    ppermute x8 -> x6, waiting for transfers between devices: 16.6 us -> 8.41 us  [flip(): return lax.ppermute(block, axis, [(i, i ^ bit) for i in range(count)])]
    ppermute x0 -> x2, waiting for transfers between devices: none -> 5.71 us  [per_device(): got = lax.ppermute(grad, ('lat', 'lon'), pairs)]
    ppermute x0 -> x2, starting transfers between devices: none -> 2.29 us  [per_device(): got = lax.ppermute(grad, ('lat', 'lon'), pairs)]
    ppermute x8 -> x6, starting transfers between devices: 11.9 us -> 11.3 us  [flip(): return lax.ppermute(block, axis, [(i, i ^ bit) for i in range(count)])]
where the time goes in v6:
time: 42.8 us; the launch traced here: 42.7 us
  starting transfers between devices  18 us (42%)
  waiting for transfers between devices  16.6 us (39%)
  Pallas kernels  3.62 us (8%)
  other arithmetic  1.82 us (4%)
  local copies, waits for them, and re-layouts  1.69 us (4%)
  between operations  0.89 us (2%)
    ppermute x6, starting transfers between devices, flip(): return lax.ppermute(block, axis, [(i, i ^ bit) for i in range(count)])  11.3 us
    ppermute x6, waiting for transfers between devices, flip(): return lax.ppermute(block, axis, [(i, i ^ bit) for i in range(count)])  8.41 us
    ppermute x2, waiting for transfers between devices, per_device(): got = lax.ppermute(grad, ('lat', 'lon'), pairs)  5.71 us
    ppermute x2, starting transfers between devices, shift(): lax.ppermute(block, axis, [(i, (i + by) % count) for i in range(count)])  4.4 us
    pallas_call x3, Pallas kernels, run(): pl.pallas_call(kernel, out_shape=outs, in_specs=[vmem] * len(operands), o...  3.62 us
    ppermute x2, waiting for transfers between devices, shift(): lax.ppermute(block, axis, [(i, (i + by) % count) for i in range(count)])  2.51 us
    ppermute x2, starting transfers between devices, per_device(): got = lax.ppermute(grad, ('lat', 'lon'), pairs)  2.29 us
    convert_element_type x1, other arithmetic, per_device(): weight_grad = grad.astype(jnp.float32).reshape(basis, channels, channels)  1.06 us
  transfers between devices with their start and end apart: 10, of which 8 were waited for; matrix products, arithmetic and copies ran while one was open for 2% of the time, Pallas kernels for 8%

profile of v6, /device:TPU:3, one launch (start us, length us, event | category | flops | bytes accessed | tf_op | source)
XLA Modules:
  0.0 42.7 jit_solution(6931556762359809186)
XLA Ops:
  0.6 0.0 copy-start.1
  0.6 0.9 %constant_dynamic-update-slice_fusion.1 = bf16[8,32,256]{2,1,0:T(8,128)(2,1)S(1)} fusion(bf16[4,32,256]{2,1,0:T(8,128)(2,1)} %param.6), kind=kLoop, calls=%fused_computation.19 | loop fusion | bytes 131072
  1.5 0.0 copy-done.1
  1.5 0.0 copy-start.3
  1.5 0.0 copy-start.4
  1.6 0.0 copy-start.2
  1.6 1.3 %collective-permute-start = (bf16[8,32,256]{2,1,0:T(8,128)(2,1)S(1)}, bf16[8,32,256]{2,1,0:T(8,128)(2,1)S(1)}, u32[]{:S(2)}, u32[]{:S(2)}) collective-permute-start(bf16[8,32,256]{2,1,0:T(8,128)(2,1)S(1)} %constant_dynamic-update-slice_fusion), channel_id=1, source_target_pairs={{0,1},{1,2},{2,3},{3,4},{4,5},{5,6},{6,7},{7,0},{8,9},{9,10},{10,1... | collective-permute-start | bytes 393224 | tf_op jit(solution)/shard_map/ppermute | solution.py:20
  2.9 3.1 %collective-permute-start.1 = (bf16[8,32,256]{2,1,0:T(8,128)(2,1)S(1)}, bf16[8,32,256]{2,1,0:T(8,128)(2,1)S(1)}, u32[]{:S(2)}, u32[]{:S(2)}) collective-permute-start(bf16[8,32,256]{2,1,0:T(8,128)(2,1)S(1)} %constant_dynamic-update-slice_fusion), channel_id=1, source_target_pairs={{0,7},{1,0},{2,1},{3,2},{4,3},{5,4},{6,5},{7,6},{8,15},{9,8},{10,9... | collective-permute-start | bytes 393224 | tf_op jit(solution)/shard_map/ppermute | solution.py:20
  6.0 0.0 copy-done.3
  6.0 0.0 copy-done.4
  6.0 0.1 broadcast_compare_fusion
  6.1 0.1 broadcast_compare_fusion.1
  6.1 0.1 and_convert_fusion
  6.2 0.0 copy-done.2
  6.2 0.1 fusion
  6.3 0.1 reshape.103.filters
  6.4 2.5 %collective-permute-done = bf16[8,32,256]{2,1,0:T(8,128)(2,1)S(1)} collective-permute-done((bf16[8,32,256]{2,1,0:T(8,128)(2,1)S(1)}, bf16[8,32,256]{2,1,0:T(8,128)(2,1)S(1)}, u32[]{:S(2)}, u32[]{:S(2)}) %collective-permute-start) | collective-permute-done | bytes 131104 | tf_op jit(solution)/shard_map/ppermute | solution.py:20
  9.0 0.0 collective-permute-done.1
  9.0 2.7 %collective-permute-start.2 = (bf16[800,256]{1,0:T(8,128)(2,1)S(1)}, bf16[800,256]{1,0:T(8,128)(2,1)S(1)}, u32[]{:S(2)}, u32[]{:S(2)}) collective-permute-start(bf16[800,256]{1,0:T(8,128)(2,1)S(1)} %pad_maximum_fusion.1), channel_id=1, source_target_pairs={{0,8},{8,0},{16,24},{24,16},{1,9},{9,1},{17,25},{25,17},{2,10},{10... | collective-permute-start | bytes 1228808 | tf_op jit(solution)/shard_map/ppermute | solution.py:25
  11.7 1.4 %collective-permute-done.2.partner = bf16[800,256]{1,0:T(8,128)(2,1)S(1)} collective-permute-done((bf16[800,256]{1,0:T(8,128)(2,1)S(1)}, bf16[800,256]{1,0:T(8,128)(2,1)S(1)}, u32[]{:S(2)}, u32[]{:S(2)}) %collective-permute-start.2) | collective-permute-done | bytes 409632 | tf_op jit(solution)/shard_map/ppermute | solution.py:25
  13.2 0.1 maximum_select_fusion.near
  13.3 0.3 collective-permute-start.3
  13.6 1.2 %weight_inner.1 = bf16[256,256]{1,0:T(8,128)(2,1)S(1)} custom-call(bf16[2,4,96,256]{3,2,1,0:T(8,128)(2,1)S(1)} %bitcast.11, bf16[32,256]{1,0:T(8,128)(2,1)S(1)} %reshape.103.filters, bf16[800,256]{1,0:T(8,128)(2,1)S(1)} %collective-permute-done.2.partner), custom_call_target="tpu_custom_call" | custom-call | flops 300000000 | bytes 1000000 | tf_op jit(solution)/shard_map/weight_inner/pallas_call | solution.py:252
  14.8 1.3 %collective-permute-start.4 = (bf16[256,256]{1,0:T(8,128)(2,1)S(1)}, bf16[256,256]{1,0:T(8,128)(2,1)S(1)}, u32[]{:S(2)}, u32[]{:S(2)}) collective-permute-start(bf16[256,256]{1,0:T(8,128)(2,1)S(1)} %weight_inner.1), channel_id=1, source_target_pairs={{0,16},{8,24},{16,0},{24,8},{1,17},{9,25},{17,1},{25,9},{2,18},{10... | collective-permute-start | bytes 393224 | tf_op jit(solution)/shard_map/ppermute | solution.py:25
  16.0 1.5 %collective-permute-done.3.far = bf16[208,256]{1,0:T(8,128)(2,1)S(1)} collective-permute-done((bf16[208,256]{1,0:T(8,128)(2,1)S(1)}, bf16[208,256]{1,0:T(8,128)(2,1)S(1)}, u32[]{:S(2)}, u32[]{:S(2)}) %collective-permute-start.3) | collective-permute-done | bytes 106528 | tf_op jit(solution)/shard_map/ppermute | solution.py:25
  17.5 2.1 %collective-permute-start.5 = (bf16[192,256]{1,0:T(8,128)(2,1)S(1)}, bf16[192,256]{1,0:T(8,128)(2,1)S(1)}, u32[]{:S(2)}, u32[]{:S(2)}) collective-permute-start(bf16[192,256]{1,0:T(8,128)(2,1)S(1)} %slice.23), channel_id=1, source_target_pairs={{0,8},{8,0},{16,24},{24,16},{1,9},{9,1},{17,25},{25,17},{2,10},{10... | collective-permute-start | bytes 294920 | tf_op jit(solution)/shard_map/ppermute | solution.py:25
  19.6 0.2 rev.9.turned
  19.8 0.2 rev.10.turned_partner
  19.9 0.6 %collective-permute-done.5.passed = bf16[192,256]{1,0:T(8,128)(2,1)S(1)} collective-permute-done((bf16[192,256]{1,0:T(8,128)(2,1)S(1)}, bf16[192,256]{1,0:T(8,128)(2,1)S(1)}, u32[]{:S(2)}, u32[]{:S(2)}) %collective-permute-start.5) | collective-permute-done | bytes 98336 | tf_op jit(solution)/shard_map/ppermute | solution.py:25
  20.5 0.7 %weight_middle.1 = f32[256,256]{1,0:T(8,128)S(1)} custom-call(bf16[400,256]{1,0:T(8,128)(2,1)S(1)} %maximum_select_fusion.near, bf16[208,256]{1,0:T(8,128)(2,1)S(1)} %collective-permute-done.3.far, bf16[192,256]{1,0:T(8,128)(2,1)S(1)} %collective-permute-done.5.passed), custom_call_target="tpu_custom_call" | custom-call | flops 100000000 | bytes 1000000 | tf_op jit(solution)/shard_map/weight_middle/pallas_call | solution.py:252
  21.2 0.0 collective-permute-done.4
  21.3 0.0 copy-start
  21.3 2.0 %collective-permute-start.6 = (bf16[256,256]{1,0:T(8,128)(2,1)S(1)}, bf16[256,256]{1,0:T(8,128)(2,1)S(1)}, u32[]{:S(2)}, u32[]{:S(2)}) collective-permute-start(bf16[256,256]{1,0:T(8,128)(2,1)S(1)} %add_convert_fusion.2), channel_id=1, source_target_pairs={{0,2},{1,3},{2,0},{3,1},{4,6},{5,7},{6,4},{7,5},{8,12},{9,13},{10,... | collective-permute-start | bytes 393224 | tf_op jit(solution)/shard_map/ppermute | solution.py:374
  23.4 0.2 rev.11.turned_outer
  23.6 0.0 copy-done
  23.6 1.8 %fields.1 = (bf16[4,32,256]{2,1,0:T(8,128)(2,1)}, bf16[4,32,256]{2,1,0:T(8,128)(2,1)}) custom-call(bf16[2,4,96,256]{3,2,1,0:T(8,128)(2,1)S(1)} %bitcast.12, bf16[32,256]{1,0:T(8,128)(2,1)S(1)} %reshape.103.filters, bf16[800,256]{1,0:T(8,128)(2,1)S(1)} %collective-permute-done.2.partner, bf16[400,256]{1,0:T(8,128)(2,1)S(1)} %maximum_select_fusion.1.outer, ...), custom_call_target="tpu_custom_call" | custom-call | flops 400000000 | bytes 1000000 | tf_op jit(solution)/shard_map/fields/pallas_call | solution.py:252
  25.4 2.1 %collective-permute-done.6 = bf16[256,256]{1,0:T(8,128)(2,1)S(1)} collective-permute-done((bf16[256,256]{1,0:T(8,128)(2,1)S(1)}, bf16[256,256]{1,0:T(8,128)(2,1)S(1)}, u32[]{:S(2)}, u32[]{:S(2)}) %collective-permute-start.6) | collective-permute-done | bytes 131104 | tf_op jit(solution)/shard_map/ppermute | solution.py:374
  27.5 0.3 collective-permute-start.7
  27.8 3.6 %collective-permute-done.7 = bf16[256,256]{1,0:T(8,128)(2,1)S(1)} collective-permute-done((bf16[256,256]{1,0:T(8,128)(2,1)S(1)}, bf16[256,256]{1,0:T(8,128)(2,1)S(1)}, u32[]{:S(2)}, u32[]{:S(2)}) %collective-permute-start.7) | collective-permute-done | bytes 131104 | tf_op jit(solution)/shard_map/ppermute | solution.py:374
  31.4 0.1 collective-permute-start.8
  31.5 3.8 %collective-permute-done.8 = bf16[256,256]{1,0:T(8,128)(2,1)S(1)} collective-permute-done((bf16[256,256]{1,0:T(8,128)(2,1)S(1)}, bf16[256,256]{1,0:T(8,128)(2,1)S(1)}, u32[]{:S(2)}, u32[]{:S(2)}) %collective-permute-start.8) | collective-permute-done | bytes 131104 | tf_op jit(solution)/shard_map/ppermute | solution.py:25
  35.4 4.9 %collective-permute-start.9 = (bf16[512,256]{1,0:T(8,128)(2,1)S(1)}, bf16[512,256]{1,0:T(8,128)(2,1)S(1)}, u32[]{:S(2)}, u32[]{:S(2)}) collective-permute-start(bf16[512,256]{1,0:T(8,128)(2,1)S(1)} %pad_maximum_fusion.2), channel_id=1, source_target_pairs={{0,8},{8,0},{16,24},{24,16},{1,9},{9,1},{17,25},{25,17},{2,10},{10... | collective-permute-start | bytes 786440 | tf_op jit(solution)/shard_map/ppermute | solution.py:25
  40.3 1.2 %collective-permute-done.9 = bf16[512,256]{1,0:T(8,128)(2,1)S(1)} collective-permute-done((bf16[512,256]{1,0:T(8,128)(2,1)S(1)}, bf16[512,256]{1,0:T(8,128)(2,1)S(1)}, u32[]{:S(2)}, u32[]{:S(2)}) %collective-permute-start.9) | collective-permute-done | bytes 262176 | tf_op jit(solution)/shard_map/ppermute | solution.py:25
  41.5 0.1 broadcast_select_fusion.1
  41.6 1.1 %convert.1 = f32[4,256,256]{2,1,0:T(8,128)} convert(bf16[4,256,256]{2,1,0:T(8,128)(2,1)S(1)} %bitcast.13) | non-fusion elementwise | flops 262144 | bytes 1572864 | tf_op jit(solution)/shard_map/convert_element_type | solution.py:380
  (29 shorter events, 0.5 us)
Async XLA Ops:
  0.6 0.9 %copy-start.1 = (bf16[4,32,256]{2,1,0:T(8,128)(2,1)S(1)}, bf16[4,32,256]{2,1,0:T(8,128)(2,1)}, u32[]{:S(2)}) copy-start(bf16[4,32,256]{2,1,0:T(8,128)(2,1)} %param.7) | copy-start | bytes 196612
  1.5 4.5 %copy-start.3 = (s32[4]{0:T(128)S(1)}, s32[4]{0:T(128)}, u32[]{:S(2)}) copy-start(s32[4]{0:T(128)} %param.11) | copy-start | bytes 52
  1.5 4.5 %copy-start.4 = (s32[4]{0:T(128)S(1)}, s32[4]{0:T(128)}, u32[]{:S(2)}) copy-start(s32[4]{0:T(128)} %param.10) | copy-start | bytes 52
  1.6 4.7 %copy-start.2 = (bf16[4,4,5,64]{3,1,2,0:T(4,128)(2,1)S(1)}, bf16[4,4,5,64]{3,1,2,0:T(4,128)(2,1)}, u32[]{:S(2)}) copy-start(bf16[4,4,5,64]{3,1,2,0:T(4,128)(2,1)} %param.9) | copy-start | bytes 30724
  1.6 7.4 %collective-permute-start = (bf16[8,32,256]{2,1,0:T(8,128)(2,1)S(1)}, bf16[8,32,256]{2,1,0:T(8,128)(2,1)S(1)}, u32[]{:S(2)}, u32[]{:S(2)}) collective-permute-start(bf16[8,32,256]{2,1,0:T(8,128)(2,1)S(1)} %constant_dynamic-update-slice_fusion), channel_id=1, source_target_pairs={{0,1},{1,2},{2,3},{3,4},{4,5},{5,6},{6,7},{7,0},{8,9},{9,10},{10,1... | collective-permute-start | bytes 393224 | tf_op jit(solution)/shard_map/ppermute | solution.py:20
  2.9 6.1 %collective-permute-start.1 = (bf16[8,32,256]{2,1,0:T(8,128)(2,1)S(1)}, bf16[8,32,256]{2,1,0:T(8,128)(2,1)S(1)}, u32[]{:S(2)}, u32[]{:S(2)}) collective-permute-start(bf16[8,32,256]{2,1,0:T(8,128)(2,1)S(1)} %constant_dynamic-update-slice_fusion), channel_id=1, source_target_pairs={{0,7},{1,0},{2,1},{3,2},{4,3},{5,4},{6,5},{7,6},{8,15},{9,8},{10,9... | collective-permute-start | bytes 393224 | tf_op jit(solution)/shard_map/ppermute | solution.py:20
  9.0 4.0 %collective-permute-start.2 = (bf16[800,256]{1,0:T(8,128)(2,1)S(1)}, bf16[800,256]{1,0:T(8,128)(2,1)S(1)}, u32[]{:S(2)}, u32[]{:S(2)}) collective-permute-start(bf16[800,256]{1,0:T(8,128)(2,1)S(1)} %pad_maximum_fusion.1), channel_id=1, source_target_pairs={{0,8},{8,0},{16,24},{24,16},{1,9},{9,1},{17,25},{25,17},{2,10},{10... | collective-permute-start | bytes 1228808 | tf_op jit(solution)/shard_map/ppermute | solution.py:25
  13.3 4.2 %collective-permute-start.3 = (bf16[208,256]{1,0:T(8,128)(2,1)S(1)}, bf16[208,256]{1,0:T(8,128)(2,1)S(1)}, u32[]{:S(2)}, u32[]{:S(2)}) collective-permute-start(bf16[208,256]{1,0:T(8,128)(2,1)S(1)} %pad_maximum_fusion.3), channel_id=1, source_target_pairs={{0,16},{8,24},{16,0},{24,8},{1,17},{9,25},{17,1},{25,9},{2,18},{10... | collective-permute-start | bytes 319496 | tf_op jit(solution)/shard_map/ppermute | solution.py:25
  14.8 6.5 %collective-permute-start.4 = (bf16[256,256]{1,0:T(8,128)(2,1)S(1)}, bf16[256,256]{1,0:T(8,128)(2,1)S(1)}, u32[]{:S(2)}, u32[]{:S(2)}) collective-permute-start(bf16[256,256]{1,0:T(8,128)(2,1)S(1)} %weight_inner.1), channel_id=1, source_target_pairs={{0,16},{8,24},{16,0},{24,8},{1,17},{9,25},{17,1},{25,9},{2,18},{10... | collective-permute-start | bytes 393224 | tf_op jit(solution)/shard_map/ppermute | solution.py:25
  17.5 3.0 %collective-permute-start.5 = (bf16[192,256]{1,0:T(8,128)(2,1)S(1)}, bf16[192,256]{1,0:T(8,128)(2,1)S(1)}, u32[]{:S(2)}, u32[]{:S(2)}) collective-permute-start(bf16[192,256]{1,0:T(8,128)(2,1)S(1)} %slice.23), channel_id=1, source_target_pairs={{0,8},{8,0},{16,24},{24,16},{1,9},{9,1},{17,25},{25,17},{2,10},{10... | collective-permute-start | bytes 294920 | tf_op jit(solution)/shard_map/ppermute | solution.py:25
  21.3 2.3 %copy-start = (bf16[4,256,256]{2,1,0:T(8,128)(2,1)S(1)}, bf16[4,256,256]{2,1,0:T(8,128)(2,1)}, u32[]{:S(2)}) copy-start(bf16[4,256,256]{2,1,0:T(8,128)(2,1)} %weight.1) | copy-start | bytes 1572868
  21.3 6.2 %collective-permute-start.6 = (bf16[256,256]{1,0:T(8,128)(2,1)S(1)}, bf16[256,256]{1,0:T(8,128)(2,1)S(1)}, u32[]{:S(2)}, u32[]{:S(2)}) collective-permute-start(bf16[256,256]{1,0:T(8,128)(2,1)S(1)} %add_convert_fusion.2), channel_id=1, source_target_pairs={{0,2},{1,3},{2,0},{3,1},{4,6},{5,7},{6,4},{7,5},{8,12},{9,13},{10,... | collective-permute-start | bytes 393224 | tf_op jit(solution)/shard_map/ppermute | solution.py:374
  27.5 3.9 %collective-permute-start.7 = (bf16[256,256]{1,0:T(8,128)(2,1)S(1)}, bf16[256,256]{1,0:T(8,128)(2,1)S(1)}, u32[]{:S(2)}, u32[]{:S(2)}) collective-permute-start(bf16[256,256]{1,0:T(8,128)(2,1)S(1)} %add_convert_fusion.1), channel_id=1, source_target_pairs={{0,4},{1,5},{2,6},{3,7},{4,0},{5,1},{6,2},{7,3},{8,10},{9,11},{10,... | collective-permute-start | bytes 393224 | tf_op jit(solution)/shard_map/ppermute | solution.py:374
  31.4 3.9 %collective-permute-start.8 = (bf16[256,256]{1,0:T(8,128)(2,1)S(1)}, bf16[256,256]{1,0:T(8,128)(2,1)S(1)}, u32[]{:S(2)}, u32[]{:S(2)}) collective-permute-start(bf16[256,256]{1,0:T(8,128)(2,1)S(1)} %add_convert_fusion), channel_id=1, source_target_pairs={{0,1},{1,0},{2,3},{3,2},{4,5},{5,4},{6,7},{7,6},{8,9},{9,8},{10,11... | collective-permute-start | bytes 393224 | tf_op jit(solution)/shard_map/ppermute | solution.py:25
  35.4 6.1 %collective-permute-start.9 = (bf16[512,256]{1,0:T(8,128)(2,1)S(1)}, bf16[512,256]{1,0:T(8,128)(2,1)S(1)}, u32[]{:S(2)}, u32[]{:S(2)}) collective-permute-start(bf16[512,256]{1,0:T(8,128)(2,1)S(1)} %pad_maximum_fusion.2), channel_id=1, source_target_pairs={{0,8},{8,0},{16,24},{24,16},{1,9},{9,1},{17,25},{25,17},{2,10},{10... | collective-permute-start | bytes 786440 | tf_op jit(solution)/shard_map/ppermute | solution.py:25

commit v7 on v6

--- a/solution.py
+++ b/solution.py
@@ -243,6 +243,45 @@
         for k in range(basis):
             total += product(mixed[k], weight[k], ((1,), (1 if is_turned else 0,)))
         out[...] = total.astype(jnp.bfloat16).reshape(out.shape)
+
+
+def widen(part, out, at, wide, sems):
+    count = sems.shape[0]
+    size = part.shape[0] // count
+    copies = []
+    for piece in range(count):
+        rows = slice(piece * size, (piece + 1) * size)
+        wide[rows] = part[rows].astype(jnp.float32)
+        target = out.at[pl.ds(pl.multiple_of(at + piece * size, size), size)]
+        copies.append(pltpu.make_async_copy(wide.at[rows], target, sems.at[piece]))
+        copies[-1].start()
+    for copy in copies:
+        copy.wait()
+
+
+def first_kernel(part, out, wide, sems):
+    widen(part, out, (lax.axis_index("lat") % 2) * part.shape[0], wide, sems)
+
+
+def second_kernel(part, kept, out, wide, sems):
+    widen(part, out, (1 - lax.axis_index("lat") % 2) * part.shape[0], wide, sems)
+
+
+def store(part, kept=None):
+    rows, channels = part.shape
+    vmem, anywhere = pl.BlockSpec(memory_space=pltpu.VMEM), pl.BlockSpec(memory_space=pl.ANY)
+    pieces = 4
+    return pl.pallas_call(
+        first_kernel if kept is None else second_kernel,
+        out_shape=jax.ShapeDtypeStruct((2 * rows, channels), jnp.float32),
+        in_specs=[vmem] if kept is None else [vmem, anywhere],
+        out_specs=anywhere,
+        input_output_aliases={} if kept is None else {1: 0},
+        scratch_shapes=[pltpu.VMEM((rows, channels), jnp.float32), pltpu.SemaphoreType.DMA((pieces,))],
+        compiler_params=pltpu.CompilerParams(vmem_limit_bytes=32 * 1024 * 1024),
+        cost_estimate=pl.CostEstimate(flops=1_000_000, bytes_accessed=1_000_000, transcendentals=0),
+        name="store_first" if kept is None else "store_second",
+    )(*([part] if kept is None else [part, kept]))
 
 
 def call(kernel, outs, scratch, flops, name):
@@ -373,11 +412,11 @@
                 pairs.append((a * lon_count_devices + o, (a ^ lat_bit) * lon_count_devices + (o ^ lon_bit)))
         got = lax.ppermute(grad, ("lat", "lon"), pairs)
         grad = (grad.astype(jnp.float32) + got.astype(jnp.float32)).astype(jnp.bfloat16)
-    for axis, index in (("lon", lon), ("lat", lat)):
-        got = flip(grad, axis, 1)
-        second = index % 2 == 1
-        grad = jnp.concatenate([jnp.where(second, got, grad), jnp.where(second, grad, got)], axis=0)
-    weight_grad = grad.astype(jnp.float32).reshape(basis, channels, channels)
+    got = flip(grad, "lon", 1)
+    second = lon % 2 == 1
+    grad = jnp.concatenate([jnp.where(second, got, grad), jnp.where(second, grad, got)], axis=0)
+    got = flip(grad, "lat", 1)
+    weight_grad = store(got, store(grad)).reshape(basis, channels, channels)
     return (output, field_grad, weight_grad)
 
 

time: 42.8 us -> 42.5 us (level)
  Pallas kernels: 3.62 us -> 5.28 us
  other arithmetic: 1.82 us -> 0.62 us
  waiting for transfers between devices: 16.6 us -> 15.8 us
    pallas_call x0 -> x2, Pallas kernels: none -> 1.66 us  [store(): pl.pallas_call(first_kernel if kept is None else second_kernel, out_shape...]
    convert_element_type x1 -> x0, other arithmetic: 1.06 us -> none  [per_device(): weight_grad = grad.astype(jnp.float32).reshape(basis, channels, channels)]
    ppermute x6, waiting for transfers between devices: 8.41 us -> 7.57 us  [flip(): return lax.ppermute(block, axis, [(i, i ^ bit) for i in range(count)])]
  transfers between devices with their start and end apart: 10 -> 10, of which waited for: 8 -> 8; matrix products, arithmetic and copies ran while one was open for 2% -> 3% of each run, Pallas kernels for 8% -> 11%
where the time goes in v7:
time: 42.5 us; the launch traced here: 42.3 us
  starting transfers between devices  18 us (42%)
  waiting for transfers between devices  15.8 us (37%)
  Pallas kernels  5.28 us (12%)
  local copies, waits for them, and re-layouts  1.69 us (4%)
  between operations  0.88 us (2%)
  other arithmetic  0.62 us (1%)
    ppermute x6, starting transfers between devices, flip(): return lax.ppermute(block, axis, [(i, i ^ bit) for i in range(count)])  11.3 us
    ppermute x6, waiting for transfers between devices, flip(): return lax.ppermute(block, axis, [(i, i ^ bit) for i in range(count)])  7.57 us
    ppermute x2, waiting for transfers between devices, per_device(): got = lax.ppermute(grad, ('lat', 'lon'), pairs)  5.71 us
    ppermute x2, starting transfers between devices, shift(): lax.ppermute(block, axis, [(i, (i + by) % count) for i in range(count)])  4.4 us
    pallas_call x3, Pallas kernels, run(): pl.pallas_call(kernel, out_shape=outs, in_specs=[vmem] * len(operands), o...  3.62 us
    ppermute x2, waiting for transfers between devices, shift(): lax.ppermute(block, axis, [(i, (i + by) % count) for i in range(count)])  2.52 us
    ppermute x2, starting transfers between devices, per_device(): got = lax.ppermute(grad, ('lat', 'lon'), pairs)  2.29 us
    pallas_call x2, Pallas kernels, store(): pl.pallas_call(first_kernel if kept is None else second_kernel, out_shape...  1.66 us
  transfers between devices with their start and end apart: 10, of which 8 were waited for; matrix products, arithmetic and copies ran while one was open for 3% of the time, Pallas kernels for 11%

profile of v7, /device:TPU:3, one launch (start us, length us, event | category | flops | bytes accessed | tf_op | source)
XLA Modules:
  0.0 42.3 jit_solution(5920637885240318434)
XLA Ops:
  0.6 0.0 copy-start.1
  0.6 0.9 %constant_dynamic-update-slice_fusion.1 = bf16[8,32,256]{2,1,0:T(8,128)(2,1)S(1)} fusion(bf16[4,32,256]{2,1,0:T(8,128)(2,1)} %param.6), kind=kLoop, calls=%fused_computation.16 | loop fusion | bytes 131072
  1.5 0.0 copy-done.1
  1.5 0.0 copy-start.3
  1.5 0.0 copy-start.4
  1.6 0.0 copy-start.2
  1.6 1.3 %collective-permute-start = (bf16[8,32,256]{2,1,0:T(8,128)(2,1)S(1)}, bf16[8,32,256]{2,1,0:T(8,128)(2,1)S(1)}, u32[]{:S(2)}, u32[]{:S(2)}) collective-permute-start(bf16[8,32,256]{2,1,0:T(8,128)(2,1)S(1)} %constant_dynamic-update-slice_fusion), channel_id=1, source_target_pairs={{0,1},{1,2},{2,3},{3,4},{4,5},{5,6},{6,7},{7,0},{8,9},{9,10},{10,1... | collective-permute-start | bytes 393224 | tf_op jit(solution)/shard_map/ppermute | solution.py:20
  2.9 3.1 %collective-permute-start.1 = (bf16[8,32,256]{2,1,0:T(8,128)(2,1)S(1)}, bf16[8,32,256]{2,1,0:T(8,128)(2,1)S(1)}, u32[]{:S(2)}, u32[]{:S(2)}) collective-permute-start(bf16[8,32,256]{2,1,0:T(8,128)(2,1)S(1)} %constant_dynamic-update-slice_fusion), channel_id=1, source_target_pairs={{0,7},{1,0},{2,1},{3,2},{4,3},{5,4},{6,5},{7,6},{8,15},{9,8},{10,9... | collective-permute-start | bytes 393224 | tf_op jit(solution)/shard_map/ppermute | solution.py:20
  6.0 0.0 copy-done.3
  6.0 0.1 broadcast_compare_fusion
  6.0 0.0 copy-done.4
  6.1 0.1 broadcast_compare_fusion.1
  6.1 0.1 and_convert_fusion
  6.2 0.0 copy-done.2
  6.2 0.1 fusion
  6.3 0.1 reshape.102.filters
  6.4 2.5 %collective-permute-done = bf16[8,32,256]{2,1,0:T(8,128)(2,1)S(1)} collective-permute-done((bf16[8,32,256]{2,1,0:T(8,128)(2,1)S(1)}, bf16[8,32,256]{2,1,0:T(8,128)(2,1)S(1)}, u32[]{:S(2)}, u32[]{:S(2)}) %collective-permute-start) | collective-permute-done | bytes 131104 | tf_op jit(solution)/shard_map/ppermute | solution.py:20
  9.0 0.0 collective-permute-done.1
  9.0 2.7 %collective-permute-start.2 = (bf16[800,256]{1,0:T(8,128)(2,1)S(1)}, bf16[800,256]{1,0:T(8,128)(2,1)S(1)}, u32[]{:S(2)}, u32[]{:S(2)}) collective-permute-start(bf16[800,256]{1,0:T(8,128)(2,1)S(1)} %pad_maximum_fusion), channel_id=1, source_target_pairs={{0,8},{8,0},{16,24},{24,16},{1,9},{9,1},{17,25},{25,17},{2,10},{10... | collective-permute-start | bytes 1228808 | tf_op jit(solution)/shard_map/ppermute | solution.py:25
  11.7 1.4 %collective-permute-done.2.partner = bf16[800,256]{1,0:T(8,128)(2,1)S(1)} collective-permute-done((bf16[800,256]{1,0:T(8,128)(2,1)S(1)}, bf16[800,256]{1,0:T(8,128)(2,1)S(1)}, u32[]{:S(2)}, u32[]{:S(2)}) %collective-permute-start.2) | collective-permute-done | bytes 409632 | tf_op jit(solution)/shard_map/ppermute | solution.py:25
  13.2 0.1 maximum_select_fusion.near
  13.3 0.3 collective-permute-start.3
  13.6 1.2 %weight_inner.1 = bf16[256,256]{1,0:T(8,128)(2,1)S(1)} custom-call(bf16[2,4,96,256]{3,2,1,0:T(8,128)(2,1)S(1)} %bitcast.10, bf16[32,256]{1,0:T(8,128)(2,1)S(1)} %reshape.102.filters, bf16[800,256]{1,0:T(8,128)(2,1)S(1)} %collective-permute-done.2.partner), custom_call_target="tpu_custom_call" | custom-call | flops 300000000 | bytes 1000000 | tf_op jit(solution)/shard_map/weight_inner/pallas_call | solution.py:291
  14.8 1.3 %collective-permute-start.4 = (bf16[256,256]{1,0:T(8,128)(2,1)S(1)}, bf16[256,256]{1,0:T(8,128)(2,1)S(1)}, u32[]{:S(2)}, u32[]{:S(2)}) collective-permute-start(bf16[256,256]{1,0:T(8,128)(2,1)S(1)} %weight_inner.1), channel_id=1, source_target_pairs={{0,16},{8,24},{16,0},{24,8},{1,17},{9,25},{17,1},{25,9},{2,18},{10... | collective-permute-start | bytes 393224 | tf_op jit(solution)/shard_map/ppermute | solution.py:25
  16.0 1.5 %collective-permute-done.3.far = bf16[208,256]{1,0:T(8,128)(2,1)S(1)} collective-permute-done((bf16[208,256]{1,0:T(8,128)(2,1)S(1)}, bf16[208,256]{1,0:T(8,128)(2,1)S(1)}, u32[]{:S(2)}, u32[]{:S(2)}) %collective-permute-start.3) | collective-permute-done | bytes 106528 | tf_op jit(solution)/shard_map/ppermute | solution.py:25
  17.5 2.1 %collective-permute-start.5 = (bf16[192,256]{1,0:T(8,128)(2,1)S(1)}, bf16[192,256]{1,0:T(8,128)(2,1)S(1)}, u32[]{:S(2)}, u32[]{:S(2)}) collective-permute-start(bf16[192,256]{1,0:T(8,128)(2,1)S(1)} %slice.23), channel_id=1, source_target_pairs={{0,8},{8,0},{16,24},{24,16},{1,9},{9,1},{17,25},{25,17},{2,10},{10... | collective-permute-start | bytes 294920 | tf_op jit(solution)/shard_map/ppermute | solution.py:25
  19.6 0.2 rev.9.turned
  19.8 0.2 rev.10.turned_partner
  19.9 0.6 %collective-permute-done.5.passed = bf16[192,256]{1,0:T(8,128)(2,1)S(1)} collective-permute-done((bf16[192,256]{1,0:T(8,128)(2,1)S(1)}, bf16[192,256]{1,0:T(8,128)(2,1)S(1)}, u32[]{:S(2)}, u32[]{:S(2)}) %collective-permute-start.5) | collective-permute-done | bytes 98336 | tf_op jit(solution)/shard_map/ppermute | solution.py:25
  20.5 0.7 %weight_middle.1 = f32[256,256]{1,0:T(8,128)S(1)} custom-call(bf16[400,256]{1,0:T(8,128)(2,1)S(1)} %maximum_select_fusion.near, bf16[208,256]{1,0:T(8,128)(2,1)S(1)} %collective-permute-done.3.far, bf16[192,256]{1,0:T(8,128)(2,1)S(1)} %collective-permute-done.5.passed), custom_call_target="tpu_custom_call" | custom-call | flops 100000000 | bytes 1000000 | tf_op jit(solution)/shard_map/weight_middle/pallas_call | solution.py:291
  21.2 0.0 collective-permute-done.4
  21.3 0.0 copy-start
  21.3 2.0 %collective-permute-start.6 = (bf16[256,256]{1,0:T(8,128)(2,1)S(1)}, bf16[256,256]{1,0:T(8,128)(2,1)S(1)}, u32[]{:S(2)}, u32[]{:S(2)}) collective-permute-start(bf16[256,256]{1,0:T(8,128)(2,1)S(1)} %add_convert_fusion.2), channel_id=1, source_target_pairs={{0,2},{1,3},{2,0},{3,1},{4,6},{5,7},{6,4},{7,5},{8,12},{9,13},{10,... | collective-permute-start | bytes 393224 | tf_op jit(solution)/shard_map/ppermute | solution.py:413
  23.4 0.2 rev.11.turned_outer
  23.6 0.0 copy-done
  23.6 1.8 %fields.1 = (bf16[4,32,256]{2,1,0:T(8,128)(2,1)}, bf16[4,32,256]{2,1,0:T(8,128)(2,1)}) custom-call(bf16[2,4,96,256]{3,2,1,0:T(8,128)(2,1)S(1)} %bitcast.11, bf16[32,256]{1,0:T(8,128)(2,1)S(1)} %reshape.102.filters, bf16[800,256]{1,0:T(8,128)(2,1)S(1)} %collective-permute-done.2.partner, bf16[400,256]{1,0:T(8,128)(2,1)S(1)} %maximum_select_fusion.1.outer, ...), custom_call_target="tpu_custom_call" | custom-call | flops 400000000 | bytes 1000000 | tf_op jit(solution)/shard_map/fields/pallas_call | solution.py:291
  25.4 2.1 %collective-permute-done.6 = bf16[256,256]{1,0:T(8,128)(2,1)S(1)} collective-permute-done((bf16[256,256]{1,0:T(8,128)(2,1)S(1)}, bf16[256,256]{1,0:T(8,128)(2,1)S(1)}, u32[]{:S(2)}, u32[]{:S(2)}) %collective-permute-start.6) | collective-permute-done | bytes 131104 | tf_op jit(solution)/shard_map/ppermute | solution.py:413
  27.5 0.3 collective-permute-start.7
  27.8 3.6 %collective-permute-done.7 = bf16[256,256]{1,0:T(8,128)(2,1)S(1)} collective-permute-done((bf16[256,256]{1,0:T(8,128)(2,1)S(1)}, bf16[256,256]{1,0:T(8,128)(2,1)S(1)}, u32[]{:S(2)}, u32[]{:S(2)}) %collective-permute-start.7) | collective-permute-done | bytes 131104 | tf_op jit(solution)/shard_map/ppermute | solution.py:413
  31.4 0.1 collective-permute-start.8
  31.5 3.8 %collective-permute-done.8 = bf16[256,256]{1,0:T(8,128)(2,1)S(1)} collective-permute-done((bf16[256,256]{1,0:T(8,128)(2,1)S(1)}, bf16[256,256]{1,0:T(8,128)(2,1)S(1)}, u32[]{:S(2)}, u32[]{:S(2)}) %collective-permute-start.8) | collective-permute-done | bytes 131104 | tf_op jit(solution)/shard_map/ppermute | solution.py:25
  35.4 4.9 %collective-permute-start.9 = (bf16[512,256]{1,0:T(8,128)(2,1)S(1)}, bf16[512,256]{1,0:T(8,128)(2,1)S(1)}, u32[]{:S(2)}, u32[]{:S(2)}) collective-permute-start(bf16[512,256]{1,0:T(8,128)(2,1)S(1)} %pad_maximum_fusion.1.part), channel_id=1, source_target_pairs={{0,8},{8,0},{16,24},{24,16},{1,9},{9,1},{17,25},{25,17},{2,10},{10... | collective-permute-start | bytes 786440 | tf_op jit(solution)/shard_map/ppermute | solution.py:25
  40.3 0.8 %store_first.1.kept = f32[1024,256]{1,0:T(8,128)} custom-call(bf16[512,256]{1,0:T(8,128)(2,1)S(1)} %pad_maximum_fusion.1.part), custom_call_target="tpu_custom_call" | custom-call | flops 1000000 | bytes 1000000 | tf_op jit(solution)/shard_map/store_first/pallas_call | solution.py:274
  41.1 0.3 collective-permute-done.9.part
  41.5 0.8 %store_second.1 = f32[1024,256]{1,0:T(8,128)} custom-call(bf16[512,256]{1,0:T(8,128)(2,1)S(1)} %collective-permute-done.9.part, f32[1024,256]{1,0:T(8,128)} %store_first.1.kept), custom_call_target="tpu_custom_call", output_to_operand_aliasing={{}: (1, {})} | custom-call | flops 1000000 | bytes 1000000 | tf_op jit(solution)/shard_map/store_second/pallas_call | solution.py:274
  (28 shorter events, 0.4 us)
Async XLA Ops:
  0.6 0.9 %copy-start.1 = (bf16[4,32,256]{2,1,0:T(8,128)(2,1)S(1)}, bf16[4,32,256]{2,1,0:T(8,128)(2,1)}, u32[]{:S(2)}) copy-start(bf16[4,32,256]{2,1,0:T(8,128)(2,1)} %param.7) | copy-start | bytes 196612
  1.5 4.5 %copy-start.3 = (s32[4]{0:T(128)S(1)}, s32[4]{0:T(128)}, u32[]{:S(2)}) copy-start(s32[4]{0:T(128)} %param.11) | copy-start | bytes 52
  1.5 4.5 %copy-start.4 = (s32[4]{0:T(128)S(1)}, s32[4]{0:T(128)}, u32[]{:S(2)}) copy-start(s32[4]{0:T(128)} %param.10) | copy-start | bytes 52
  1.6 4.7 %copy-start.2 = (bf16[4,4,5,64]{3,1,2,0:T(4,128)(2,1)S(1)}, bf16[4,4,5,64]{3,1,2,0:T(4,128)(2,1)}, u32[]{:S(2)}) copy-start(bf16[4,4,5,64]{3,1,2,0:T(4,128)(2,1)} %param.9) | copy-start | bytes 30724
  1.6 7.4 %collective-permute-start = (bf16[8,32,256]{2,1,0:T(8,128)(2,1)S(1)}, bf16[8,32,256]{2,1,0:T(8,128)(2,1)S(1)}, u32[]{:S(2)}, u32[]{:S(2)}) collective-permute-start(bf16[8,32,256]{2,1,0:T(8,128)(2,1)S(1)} %constant_dynamic-update-slice_fusion), channel_id=1, source_target_pairs={{0,1},{1,2},{2,3},{3,4},{4,5},{5,6},{6,7},{7,0},{8,9},{9,10},{10,1... | collective-permute-start | bytes 393224 | tf_op jit(solution)/shard_map/ppermute | solution.py:20
  2.9 6.1 %collective-permute-start.1 = (bf16[8,32,256]{2,1,0:T(8,128)(2,1)S(1)}, bf16[8,32,256]{2,1,0:T(8,128)(2,1)S(1)}, u32[]{:S(2)}, u32[]{:S(2)}) collective-permute-start(bf16[8,32,256]{2,1,0:T(8,128)(2,1)S(1)} %constant_dynamic-update-slice_fusion), channel_id=1, source_target_pairs={{0,7},{1,0},{2,1},{3,2},{4,3},{5,4},{6,5},{7,6},{8,15},{9,8},{10,9... | collective-permute-start | bytes 393224 | tf_op jit(solution)/shard_map/ppermute | solution.py:20
  9.0 4.0 %collective-permute-start.2 = (bf16[800,256]{1,0:T(8,128)(2,1)S(1)}, bf16[800,256]{1,0:T(8,128)(2,1)S(1)}, u32[]{:S(2)}, u32[]{:S(2)}) collective-permute-start(bf16[800,256]{1,0:T(8,128)(2,1)S(1)} %pad_maximum_fusion), channel_id=1, source_target_pairs={{0,8},{8,0},{16,24},{24,16},{1,9},{9,1},{17,25},{25,17},{2,10},{10... | collective-permute-start | bytes 1228808 | tf_op jit(solution)/shard_map/ppermute | solution.py:25
  13.3 4.2 %collective-permute-start.3 = (bf16[208,256]{1,0:T(8,128)(2,1)S(1)}, bf16[208,256]{1,0:T(8,128)(2,1)S(1)}, u32[]{:S(2)}, u32[]{:S(2)}) collective-permute-start(bf16[208,256]{1,0:T(8,128)(2,1)S(1)} %pad_maximum_fusion.2), channel_id=1, source_target_pairs={{0,16},{8,24},{16,0},{24,8},{1,17},{9,25},{17,1},{25,9},{2,18},{10... | collective-permute-start | bytes 319496 | tf_op jit(solution)/shard_map/ppermute | solution.py:25
  14.8 6.5 %collective-permute-start.4 = (bf16[256,256]{1,0:T(8,128)(2,1)S(1)}, bf16[256,256]{1,0:T(8,128)(2,1)S(1)}, u32[]{:S(2)}, u32[]{:S(2)}) collective-permute-start(bf16[256,256]{1,0:T(8,128)(2,1)S(1)} %weight_inner.1), channel_id=1, source_target_pairs={{0,16},{8,24},{16,0},{24,8},{1,17},{9,25},{17,1},{25,9},{2,18},{10... | collective-permute-start | bytes 393224 | tf_op jit(solution)/shard_map/ppermute | solution.py:25
  17.5 3.0 %collective-permute-start.5 = (bf16[192,256]{1,0:T(8,128)(2,1)S(1)}, bf16[192,256]{1,0:T(8,128)(2,1)S(1)}, u32[]{:S(2)}, u32[]{:S(2)}) collective-permute-start(bf16[192,256]{1,0:T(8,128)(2,1)S(1)} %slice.23), channel_id=1, source_target_pairs={{0,8},{8,0},{16,24},{24,16},{1,9},{9,1},{17,25},{25,17},{2,10},{10... | collective-permute-start | bytes 294920 | tf_op jit(solution)/shard_map/ppermute | solution.py:25
  21.3 2.3 %copy-start = (bf16[4,256,256]{2,1,0:T(8,128)(2,1)S(1)}, bf16[4,256,256]{2,1,0:T(8,128)(2,1)}, u32[]{:S(2)}) copy-start(bf16[4,256,256]{2,1,0:T(8,128)(2,1)} %weight.1) | copy-start | bytes 1572868
  21.3 6.2 %collective-permute-start.6 = (bf16[256,256]{1,0:T(8,128)(2,1)S(1)}, bf16[256,256]{1,0:T(8,128)(2,1)S(1)}, u32[]{:S(2)}, u32[]{:S(2)}) collective-permute-start(bf16[256,256]{1,0:T(8,128)(2,1)S(1)} %add_convert_fusion.2), channel_id=1, source_target_pairs={{0,2},{1,3},{2,0},{3,1},{4,6},{5,7},{6,4},{7,5},{8,12},{9,13},{10,... | collective-permute-start | bytes 393224 | tf_op jit(solution)/shard_map/ppermute | solution.py:413
  27.5 3.9 %collective-permute-start.7 = (bf16[256,256]{1,0:T(8,128)(2,1)S(1)}, bf16[256,256]{1,0:T(8,128)(2,1)S(1)}, u32[]{:S(2)}, u32[]{:S(2)}) collective-permute-start(bf16[256,256]{1,0:T(8,128)(2,1)S(1)} %add_convert_fusion.1), channel_id=1, source_target_pairs={{0,4},{1,5},{2,6},{3,7},{4,0},{5,1},{6,2},{7,3},{8,10},{9,11},{10,... | collective-permute-start | bytes 393224 | tf_op jit(solution)/shard_map/ppermute | solution.py:413
  31.4 3.9 %collective-permute-start.8 = (bf16[256,256]{1,0:T(8,128)(2,1)S(1)}, bf16[256,256]{1,0:T(8,128)(2,1)S(1)}, u32[]{:S(2)}, u32[]{:S(2)}) collective-permute-start(bf16[256,256]{1,0:T(8,128)(2,1)S(1)} %add_convert_fusion), channel_id=1, source_target_pairs={{0,1},{1,0},{2,3},{3,2},{4,5},{5,4},{6,7},{7,6},{8,9},{9,8},{10,11... | collective-permute-start | bytes 393224 | tf_op jit(solution)/shard_map/ppermute | solution.py:25
  35.4 6.1 %collective-permute-start.9 = (bf16[512,256]{1,0:T(8,128)(2,1)S(1)}, bf16[512,256]{1,0:T(8,128)(2,1)S(1)}, u32[]{:S(2)}, u32[]{:S(2)}) collective-permute-start(bf16[512,256]{1,0:T(8,128)(2,1)S(1)} %pad_maximum_fusion.1.part), channel_id=1, source_target_pairs={{0,8},{8,0},{16,24},{24,16},{1,9},{9,1},{17,25},{25,17},{2,10},{10... | collective-permute-start | bytes 786440 | tf_op jit(solution)/shard_map/ppermute | solution.py:25

commit v8 on v7

--- a/solution.py
+++ b/solution.py
@@ -61,10 +61,6 @@
 def put_row(lay, window, field, at, cells):
     window[field, at, : lay.strip] = cells
     window[field, at, lay.strip :] = jnp.zeros((LANES - lay.strip, lay.channels), jnp.bfloat16)
-
-
-def tile(message, start, row):
-    return message[start + row * TAP_ROWS : start + (row + 1) * TAP_ROWS]
 
 
 def put_taps(taps, at, count, message, start):
@@ -332,8 +328,19 @@
     upper = (lat // 2) % 2 == 0
     beside = (lat % 2 == 1) == upper
     near = jnp.where(beside, edge(strip, filters, upper), edge(partner[: lay.cells], partner_taps, upper))
-    piece = lax.dynamic_slice_in_dim(near, (lat % 2) * lay.side, lay.side, 0)
-    far = flip(jnp.concatenate([piece, near[2 * lay.side :]], axis=0), "lat", 2)
+    at = (lat % 2) * rows * lay.strip + jnp.where(upper, rows - reach, 0) * lay.strip
+    at_taps = jnp.where(upper, rows - reach, 0) * TAP_ROWS
+    piece = jnp.where(
+        beside,
+        lax.dynamic_slice_in_dim(strip.reshape(-1, channels), at, lay.side, 0),
+        lax.dynamic_slice_in_dim(partner, at, lay.side, 0),
+    )
+    piece_taps = jnp.where(
+        beside,
+        lax.dynamic_slice_in_dim(filters, at_taps, reach * TAP_ROWS, 0),
+        lax.dynamic_slice_in_dim(partner, lay.cells + at_taps, reach * TAP_ROWS, 0),
+    )
+    far = flip(jnp.concatenate([piece, piece_taps], axis=0), "lat", 2)
 
     def scratch(window_rows, basis_rows):
         return [
@@ -397,19 +404,19 @@
         weight,
     )
 
-    lat_count, lon_count_devices = lax.axis_size("lat"), lax.axis_size("lon")
-    lat_bits = [1 << b for b in range(2, lat_count.bit_length() - 1)]
-    lon_bits = [1 << b for b in range(1, lon_count_devices.bit_length() - 1)]
+    lat_size, lon_size = lax.axis_size("lat"), lax.axis_size("lon")
+    lat_bits = [1 << b for b in range(2, lat_size.bit_length() - 1)]
+    lon_bits = [1 << b for b in range(1, lon_size.bit_length() - 1)]
     rounds = [(bit, bit, 0, 0) for bit in lat_bits]
     rounds += [(0, 0, up, down) for up, down in zip(lon_bits, lon_bits[::-1], strict=True)]
     for step, (lat_even, lat_odd, lon_even, lon_odd) in enumerate(rounds):
         if step == 1:
             grad, output, field_grad = lax.optimization_barrier((grad, output, field_grad))
         pairs = []
-        for a in range(lat_count):
+        for a in range(lat_size):
             lat_bit, lon_bit = (lat_odd, lon_odd) if a % 2 else (lat_even, lon_even)
-            for o in range(lon_count_devices):
-                pairs.append((a * lon_count_devices + o, (a ^ lat_bit) * lon_count_devices + (o ^ lon_bit)))
+            for o in range(lon_size):
+                pairs.append((a * lon_size + o, (a ^ lat_bit) * lon_size + (o ^ lon_bit)))
         got = lax.ppermute(grad, ("lat", "lon"), pairs)
         grad = (grad.astype(jnp.float32) + got.astype(jnp.float32)).astype(jnp.bfloat16)
     got = flip(grad, "lon", 1)

time: 42.5 us -> 42.3 us (level)
  no operation moved by 1% of the time
where the time goes in v8:
time: 42.3 us; the launch traced here: 42.2 us
  starting transfers between devices  18.1 us (43%)
  waiting for transfers between devices  15.6 us (37%)
  Pallas kernels  5.29 us (13%)
  local copies, waits for them, and re-layouts  1.69 us (4%)
  between operations  0.87 us (2%)
  other arithmetic  0.66 us (2%)
    ppermute x6, starting transfers between devices, flip(): return lax.ppermute(block, axis, [(i, i ^ bit) for i in range(count)])  11.4 us
    ppermute x6, waiting for transfers between devices, flip(): return lax.ppermute(block, axis, [(i, i ^ bit) for i in range(count)])  7.39 us
    ppermute x2, waiting for transfers between devices, per_device(): got = lax.ppermute(grad, ('lat', 'lon'), pairs)  5.7 us
    ppermute x2, starting transfers between devices, shift(): lax.ppermute(block, axis, [(i, (i + by) % count) for i in range(count)])  4.4 us
    pallas_call x3, Pallas kernels, run(): pl.pallas_call(kernel, out_shape=outs, in_specs=[vmem] * len(operands), o...  3.63 us
    ppermute x2, waiting for transfers between devices, shift(): lax.ppermute(block, axis, [(i, (i + by) % count) for i in range(count)])  2.52 us
    ppermute x2, starting transfers between devices, per_device(): got = lax.ppermute(grad, ('lat', 'lon'), pairs)  2.3 us
    pallas_call x2, Pallas kernels, store(): pl.pallas_call(first_kernel if kept is None else second_kernel, out_shape...  1.66 us
  transfers between devices with their start and end apart: 10, of which 8 were waited for; matrix products, arithmetic and copies ran while one was open for 3% of the time, Pallas kernels for 11%

profile of v8, /device:TPU:3, one launch (start us, length us, event | category | flops | bytes accessed | tf_op | source)
XLA Modules:
  0.0 42.2 jit_solution(11154577926070203950)
XLA Ops:
  0.6 0.0 copy-start.1
  0.6 0.9 %constant_dynamic-update-slice_fusion.1 = bf16[8,32,256]{2,1,0:T(8,128)(2,1)S(1)} fusion(bf16[4,32,256]{2,1,0:T(8,128)(2,1)} %param.6), kind=kLoop, calls=%fused_computation.17 | loop fusion | bytes 131072
  1.5 0.0 copy-done.1
  1.5 0.0 copy-start.3
  1.5 0.0 copy-start.4
  1.6 0.0 copy-start.2
  1.6 1.3 %collective-permute-start = (bf16[8,32,256]{2,1,0:T(8,128)(2,1)S(1)}, bf16[8,32,256]{2,1,0:T(8,128)(2,1)S(1)}, u32[]{:S(2)}, u32[]{:S(2)}) collective-permute-start(bf16[8,32,256]{2,1,0:T(8,128)(2,1)S(1)} %constant_dynamic-update-slice_fusion), channel_id=1, source_target_pairs={{0,1},{1,2},{2,3},{3,4},{4,5},{5,6},{6,7},{7,0},{8,9},{9,10},{10,1... | collective-permute-start | bytes 393224 | tf_op jit(solution)/shard_map/ppermute | solution.py:20
  2.9 3.1 %collective-permute-start.1 = (bf16[8,32,256]{2,1,0:T(8,128)(2,1)S(1)}, bf16[8,32,256]{2,1,0:T(8,128)(2,1)S(1)}, u32[]{:S(2)}, u32[]{:S(2)}) collective-permute-start(bf16[8,32,256]{2,1,0:T(8,128)(2,1)S(1)} %constant_dynamic-update-slice_fusion), channel_id=1, source_target_pairs={{0,7},{1,0},{2,1},{3,2},{4,3},{5,4},{6,5},{7,6},{8,15},{9,8},{10,9... | collective-permute-start | bytes 393224 | tf_op jit(solution)/shard_map/ppermute | solution.py:20
  6.0 0.0 copy-done.3
  6.0 0.1 broadcast_compare_fusion
  6.0 0.0 copy-done.4
  6.1 0.1 broadcast_compare_fusion.1
  6.1 0.1 and_convert_fusion
  6.2 0.0 copy-done.2
  6.2 0.1 fusion
  6.3 0.1 reshape.100.filters
  6.4 2.5 %collective-permute-done = bf16[8,32,256]{2,1,0:T(8,128)(2,1)S(1)} collective-permute-done((bf16[8,32,256]{2,1,0:T(8,128)(2,1)S(1)}, bf16[8,32,256]{2,1,0:T(8,128)(2,1)S(1)}, u32[]{:S(2)}, u32[]{:S(2)}) %collective-permute-start) | collective-permute-done | bytes 131104 | tf_op jit(solution)/shard_map/ppermute | solution.py:20
  9.0 0.0 collective-permute-done.1
  9.0 2.7 %collective-permute-start.2 = (bf16[800,256]{1,0:T(8,128)(2,1)S(1)}, bf16[800,256]{1,0:T(8,128)(2,1)S(1)}, u32[]{:S(2)}, u32[]{:S(2)}) collective-permute-start(bf16[800,256]{1,0:T(8,128)(2,1)S(1)} %pad_maximum_fusion), channel_id=1, source_target_pairs={{0,8},{8,0},{16,24},{24,16},{1,9},{9,1},{17,25},{25,17},{2,10},{10... | collective-permute-start | bytes 1228808 | tf_op jit(solution)/shard_map/ppermute | solution.py:25
  11.7 0.2 rev.9.turned
  11.9 1.2 %collective-permute-done.2.partner = bf16[800,256]{1,0:T(8,128)(2,1)S(1)} collective-permute-done((bf16[800,256]{1,0:T(8,128)(2,1)S(1)}, bf16[800,256]{1,0:T(8,128)(2,1)S(1)}, u32[]{:S(2)}, u32[]{:S(2)}) %collective-permute-start.2) | collective-permute-done | bytes 409632 | tf_op jit(solution)/shard_map/ppermute | solution.py:25
  13.1 0.3 collective-permute-start.3
  13.5 1.2 %weight_inner.1 = bf16[256,256]{1,0:T(8,128)(2,1)S(1)} custom-call(bf16[2,4,96,256]{3,2,1,0:T(8,128)(2,1)S(1)} %bitcast.11, bf16[32,256]{1,0:T(8,128)(2,1)S(1)} %reshape.100.filters, bf16[800,256]{1,0:T(8,128)(2,1)S(1)} %collective-permute-done.2.partner), custom_call_target="tpu_custom_call" | custom-call | flops 300000000 | bytes 1000000 | tf_op jit(solution)/shard_map/weight_inner/pallas_call | solution.py:287
  14.6 1.3 %collective-permute-start.4 = (bf16[256,256]{1,0:T(8,128)(2,1)S(1)}, bf16[256,256]{1,0:T(8,128)(2,1)S(1)}, u32[]{:S(2)}, u32[]{:S(2)}) collective-permute-start(bf16[256,256]{1,0:T(8,128)(2,1)S(1)} %weight_inner.1), channel_id=1, source_target_pairs={{0,16},{8,24},{16,0},{24,8},{1,17},{9,25},{17,1},{25,9},{2,18},{10... | collective-permute-start | bytes 393224 | tf_op jit(solution)/shard_map/ppermute | solution.py:25
  16.0 0.2 rev.10.turned_partner
  16.2 1.2 %collective-permute-done.3.far = bf16[208,256]{1,0:T(8,128)(2,1)S(1)} collective-permute-done((bf16[208,256]{1,0:T(8,128)(2,1)S(1)}, bf16[208,256]{1,0:T(8,128)(2,1)S(1)}, u32[]{:S(2)}, u32[]{:S(2)}) %collective-permute-start.3) | collective-permute-done | bytes 106528 | tf_op jit(solution)/shard_map/ppermute | solution.py:25
  17.4 2.1 %collective-permute-start.5 = (bf16[192,256]{1,0:T(8,128)(2,1)S(1)}, bf16[192,256]{1,0:T(8,128)(2,1)S(1)}, u32[]{:S(2)}, u32[]{:S(2)}) collective-permute-start(bf16[192,256]{1,0:T(8,128)(2,1)S(1)} %slice.19), channel_id=1, source_target_pairs={{0,8},{8,0},{16,24},{24,16},{1,9},{9,1},{17,25},{25,17},{2,10},{10... | collective-permute-start | bytes 294920 | tf_op jit(solution)/shard_map/ppermute | solution.py:25
  19.5 0.1 maximum_select_fusion.near
  19.5 0.9 %collective-permute-done.5.passed = bf16[192,256]{1,0:T(8,128)(2,1)S(1)} collective-permute-done((bf16[192,256]{1,0:T(8,128)(2,1)S(1)}, bf16[192,256]{1,0:T(8,128)(2,1)S(1)}, u32[]{:S(2)}, u32[]{:S(2)}) %collective-permute-start.5) | collective-permute-done | bytes 98336 | tf_op jit(solution)/shard_map/ppermute | solution.py:25
  20.4 0.7 %weight_middle.1 = f32[256,256]{1,0:T(8,128)S(1)} custom-call(bf16[400,256]{1,0:T(8,128)(2,1)S(1)} %maximum_select_fusion.near, bf16[208,256]{1,0:T(8,128)(2,1)S(1)} %collective-permute-done.3.far, bf16[192,256]{1,0:T(8,128)(2,1)S(1)} %collective-permute-done.5.passed), custom_call_target="tpu_custom_call" | custom-call | flops 100000000 | bytes 1000000 | tf_op jit(solution)/shard_map/weight_middle/pallas_call | solution.py:287
  21.1 0.0 collective-permute-done.4
  21.1 0.0 copy-start
  21.1 2.0 %collective-permute-start.6 = (bf16[256,256]{1,0:T(8,128)(2,1)S(1)}, bf16[256,256]{1,0:T(8,128)(2,1)S(1)}, u32[]{:S(2)}, u32[]{:S(2)}) collective-permute-start(bf16[256,256]{1,0:T(8,128)(2,1)S(1)} %add_convert_fusion.2), channel_id=1, source_target_pairs={{0,2},{1,3},{2,0},{3,1},{4,6},{5,7},{6,4},{7,5},{8,12},{9,13},{10,... | collective-permute-start | bytes 393224 | tf_op jit(solution)/shard_map/ppermute | solution.py:420
  23.2 0.2 rev.11.turned_outer
  23.4 0.0 copy-done
  23.4 1.8 %fields.1 = (bf16[4,32,256]{2,1,0:T(8,128)(2,1)}, bf16[4,32,256]{2,1,0:T(8,128)(2,1)}) custom-call(bf16[2,4,96,256]{3,2,1,0:T(8,128)(2,1)S(1)} %bitcast.12, bf16[32,256]{1,0:T(8,128)(2,1)S(1)} %reshape.100.filters, bf16[800,256]{1,0:T(8,128)(2,1)S(1)} %collective-permute-done.2.partner, bf16[400,256]{1,0:T(8,128)(2,1)S(1)} %maximum_select_fusion.1.outer, ...), custom_call_target="tpu_custom_call" | custom-call | flops 400000000 | bytes 1000000 | tf_op jit(solution)/shard_map/fields/pallas_call | solution.py:287
  25.2 2.1 %collective-permute-done.6 = bf16[256,256]{1,0:T(8,128)(2,1)S(1)} collective-permute-done((bf16[256,256]{1,0:T(8,128)(2,1)S(1)}, bf16[256,256]{1,0:T(8,128)(2,1)S(1)}, u32[]{:S(2)}, u32[]{:S(2)}) %collective-permute-start.6) | collective-permute-done | bytes 131104 | tf_op jit(solution)/shard_map/ppermute | solution.py:420
  27.4 0.3 collective-permute-start.7
  27.6 3.6 %collective-permute-done.7 = bf16[256,256]{1,0:T(8,128)(2,1)S(1)} collective-permute-done((bf16[256,256]{1,0:T(8,128)(2,1)S(1)}, bf16[256,256]{1,0:T(8,128)(2,1)S(1)}, u32[]{:S(2)}, u32[]{:S(2)}) %collective-permute-start.7) | collective-permute-done | bytes 131104 | tf_op jit(solution)/shard_map/ppermute | solution.py:420
  31.3 0.1 collective-permute-start.8
  31.4 3.8 %collective-permute-done.8 = bf16[256,256]{1,0:T(8,128)(2,1)S(1)} collective-permute-done((bf16[256,256]{1,0:T(8,128)(2,1)S(1)}, bf16[256,256]{1,0:T(8,128)(2,1)S(1)}, u32[]{:S(2)}, u32[]{:S(2)}) %collective-permute-start.8) | collective-permute-done | bytes 131104 | tf_op jit(solution)/shard_map/ppermute | solution.py:25
  35.2 4.9 %collective-permute-start.9 = (bf16[512,256]{1,0:T(8,128)(2,1)S(1)}, bf16[512,256]{1,0:T(8,128)(2,1)S(1)}, u32[]{:S(2)}, u32[]{:S(2)}) collective-permute-start(bf16[512,256]{1,0:T(8,128)(2,1)S(1)} %pad_maximum_fusion.1.part), channel_id=1, source_target_pairs={{0,8},{8,0},{16,24},{24,16},{1,9},{9,1},{17,25},{25,17},{2,10},{10... | collective-permute-start | bytes 786440 | tf_op jit(solution)/shard_map/ppermute | solution.py:25
  40.2 0.8 %store_first.1.kept = f32[1024,256]{1,0:T(8,128)} custom-call(bf16[512,256]{1,0:T(8,128)(2,1)S(1)} %pad_maximum_fusion.1.part), custom_call_target="tpu_custom_call" | custom-call | flops 1000000 | bytes 1000000 | tf_op jit(solution)/shard_map/store_first/pallas_call | solution.py:270
  41.0 0.3 collective-permute-done.9.part
  41.3 0.8 %store_second.1 = f32[1024,256]{1,0:T(8,128)} custom-call(bf16[512,256]{1,0:T(8,128)(2,1)S(1)} %collective-permute-done.9.part, f32[1024,256]{1,0:T(8,128)} %store_first.1.kept), custom_call_target="tpu_custom_call", output_to_operand_aliasing={{}: (1, {})} | custom-call | flops 1000000 | bytes 1000000 | tf_op jit(solution)/shard_map/store_second/pallas_call | solution.py:270
  (27 shorter events, 0.5 us)
Async XLA Ops:
  0.6 0.9 %copy-start.1 = (bf16[4,32,256]{2,1,0:T(8,128)(2,1)S(1)}, bf16[4,32,256]{2,1,0:T(8,128)(2,1)}, u32[]{:S(2)}) copy-start(bf16[4,32,256]{2,1,0:T(8,128)(2,1)} %param.7) | copy-start | bytes 196612
  1.5 4.5 %copy-start.3 = (s32[4]{0:T(128)S(1)}, s32[4]{0:T(128)}, u32[]{:S(2)}) copy-start(s32[4]{0:T(128)} %param.11) | copy-start | bytes 52
  1.5 4.5 %copy-start.4 = (s32[4]{0:T(128)S(1)}, s32[4]{0:T(128)}, u32[]{:S(2)}) copy-start(s32[4]{0:T(128)} %param.10) | copy-start | bytes 52
  1.6 4.7 %copy-start.2 = (bf16[4,4,5,64]{3,1,2,0:T(4,128)(2,1)S(1)}, bf16[4,4,5,64]{3,1,2,0:T(4,128)(2,1)}, u32[]{:S(2)}) copy-start(bf16[4,4,5,64]{3,1,2,0:T(4,128)(2,1)} %param.9) | copy-start | bytes 30724
  1.6 7.4 %collective-permute-start = (bf16[8,32,256]{2,1,0:T(8,128)(2,1)S(1)}, bf16[8,32,256]{2,1,0:T(8,128)(2,1)S(1)}, u32[]{:S(2)}, u32[]{:S(2)}) collective-permute-start(bf16[8,32,256]{2,1,0:T(8,128)(2,1)S(1)} %constant_dynamic-update-slice_fusion), channel_id=1, source_target_pairs={{0,1},{1,2},{2,3},{3,4},{4,5},{5,6},{6,7},{7,0},{8,9},{9,10},{10,1... | collective-permute-start | bytes 393224 | tf_op jit(solution)/shard_map/ppermute | solution.py:20
  2.9 6.1 %collective-permute-start.1 = (bf16[8,32,256]{2,1,0:T(8,128)(2,1)S(1)}, bf16[8,32,256]{2,1,0:T(8,128)(2,1)S(1)}, u32[]{:S(2)}, u32[]{:S(2)}) collective-permute-start(bf16[8,32,256]{2,1,0:T(8,128)(2,1)S(1)} %constant_dynamic-update-slice_fusion), channel_id=1, source_target_pairs={{0,7},{1,0},{2,1},{3,2},{4,3},{5,4},{6,5},{7,6},{8,15},{9,8},{10,9... | collective-permute-start | bytes 393224 | tf_op jit(solution)/shard_map/ppermute | solution.py:20
  9.0 4.0 %collective-permute-start.2 = (bf16[800,256]{1,0:T(8,128)(2,1)S(1)}, bf16[800,256]{1,0:T(8,128)(2,1)S(1)}, u32[]{:S(2)}, u32[]{:S(2)}) collective-permute-start(bf16[800,256]{1,0:T(8,128)(2,1)S(1)} %pad_maximum_fusion), channel_id=1, source_target_pairs={{0,8},{8,0},{16,24},{24,16},{1,9},{9,1},{17,25},{25,17},{2,10},{10... | collective-permute-start | bytes 1228808 | tf_op jit(solution)/shard_map/ppermute | solution.py:25
  13.1 4.2 %collective-permute-start.3 = (bf16[208,256]{1,0:T(8,128)(2,1)S(1)}, bf16[208,256]{1,0:T(8,128)(2,1)S(1)}, u32[]{:S(2)}, u32[]{:S(2)}) collective-permute-start(bf16[208,256]{1,0:T(8,128)(2,1)S(1)} %pad_maximum_fusion.2), channel_id=1, source_target_pairs={{0,16},{8,24},{16,0},{24,8},{1,17},{9,25},{17,1},{25,9},{2,18},{10... | collective-permute-start | bytes 319496 | tf_op jit(solution)/shard_map/ppermute | solution.py:25
  14.6 6.5 %collective-permute-start.4 = (bf16[256,256]{1,0:T(8,128)(2,1)S(1)}, bf16[256,256]{1,0:T(8,128)(2,1)S(1)}, u32[]{:S(2)}, u32[]{:S(2)}) collective-permute-start(bf16[256,256]{1,0:T(8,128)(2,1)S(1)} %weight_inner.1), channel_id=1, source_target_pairs={{0,16},{8,24},{16,0},{24,8},{1,17},{9,25},{17,1},{25,9},{2,18},{10... | collective-permute-start | bytes 393224 | tf_op jit(solution)/shard_map/ppermute | solution.py:25
  17.4 3.0 %collective-permute-start.5 = (bf16[192,256]{1,0:T(8,128)(2,1)S(1)}, bf16[192,256]{1,0:T(8,128)(2,1)S(1)}, u32[]{:S(2)}, u32[]{:S(2)}) collective-permute-start(bf16[192,256]{1,0:T(8,128)(2,1)S(1)} %slice.19), channel_id=1, source_target_pairs={{0,8},{8,0},{16,24},{24,16},{1,9},{9,1},{17,25},{25,17},{2,10},{10... | collective-permute-start | bytes 294920 | tf_op jit(solution)/shard_map/ppermute | solution.py:25
  21.1 2.3 %copy-start = (bf16[4,256,256]{2,1,0:T(8,128)(2,1)S(1)}, bf16[4,256,256]{2,1,0:T(8,128)(2,1)}, u32[]{:S(2)}) copy-start(bf16[4,256,256]{2,1,0:T(8,128)(2,1)} %weight.1) | copy-start | bytes 1572868
  21.1 6.2 %collective-permute-start.6 = (bf16[256,256]{1,0:T(8,128)(2,1)S(1)}, bf16[256,256]{1,0:T(8,128)(2,1)S(1)}, u32[]{:S(2)}, u32[]{:S(2)}) collective-permute-start(bf16[256,256]{1,0:T(8,128)(2,1)S(1)} %add_convert_fusion.2), channel_id=1, source_target_pairs={{0,2},{1,3},{2,0},{3,1},{4,6},{5,7},{6,4},{7,5},{8,12},{9,13},{10,... | collective-permute-start | bytes 393224 | tf_op jit(solution)/shard_map/ppermute | solution.py:420
  27.4 3.9 %collective-permute-start.7 = (bf16[256,256]{1,0:T(8,128)(2,1)S(1)}, bf16[256,256]{1,0:T(8,128)(2,1)S(1)}, u32[]{:S(2)}, u32[]{:S(2)}) collective-permute-start(bf16[256,256]{1,0:T(8,128)(2,1)S(1)} %add_convert_fusion.1), channel_id=1, source_target_pairs={{0,4},{1,5},{2,6},{3,7},{4,0},{5,1},{6,2},{7,3},{8,10},{9,11},{10,... | collective-permute-start | bytes 393224 | tf_op jit(solution)/shard_map/ppermute | solution.py:420
  31.3 3.9 %collective-permute-start.8 = (bf16[256,256]{1,0:T(8,128)(2,1)S(1)}, bf16[256,256]{1,0:T(8,128)(2,1)S(1)}, u32[]{:S(2)}, u32[]{:S(2)}) collective-permute-start(bf16[256,256]{1,0:T(8,128)(2,1)S(1)} %add_convert_fusion), channel_id=1, source_target_pairs={{0,1},{1,0},{2,3},{3,2},{4,5},{5,4},{6,7},{7,6},{8,9},{9,8},{10,11... | collective-permute-start | bytes 393224 | tf_op jit(solution)/shard_map/ppermute | solution.py:25
  35.2 6.1 %collective-permute-start.9 = (bf16[512,256]{1,0:T(8,128)(2,1)S(1)}, bf16[512,256]{1,0:T(8,128)(2,1)S(1)}, u32[]{:S(2)}, u32[]{:S(2)}) collective-permute-start(bf16[512,256]{1,0:T(8,128)(2,1)S(1)} %pad_maximum_fusion.1.part), channel_id=1, source_target_pairs={{0,8},{8,0},{16,24},{24,16},{1,9},{9,1},{17,25},{25,17},{2,10},{10... | collective-permute-start | bytes 786440 | tf_op jit(solution)/shard_map/ppermute | solution.py:25

commit v9 on v8

--- a/solution.py
+++ b/solution.py
@@ -315,9 +315,18 @@
     filters = jnp.pad(jnp.swapaxes(filters, 1, 2), ((0, 0), (0, TAP_ROWS - lat_taps), (0, 0), (0, 0)))
     filters = filters.reshape(rows * TAP_ROWS, channels)
 
+    late, filters = lax.optimization_barrier((own, filters))
+    ahead = flip(late, "lat", 1)
     strip = jnp.concatenate([west, own, east], axis=1).reshape(2, rows, lay.strip, channels)
-    partner = flip(jnp.concatenate([strip.reshape(-1, channels), filters], axis=0), "lat", 1)
-    partner_taps = partner[lay.cells :]
+    message = jnp.concatenate([west.reshape(-1, channels), east.reshape(-1, channels), filters], axis=0)
+    message, ahead = lax.optimization_barrier((message, ahead))
+    sides = flip(message, "lat", 1)
+    part = 2 * rows * width
+    partner_taps = sides[2 * part :]
+    partner = jnp.concatenate(
+        [sides[:part].reshape(own.shape), ahead, sides[part : 2 * part].reshape(own.shape)], axis=1
+    ).reshape(-1, channels)
+    partner = jnp.concatenate([partner, partner_taps], axis=0)
 
     def edge(cells, taps, bottom):
         start = jnp.where(bottom, rows - reach, 0)

time: 42.3 us -> 42.4 us (level)
  waiting for transfers between devices: 15.6 us -> 14.3 us
  starting transfers between devices: 18.1 us -> 19.2 us
    ppermute x2, waiting for transfers between devices: 2.52 us -> 1.24 us  [shift(): lax.ppermute(block, axis, [(i, (i + by) % count) for i in range(count)])]
    ppermute x6 -> x7, starting transfers between devices: 11.4 us -> 12.5 us  [flip(): return lax.ppermute(block, axis, [(i, i ^ bit) for i in range(count)])]
    ppermute x6 -> x7, waiting for transfers between devices: 7.39 us -> 7.39 us  [flip(): return lax.ppermute(block, axis, [(i, i ^ bit) for i in range(count)])]
  transfers between devices with their start and end apart: 10 -> 11, of which waited for: 8 -> 9; matrix products, arithmetic and copies ran while one was open for 3% -> 3% of each run, Pallas kernels for 11% -> 11%
where the time goes in v9:
time: 42.4 us; the launch traced here: 42.2 us
  starting transfers between devices  19.2 us (45%)
  waiting for transfers between devices  14.3 us (34%)
  Pallas kernels  5.29 us (12%)
  local copies, waits for them, and re-layouts  1.66 us (4%)
  between operations  0.9 us (2%)
  other arithmetic  0.84 us (2%)
    ppermute x7, starting transfers between devices, flip(): return lax.ppermute(block, axis, [(i, i ^ bit) for i in range(count)])  12.5 us
    ppermute x7, waiting for transfers between devices, flip(): return lax.ppermute(block, axis, [(i, i ^ bit) for i in range(count)])  7.39 us
    ppermute x2, waiting for transfers between devices, per_device(): got = lax.ppermute(grad, ('lat', 'lon'), pairs)  5.7 us
    ppermute x2, starting transfers between devices, shift(): lax.ppermute(block, axis, [(i, (i + by) % count) for i in range(count)])  4.4 us
    pallas_call x3, Pallas kernels, run(): pl.pallas_call(kernel, out_shape=outs, in_specs=[vmem] * len(operands), o...  3.63 us
    ppermute x2, starting transfers between devices, per_device(): got = lax.ppermute(grad, ('lat', 'lon'), pairs)  2.3 us
    pallas_call x2, Pallas kernels, store(): pl.pallas_call(first_kernel if kept is None else second_kernel, out_shape...  1.66 us
    ppermute x2, waiting for transfers between devices, shift(): lax.ppermute(block, axis, [(i, (i + by) % count) for i in range(count)])  1.24 us
  transfers between devices with their start and end apart: 11, of which 9 were waited for; matrix products, arithmetic and copies ran while one was open for 3% of the time, Pallas kernels for 11%

profile of v9, /device:TPU:3, one launch (start us, length us, event | category | flops | bytes accessed | tf_op | source)
XLA Modules:
  0.0 42.2 jit_solution(5989079706928953431)
XLA Ops:
  0.6 0.0 copy-start.1
  0.6 0.9 %constant_dynamic-update-slice_fusion.1 = bf16[8,32,256]{2,1,0:T(8,128)(2,1)S(1)} fusion(bf16[4,32,256]{2,1,0:T(8,128)(2,1)} %param.6), kind=kLoop, calls=%fused_computation.29 | loop fusion | bytes 131072
  1.5 0.0 copy-done.1
  1.5 0.0 copy-start.3
  1.5 0.0 copy-start.4
  1.6 0.0 copy-start.2
  1.6 1.3 %collective-permute-start = (bf16[8,32,256]{2,1,0:T(8,128)(2,1)S(1)}, bf16[8,32,256]{2,1,0:T(8,128)(2,1)S(1)}, u32[]{:S(2)}, u32[]{:S(2)}) collective-permute-start(bf16[8,32,256]{2,1,0:T(8,128)(2,1)S(1)} %constant_dynamic-update-slice_fusion), channel_id=1, source_target_pairs={{0,1},{1,2},{2,3},{3,4},{4,5},{5,6},{6,7},{7,0},{8,9},{9,10},{10,1... | collective-permute-start | bytes 393224 | tf_op jit(solution)/shard_map/ppermute | solution.py:20
  2.9 3.1 %collective-permute-start.1 = (bf16[8,32,256]{2,1,0:T(8,128)(2,1)S(1)}, bf16[8,32,256]{2,1,0:T(8,128)(2,1)S(1)}, u32[]{:S(2)}, u32[]{:S(2)}) collective-permute-start(bf16[8,32,256]{2,1,0:T(8,128)(2,1)S(1)} %constant_dynamic-update-slice_fusion), channel_id=1, source_target_pairs={{0,7},{1,0},{2,1},{3,2},{4,3},{5,4},{6,5},{7,6},{8,15},{9,8},{10,9... | collective-permute-start | bytes 393224 | tf_op jit(solution)/shard_map/ppermute | solution.py:20
  6.0 0.0 copy-done.3
  6.0 0.1 broadcast_compare_fusion
  6.0 0.0 copy-done.4
  6.1 0.1 broadcast_compare_fusion.1
  6.1 0.1 and_convert_fusion
  6.2 0.0 copy-done.2
  6.2 0.1 fusion.4
  6.3 0.1 reshape.119.filters
  6.4 1.1 %collective-permute-start.2 = (bf16[8,32,256]{2,1,0:T(8,128)(2,1)S(1)}, bf16[8,32,256]{2,1,0:T(8,128)(2,1)S(1)}, u32[]{:S(2)}, u32[]{:S(2)}) collective-permute-start(bf16[8,32,256]{2,1,0:T(8,128)(2,1)S(1)} %constant_dynamic-update-slice_fusion), channel_id=1, source_target_pairs={{0,8},{8,0},{16,24},{24,16},{1,9},{9,1},{17,25},{25,17},{2,10},{10... | collective-permute-start | bytes 393224 | tf_op jit(solution)/shard_map/ppermute | solution.py:25
  7.5 0.2 rev.9.turned
  7.7 0.2 collective-permute-done.1
  7.9 1.0 %collective-permute-done = bf16[8,32,256]{2,1,0:T(8,128)(2,1)S(1)} collective-permute-done((bf16[8,32,256]{2,1,0:T(8,128)(2,1)S(1)}, bf16[8,32,256]{2,1,0:T(8,128)(2,1)S(1)}, u32[]{:S(2)}, u32[]{:S(2)}) %collective-permute-start) | collective-permute-done | bytes 131104 | tf_op jit(solution)/shard_map/ppermute | solution.py:20
  9.0 0.0 collective-permute-done.2
  9.0 2.7 %collective-permute-start.3 = (bf16[544,256]{1,0:T(8,128)(2,1)S(1)}, bf16[544,256]{1,0:T(8,128)(2,1)S(1)}, u32[]{:S(2)}, u32[]{:S(2)}) collective-permute-start(bf16[544,256]{1,0:T(8,128)(2,1)S(1)} %pad_maximum_fusion.2), channel_id=1, source_target_pairs={{0,8},{8,0},{16,24},{24,16},{1,9},{9,1},{17,25},{25,17},{2,10},{10... | collective-permute-start | bytes 835592 | tf_op jit(solution)/shard_map/ppermute | solution.py:25
  11.8 1.1 %collective-permute-done.3 = bf16[544,256]{1,0:T(8,128)(2,1)S(1)} collective-permute-done((bf16[544,256]{1,0:T(8,128)(2,1)S(1)}, bf16[544,256]{1,0:T(8,128)(2,1)S(1)}, u32[]{:S(2)}, u32[]{:S(2)}) %collective-permute-start.3) | collective-permute-done | bytes 278560 | tf_op jit(solution)/shard_map/ppermute | solution.py:25
  13.0 0.1 fusion.3
  13.2 0.3 collective-permute-start.4
  13.5 1.2 %weight_inner.1 = bf16[256,256]{1,0:T(8,128)(2,1)S(1)} custom-call(bf16[2,4,96,256]{3,2,1,0:T(8,128)(2,1)S(1)} %bitcast.17, bf16[32,256]{1,0:T(8,128)(2,1)S(1)} %reshape.119.filters, bf16[800,256]{1,0:T(8,128)(2,1)S(1)} %pad_maximum_fusion.partner), custom_call_target="tpu_custom_call" | custom-call | flops 300000000 | bytes 1000000 | tf_op jit(solution)/shard_map/weight_inner/pallas_call | solution.py:287
  14.7 1.3 %collective-permute-start.5 = (bf16[256,256]{1,0:T(8,128)(2,1)S(1)}, bf16[256,256]{1,0:T(8,128)(2,1)S(1)}, u32[]{:S(2)}, u32[]{:S(2)}) collective-permute-start(bf16[256,256]{1,0:T(8,128)(2,1)S(1)} %weight_inner.1), channel_id=1, source_target_pairs={{0,16},{8,24},{16,0},{24,8},{1,17},{9,25},{17,1},{25,9},{2,18},{10... | collective-permute-start | bytes 393224 | tf_op jit(solution)/shard_map/ppermute | solution.py:25
  16.0 0.2 rev.10.turned_partner
  16.1 1.3 %collective-permute-done.4.far = bf16[208,256]{1,0:T(8,128)(2,1)S(1)} collective-permute-done((bf16[208,256]{1,0:T(8,128)(2,1)S(1)}, bf16[208,256]{1,0:T(8,128)(2,1)S(1)}, u32[]{:S(2)}, u32[]{:S(2)}) %collective-permute-start.4) | collective-permute-done | bytes 106528 | tf_op jit(solution)/shard_map/ppermute | solution.py:25
  17.4 2.1 %collective-permute-start.6 = (bf16[192,256]{1,0:T(8,128)(2,1)S(1)}, bf16[192,256]{1,0:T(8,128)(2,1)S(1)}, u32[]{:S(2)}, u32[]{:S(2)}) collective-permute-start(bf16[192,256]{1,0:T(8,128)(2,1)S(1)} %slice.23), channel_id=1, source_target_pairs={{0,8},{8,0},{16,24},{24,16},{1,9},{9,1},{17,25},{25,17},{2,10},{10... | collective-permute-start | bytes 294920 | tf_op jit(solution)/shard_map/ppermute | solution.py:25
  19.6 0.9 %collective-permute-done.6.passed = bf16[192,256]{1,0:T(8,128)(2,1)S(1)} collective-permute-done((bf16[192,256]{1,0:T(8,128)(2,1)S(1)}, bf16[192,256]{1,0:T(8,128)(2,1)S(1)}, u32[]{:S(2)}, u32[]{:S(2)}) %collective-permute-start.6) | collective-permute-done | bytes 98336 | tf_op jit(solution)/shard_map/ppermute | solution.py:25
  20.4 0.7 %weight_middle.1 = f32[256,256]{1,0:T(8,128)S(1)} custom-call(bf16[400,256]{1,0:T(8,128)(2,1)S(1)} %maximum_select_fusion.near, bf16[208,256]{1,0:T(8,128)(2,1)S(1)} %collective-permute-done.4.far, bf16[192,256]{1,0:T(8,128)(2,1)S(1)} %collective-permute-done.6.passed), custom_call_target="tpu_custom_call" | custom-call | flops 100000000 | bytes 1000000 | tf_op jit(solution)/shard_map/weight_middle/pallas_call | solution.py:287
  21.1 0.0 collective-permute-done.5
  21.2 0.0 copy-start
  21.2 2.0 %collective-permute-start.7 = (bf16[256,256]{1,0:T(8,128)(2,1)S(1)}, bf16[256,256]{1,0:T(8,128)(2,1)S(1)}, u32[]{:S(2)}, u32[]{:S(2)}) collective-permute-start(bf16[256,256]{1,0:T(8,128)(2,1)S(1)} %add_convert_fusion.2), channel_id=1, source_target_pairs={{0,2},{1,3},{2,0},{3,1},{4,6},{5,7},{6,4},{7,5},{8,12},{9,13},{10,... | collective-permute-start | bytes 393224 | tf_op jit(solution)/shard_map/ppermute | solution.py:429
  23.3 0.2 rev.11.turned_outer
  23.5 0.0 copy-done
  23.5 1.8 %fields.1 = (bf16[4,32,256]{2,1,0:T(8,128)(2,1)}, bf16[4,32,256]{2,1,0:T(8,128)(2,1)}) custom-call(bf16[2,4,96,256]{3,2,1,0:T(8,128)(2,1)S(1)} %bitcast.18, bf16[32,256]{1,0:T(8,128)(2,1)S(1)} %reshape.119.filters, bf16[800,256]{1,0:T(8,128)(2,1)S(1)} %pad_maximum_fusion.partner, bf16[400,256]{1,0:T(8,128)(2,1)S(1)} %maximum_select_fusion.1.outer, ...), custom_call_target="tpu_custom_call" | custom-call | flops 400000000 | bytes 1000000 | tf_op jit(solution)/shard_map/fields/pallas_call | solution.py:287
  25.3 2.1 %collective-permute-done.7 = bf16[256,256]{1,0:T(8,128)(2,1)S(1)} collective-permute-done((bf16[256,256]{1,0:T(8,128)(2,1)S(1)}, bf16[256,256]{1,0:T(8,128)(2,1)S(1)}, u32[]{:S(2)}, u32[]{:S(2)}) %collective-permute-start.7) | collective-permute-done | bytes 131104 | tf_op jit(solution)/shard_map/ppermute | solution.py:429
  27.4 0.3 collective-permute-start.8
  27.7 3.6 %collective-permute-done.8 = bf16[256,256]{1,0:T(8,128)(2,1)S(1)} collective-permute-done((bf16[256,256]{1,0:T(8,128)(2,1)S(1)}, bf16[256,256]{1,0:T(8,128)(2,1)S(1)}, u32[]{:S(2)}, u32[]{:S(2)}) %collective-permute-start.8) | collective-permute-done | bytes 131104 | tf_op jit(solution)/shard_map/ppermute | solution.py:429
  31.3 0.1 collective-permute-start.9
  31.4 3.8 %collective-permute-done.9 = bf16[256,256]{1,0:T(8,128)(2,1)S(1)} collective-permute-done((bf16[256,256]{1,0:T(8,128)(2,1)S(1)}, bf16[256,256]{1,0:T(8,128)(2,1)S(1)}, u32[]{:S(2)}, u32[]{:S(2)}) %collective-permute-start.9) | collective-permute-done | bytes 131104 | tf_op jit(solution)/shard_map/ppermute | solution.py:25
  35.3 4.9 %collective-permute-start.10 = (bf16[512,256]{1,0:T(8,128)(2,1)S(1)}, bf16[512,256]{1,0:T(8,128)(2,1)S(1)}, u32[]{:S(2)}, u32[]{:S(2)}) collective-permute-start(bf16[512,256]{1,0:T(8,128)(2,1)S(1)} %pad_maximum_fusion.3.part), channel_id=1, source_target_pairs={{0,8},{8,0},{16,24},{24,16},{1,9},{9,1},{17,25},{25,17},{2,10},{10... | collective-permute-start | bytes 786440 | tf_op jit(solution)/shard_map/ppermute | solution.py:25
  40.2 0.8 %store_first.1.kept = f32[1024,256]{1,0:T(8,128)} custom-call(bf16[512,256]{1,0:T(8,128)(2,1)S(1)} %pad_maximum_fusion.3.part), custom_call_target="tpu_custom_call" | custom-call | flops 1000000 | bytes 1000000 | tf_op jit(solution)/shard_map/store_first/pallas_call | solution.py:270
  41.0 0.3 collective-permute-done.10.part
  41.4 0.8 %store_second.1 = f32[1024,256]{1,0:T(8,128)} custom-call(bf16[512,256]{1,0:T(8,128)(2,1)S(1)} %collective-permute-done.10.part, f32[1024,256]{1,0:T(8,128)} %store_first.1.kept), custom_call_target="tpu_custom_call", output_to_operand_aliasing={{}: (1, {})} | custom-call | flops 1000000 | bytes 1000000 | tf_op jit(solution)/shard_map/store_second/pallas_call | solution.py:270
  (28 shorter events, 0.5 us)
Async XLA Ops:
  0.6 0.9 %copy-start.1 = (bf16[4,32,256]{2,1,0:T(8,128)(2,1)S(1)}, bf16[4,32,256]{2,1,0:T(8,128)(2,1)}, u32[]{:S(2)}) copy-start(bf16[4,32,256]{2,1,0:T(8,128)(2,1)} %param.7) | copy-start | bytes 196612
  1.5 4.5 %copy-start.3 = (s32[4]{0:T(128)S(1)}, s32[4]{0:T(128)}, u32[]{:S(2)}) copy-start(s32[4]{0:T(128)} %param.11) | copy-start | bytes 52
  1.5 4.5 %copy-start.4 = (s32[4]{0:T(128)S(1)}, s32[4]{0:T(128)}, u32[]{:S(2)}) copy-start(s32[4]{0:T(128)} %param.10) | copy-start | bytes 52
  1.6 4.7 %copy-start.2 = (bf16[4,4,5,64]{3,1,2,0:T(4,128)(2,1)S(1)}, bf16[4,4,5,64]{3,1,2,0:T(4,128)(2,1)}, u32[]{:S(2)}) copy-start(bf16[4,4,5,64]{3,1,2,0:T(4,128)(2,1)} %param.9) | copy-start | bytes 30724
  1.6 7.4 %collective-permute-start = (bf16[8,32,256]{2,1,0:T(8,128)(2,1)S(1)}, bf16[8,32,256]{2,1,0:T(8,128)(2,1)S(1)}, u32[]{:S(2)}, u32[]{:S(2)}) collective-permute-start(bf16[8,32,256]{2,1,0:T(8,128)(2,1)S(1)} %constant_dynamic-update-slice_fusion), channel_id=1, source_target_pairs={{0,1},{1,2},{2,3},{3,4},{4,5},{5,6},{6,7},{7,0},{8,9},{9,10},{10,1... | collective-permute-start | bytes 393224 | tf_op jit(solution)/shard_map/ppermute | solution.py:20
  2.9 5.1 %collective-permute-start.1 = (bf16[8,32,256]{2,1,0:T(8,128)(2,1)S(1)}, bf16[8,32,256]{2,1,0:T(8,128)(2,1)S(1)}, u32[]{:S(2)}, u32[]{:S(2)}) collective-permute-start(bf16[8,32,256]{2,1,0:T(8,128)(2,1)S(1)} %constant_dynamic-update-slice_fusion), channel_id=1, source_target_pairs={{0,7},{1,0},{2,1},{3,2},{4,3},{5,4},{6,5},{7,6},{8,15},{9,8},{10,9... | collective-permute-start | bytes 393224 | tf_op jit(solution)/shard_map/ppermute | solution.py:20
  6.4 2.5 %collective-permute-start.2 = (bf16[8,32,256]{2,1,0:T(8,128)(2,1)S(1)}, bf16[8,32,256]{2,1,0:T(8,128)(2,1)S(1)}, u32[]{:S(2)}, u32[]{:S(2)}) collective-permute-start(bf16[8,32,256]{2,1,0:T(8,128)(2,1)S(1)} %constant_dynamic-update-slice_fusion), channel_id=1, source_target_pairs={{0,8},{8,0},{16,24},{24,16},{1,9},{9,1},{17,25},{25,17},{2,10},{10... | collective-permute-start | bytes 393224 | tf_op jit(solution)/shard_map/ppermute | solution.py:25
  9.0 3.9 %collective-permute-start.3 = (bf16[544,256]{1,0:T(8,128)(2,1)S(1)}, bf16[544,256]{1,0:T(8,128)(2,1)S(1)}, u32[]{:S(2)}, u32[]{:S(2)}) collective-permute-start(bf16[544,256]{1,0:T(8,128)(2,1)S(1)} %pad_maximum_fusion.2), channel_id=1, source_target_pairs={{0,8},{8,0},{16,24},{24,16},{1,9},{9,1},{17,25},{25,17},{2,10},{10... | collective-permute-start | bytes 835592 | tf_op jit(solution)/shard_map/ppermute | solution.py:25
  13.2 4.2 %collective-permute-start.4 = (bf16[208,256]{1,0:T(8,128)(2,1)S(1)}, bf16[208,256]{1,0:T(8,128)(2,1)S(1)}, u32[]{:S(2)}, u32[]{:S(2)}) collective-permute-start(bf16[208,256]{1,0:T(8,128)(2,1)S(1)} %pad_maximum_fusion.4), channel_id=1, source_target_pairs={{0,16},{8,24},{16,0},{24,8},{1,17},{9,25},{17,1},{25,9},{2,18},{10... | collective-permute-start | bytes 319496 | tf_op jit(solution)/shard_map/ppermute | solution.py:25
  14.7 6.5 %collective-permute-start.5 = (bf16[256,256]{1,0:T(8,128)(2,1)S(1)}, bf16[256,256]{1,0:T(8,128)(2,1)S(1)}, u32[]{:S(2)}, u32[]{:S(2)}) collective-permute-start(bf16[256,256]{1,0:T(8,128)(2,1)S(1)} %weight_inner.1), channel_id=1, source_target_pairs={{0,16},{8,24},{16,0},{24,8},{1,17},{9,25},{17,1},{25,9},{2,18},{10... | collective-permute-start | bytes 393224 | tf_op jit(solution)/shard_map/ppermute | solution.py:25
  17.4 3.0 %collective-permute-start.6 = (bf16[192,256]{1,0:T(8,128)(2,1)S(1)}, bf16[192,256]{1,0:T(8,128)(2,1)S(1)}, u32[]{:S(2)}, u32[]{:S(2)}) collective-permute-start(bf16[192,256]{1,0:T(8,128)(2,1)S(1)} %slice.23), channel_id=1, source_target_pairs={{0,8},{8,0},{16,24},{24,16},{1,9},{9,1},{17,25},{25,17},{2,10},{10... | collective-permute-start | bytes 294920 | tf_op jit(solution)/shard_map/ppermute | solution.py:25
  21.2 2.3 %copy-start = (bf16[4,256,256]{2,1,0:T(8,128)(2,1)S(1)}, bf16[4,256,256]{2,1,0:T(8,128)(2,1)}, u32[]{:S(2)}) copy-start(bf16[4,256,256]{2,1,0:T(8,128)(2,1)} %weight.1) | copy-start | bytes 1572868
  21.2 6.2 %collective-permute-start.7 = (bf16[256,256]{1,0:T(8,128)(2,1)S(1)}, bf16[256,256]{1,0:T(8,128)(2,1)S(1)}, u32[]{:S(2)}, u32[]{:S(2)}) collective-permute-start(bf16[256,256]{1,0:T(8,128)(2,1)S(1)} %add_convert_fusion.2), channel_id=1, source_target_pairs={{0,2},{1,3},{2,0},{3,1},{4,6},{5,7},{6,4},{7,5},{8,12},{9,13},{10,... | collective-permute-start | bytes 393224 | tf_op jit(solution)/shard_map/ppermute | solution.py:429
  27.4 3.9 %collective-permute-start.8 = (bf16[256,256]{1,0:T(8,128)(2,1)S(1)}, bf16[256,256]{1,0:T(8,128)(2,1)S(1)}, u32[]{:S(2)}, u32[]{:S(2)}) collective-permute-start(bf16[256,256]{1,0:T(8,128)(2,1)S(1)} %add_convert_fusion.1), channel_id=1, source_target_pairs={{0,4},{1,5},{2,6},{3,7},{4,0},{5,1},{6,2},{7,3},{8,10},{9,11},{10,... | collective-permute-start | bytes 393224 | tf_op jit(solution)/shard_map/ppermute | solution.py:429
  31.3 3.9 %collective-permute-start.9 = (bf16[256,256]{1,0:T(8,128)(2,1)S(1)}, bf16[256,256]{1,0:T(8,128)(2,1)S(1)}, u32[]{:S(2)}, u32[]{:S(2)}) collective-permute-start(bf16[256,256]{1,0:T(8,128)(2,1)S(1)} %add_convert_fusion), channel_id=1, source_target_pairs={{0,1},{1,0},{2,3},{3,2},{4,5},{5,4},{6,7},{7,6},{8,9},{9,8},{10,11... | collective-permute-start | bytes 393224 | tf_op jit(solution)/shard_map/ppermute | solution.py:25
  35.3 6.1 %collective-permute-start.10 = (bf16[512,256]{1,0:T(8,128)(2,1)S(1)}, bf16[512,256]{1,0:T(8,128)(2,1)S(1)}, u32[]{:S(2)}, u32[]{:S(2)}) collective-permute-start(bf16[512,256]{1,0:T(8,128)(2,1)S(1)} %pad_maximum_fusion.3.part), channel_id=1, source_target_pairs={{0,8},{8,0},{16,24},{24,16},{1,9},{9,1},{17,25},{25,17},{2,10},{10... | collective-permute-start | bytes 786440 | tf_op jit(solution)/shard_map/ppermute | solution.py:25

commit v10 on v9

--- a/solution.py
+++ b/solution.py
@@ -266,7 +266,7 @@
 def store(part, kept=None):
     rows, channels = part.shape
     vmem, anywhere = pl.BlockSpec(memory_space=pltpu.VMEM), pl.BlockSpec(memory_space=pl.ANY)
-    pieces = 4
+    pieces = 2
     return pl.pallas_call(
         first_kernel if kept is None else second_kernel,
         out_shape=jax.ShapeDtypeStruct((2 * rows, channels), jnp.float32),
@@ -347,7 +347,7 @@
     piece_taps = jnp.where(
         beside,
         lax.dynamic_slice_in_dim(filters, at_taps, reach * TAP_ROWS, 0),
-        lax.dynamic_slice_in_dim(partner, lay.cells + at_taps, reach * TAP_ROWS, 0),
+        lax.dynamic_slice_in_dim(partner_taps, at_taps, reach * TAP_ROWS, 0),
     )
     far = flip(jnp.concatenate([piece, piece_taps], axis=0), "lat", 2)
 

time: 42.4 us -> 42.3 us (level)
  no operation moved by 1% of the time
where the time goes in v10:
time: 42.3 us; the launch traced here: 42.2 us
  starting transfers between devices  19.2 us (45%)
  waiting for transfers between devices  14.3 us (34%)
  Pallas kernels  5.27 us (12%)
  local copies, waits for them, and re-layouts  1.66 us (4%)
  between operations  0.9 us (2%)
  other arithmetic  0.82 us (2%)
    ppermute x7, starting transfers between devices, flip(): return lax.ppermute(block, axis, [(i, i ^ bit) for i in range(count)])  12.5 us
    ppermute x7, waiting for transfers between devices, flip(): return lax.ppermute(block, axis, [(i, i ^ bit) for i in range(count)])  7.4 us
    ppermute x2, waiting for transfers between devices, per_device(): got = lax.ppermute(grad, ('lat', 'lon'), pairs)  5.71 us
    ppermute x2, starting transfers between devices, shift(): lax.ppermute(block, axis, [(i, (i + by) % count) for i in range(count)])  4.4 us
    pallas_call x3, Pallas kernels, run(): pl.pallas_call(kernel, out_shape=outs, in_specs=[vmem] * len(operands), o...  3.62 us
    ppermute x2, starting transfers between devices, per_device(): got = lax.ppermute(grad, ('lat', 'lon'), pairs)  2.29 us
    pallas_call x2, Pallas kernels, store(): pl.pallas_call(first_kernel if kept is None else second_kernel, out_shape...  1.65 us
    ppermute x2, waiting for transfers between devices, shift(): lax.ppermute(block, axis, [(i, (i + by) % count) for i in range(count)])  1.24 us
  transfers between devices with their start and end apart: 11, of which 9 were waited for; matrix products, arithmetic and copies ran while one was open for 3% of the time, Pallas kernels for 11%

profile of v10, /device:TPU:3, one launch (start us, length us, event | category | flops | bytes accessed | tf_op | source)
XLA Modules:
  0.0 42.2 jit_solution(9459025278548343895)
XLA Ops:
  0.6 0.0 copy-start.1
  0.6 0.9 %constant_dynamic-update-slice_fusion.1 = bf16[8,32,256]{2,1,0:T(8,128)(2,1)S(1)} fusion(bf16[4,32,256]{2,1,0:T(8,128)(2,1)} %param.6), kind=kLoop, calls=%fused_computation.27 | loop fusion | bytes 131072
  1.5 0.0 copy-done.1
  1.5 0.0 copy-start.3
  1.5 0.0 copy-start.4
  1.6 0.0 copy-start.2
  1.6 1.3 %collective-permute-start = (bf16[8,32,256]{2,1,0:T(8,128)(2,1)S(1)}, bf16[8,32,256]{2,1,0:T(8,128)(2,1)S(1)}, u32[]{:S(2)}, u32[]{:S(2)}) collective-permute-start(bf16[8,32,256]{2,1,0:T(8,128)(2,1)S(1)} %constant_dynamic-update-slice_fusion), channel_id=1, source_target_pairs={{0,1},{1,2},{2,3},{3,4},{4,5},{5,6},{6,7},{7,0},{8,9},{9,10},{10,1... | collective-permute-start | bytes 393224 | tf_op jit(solution)/shard_map/ppermute | solution.py:20
  2.9 3.1 %collective-permute-start.1 = (bf16[8,32,256]{2,1,0:T(8,128)(2,1)S(1)}, bf16[8,32,256]{2,1,0:T(8,128)(2,1)S(1)}, u32[]{:S(2)}, u32[]{:S(2)}) collective-permute-start(bf16[8,32,256]{2,1,0:T(8,128)(2,1)S(1)} %constant_dynamic-update-slice_fusion), channel_id=1, source_target_pairs={{0,7},{1,0},{2,1},{3,2},{4,3},{5,4},{6,5},{7,6},{8,15},{9,8},{10,9... | collective-permute-start | bytes 393224 | tf_op jit(solution)/shard_map/ppermute | solution.py:20
  6.0 0.0 copy-done.3
  6.0 0.1 broadcast_compare_fusion
  6.0 0.0 copy-done.4
  6.1 0.1 broadcast_compare_fusion.1
  6.1 0.1 and_convert_fusion
  6.2 0.0 copy-done.2
  6.2 0.1 fusion.4
  6.3 0.1 reshape.119.filters
  6.4 1.1 %collective-permute-start.2 = (bf16[8,32,256]{2,1,0:T(8,128)(2,1)S(1)}, bf16[8,32,256]{2,1,0:T(8,128)(2,1)S(1)}, u32[]{:S(2)}, u32[]{:S(2)}) collective-permute-start(bf16[8,32,256]{2,1,0:T(8,128)(2,1)S(1)} %constant_dynamic-update-slice_fusion), channel_id=1, source_target_pairs={{0,8},{8,0},{16,24},{24,16},{1,9},{9,1},{17,25},{25,17},{2,10},{10... | collective-permute-start | bytes 393224 | tf_op jit(solution)/shard_map/ppermute | solution.py:25
  7.5 0.2 rev.9.turned
  7.7 0.2 collective-permute-done.1
  7.9 1.0 %collective-permute-done = bf16[8,32,256]{2,1,0:T(8,128)(2,1)S(1)} collective-permute-done((bf16[8,32,256]{2,1,0:T(8,128)(2,1)S(1)}, bf16[8,32,256]{2,1,0:T(8,128)(2,1)S(1)}, u32[]{:S(2)}, u32[]{:S(2)}) %collective-permute-start) | collective-permute-done | bytes 131104 | tf_op jit(solution)/shard_map/ppermute | solution.py:20
  9.0 0.0 collective-permute-done.2
  9.0 2.7 %collective-permute-start.3 = (bf16[544,256]{1,0:T(8,128)(2,1)S(1)}, bf16[544,256]{1,0:T(8,128)(2,1)S(1)}, u32[]{:S(2)}, u32[]{:S(2)}) collective-permute-start(bf16[544,256]{1,0:T(8,128)(2,1)S(1)} %pad_maximum_fusion.2), channel_id=1, source_target_pairs={{0,8},{8,0},{16,24},{24,16},{1,9},{9,1},{17,25},{25,17},{2,10},{10... | collective-permute-start | bytes 835592 | tf_op jit(solution)/shard_map/ppermute | solution.py:25
  11.8 1.1 %collective-permute-done.3 = bf16[544,256]{1,0:T(8,128)(2,1)S(1)} collective-permute-done((bf16[544,256]{1,0:T(8,128)(2,1)S(1)}, bf16[544,256]{1,0:T(8,128)(2,1)S(1)}, u32[]{:S(2)}, u32[]{:S(2)}) %collective-permute-start.3) | collective-permute-done | bytes 278560 | tf_op jit(solution)/shard_map/ppermute | solution.py:25
  13.0 0.1 fusion.3
  13.2 0.3 collective-permute-start.4
  13.5 1.2 %weight_inner.1 = bf16[256,256]{1,0:T(8,128)(2,1)S(1)} custom-call(bf16[2,4,96,256]{3,2,1,0:T(8,128)(2,1)S(1)} %bitcast.17, bf16[32,256]{1,0:T(8,128)(2,1)S(1)} %reshape.119.filters, bf16[800,256]{1,0:T(8,128)(2,1)S(1)} %pad_maximum_fusion.partner), custom_call_target="tpu_custom_call" | custom-call | flops 300000000 | bytes 1000000 | tf_op jit(solution)/shard_map/weight_inner/pallas_call | solution.py:287
  14.6 1.3 %collective-permute-start.5 = (bf16[256,256]{1,0:T(8,128)(2,1)S(1)}, bf16[256,256]{1,0:T(8,128)(2,1)S(1)}, u32[]{:S(2)}, u32[]{:S(2)}) collective-permute-start(bf16[256,256]{1,0:T(8,128)(2,1)S(1)} %weight_inner.1), channel_id=1, source_target_pairs={{0,16},{8,24},{16,0},{24,8},{1,17},{9,25},{17,1},{25,9},{2,18},{10... | collective-permute-start | bytes 393224 | tf_op jit(solution)/shard_map/ppermute | solution.py:25
  15.9 0.2 rev.10.turned_partner
  16.1 1.3 %collective-permute-done.4.far = bf16[208,256]{1,0:T(8,128)(2,1)S(1)} collective-permute-done((bf16[208,256]{1,0:T(8,128)(2,1)S(1)}, bf16[208,256]{1,0:T(8,128)(2,1)S(1)}, u32[]{:S(2)}, u32[]{:S(2)}) %collective-permute-start.4) | collective-permute-done | bytes 106528 | tf_op jit(solution)/shard_map/ppermute | solution.py:25
  17.4 2.1 %collective-permute-start.6 = (bf16[192,256]{1,0:T(8,128)(2,1)S(1)}, bf16[192,256]{1,0:T(8,128)(2,1)S(1)}, u32[]{:S(2)}, u32[]{:S(2)}) collective-permute-start(bf16[192,256]{1,0:T(8,128)(2,1)S(1)} %slice.23), channel_id=1, source_target_pairs={{0,8},{8,0},{16,24},{24,16},{1,9},{9,1},{17,25},{25,17},{2,10},{10... | collective-permute-start | bytes 294920 | tf_op jit(solution)/shard_map/ppermute | solution.py:25
  19.5 0.1 maximum_select_fusion.near
  19.5 0.9 %collective-permute-done.6.passed = bf16[192,256]{1,0:T(8,128)(2,1)S(1)} collective-permute-done((bf16[192,256]{1,0:T(8,128)(2,1)S(1)}, bf16[192,256]{1,0:T(8,128)(2,1)S(1)}, u32[]{:S(2)}, u32[]{:S(2)}) %collective-permute-start.6) | collective-permute-done | bytes 98336 | tf_op jit(solution)/shard_map/ppermute | solution.py:25
  20.4 0.7 %weight_middle.1 = f32[256,256]{1,0:T(8,128)S(1)} custom-call(bf16[400,256]{1,0:T(8,128)(2,1)S(1)} %maximum_select_fusion.near, bf16[208,256]{1,0:T(8,128)(2,1)S(1)} %collective-permute-done.4.far, bf16[192,256]{1,0:T(8,128)(2,1)S(1)} %collective-permute-done.6.passed), custom_call_target="tpu_custom_call" | custom-call | flops 100000000 | bytes 1000000 | tf_op jit(solution)/shard_map/weight_middle/pallas_call | solution.py:287
  21.1 0.0 collective-permute-done.5
  21.2 0.0 copy-start
  21.2 2.0 %collective-permute-start.7 = (bf16[256,256]{1,0:T(8,128)(2,1)S(1)}, bf16[256,256]{1,0:T(8,128)(2,1)S(1)}, u32[]{:S(2)}, u32[]{:S(2)}) collective-permute-start(bf16[256,256]{1,0:T(8,128)(2,1)S(1)} %add_convert_fusion.2), channel_id=1, source_target_pairs={{0,2},{1,3},{2,0},{3,1},{4,6},{5,7},{6,4},{7,5},{8,12},{9,13},{10,... | collective-permute-start | bytes 393224 | tf_op jit(solution)/shard_map/ppermute | solution.py:429
  23.3 0.2 rev.11.turned_outer
  23.5 0.0 copy-done
  23.5 1.8 %fields.1 = (bf16[4,32,256]{2,1,0:T(8,128)(2,1)}, bf16[4,32,256]{2,1,0:T(8,128)(2,1)}) custom-call(bf16[2,4,96,256]{3,2,1,0:T(8,128)(2,1)S(1)} %bitcast.18, bf16[32,256]{1,0:T(8,128)(2,1)S(1)} %reshape.119.filters, bf16[800,256]{1,0:T(8,128)(2,1)S(1)} %pad_maximum_fusion.partner, bf16[400,256]{1,0:T(8,128)(2,1)S(1)} %maximum_select_fusion.1.outer, ...), custom_call_target="tpu_custom_call" | custom-call | flops 400000000 | bytes 1000000 | tf_op jit(solution)/shard_map/fields/pallas_call | solution.py:287
  25.3 2.1 %collective-permute-done.7 = bf16[256,256]{1,0:T(8,128)(2,1)S(1)} collective-permute-done((bf16[256,256]{1,0:T(8,128)(2,1)S(1)}, bf16[256,256]{1,0:T(8,128)(2,1)S(1)}, u32[]{:S(2)}, u32[]{:S(2)}) %collective-permute-start.7) | collective-permute-done | bytes 131104 | tf_op jit(solution)/shard_map/ppermute | solution.py:429
  27.4 0.3 collective-permute-start.8
  27.7 3.6 %collective-permute-done.8 = bf16[256,256]{1,0:T(8,128)(2,1)S(1)} collective-permute-done((bf16[256,256]{1,0:T(8,128)(2,1)S(1)}, bf16[256,256]{1,0:T(8,128)(2,1)S(1)}, u32[]{:S(2)}, u32[]{:S(2)}) %collective-permute-start.8) | collective-permute-done | bytes 131104 | tf_op jit(solution)/shard_map/ppermute | solution.py:429
  31.3 0.1 collective-permute-start.9
  31.4 3.8 %collective-permute-done.9 = bf16[256,256]{1,0:T(8,128)(2,1)S(1)} collective-permute-done((bf16[256,256]{1,0:T(8,128)(2,1)S(1)}, bf16[256,256]{1,0:T(8,128)(2,1)S(1)}, u32[]{:S(2)}, u32[]{:S(2)}) %collective-permute-start.9) | collective-permute-done | bytes 131104 | tf_op jit(solution)/shard_map/ppermute | solution.py:25
  35.3 4.9 %collective-permute-start.10 = (bf16[512,256]{1,0:T(8,128)(2,1)S(1)}, bf16[512,256]{1,0:T(8,128)(2,1)S(1)}, u32[]{:S(2)}, u32[]{:S(2)}) collective-permute-start(bf16[512,256]{1,0:T(8,128)(2,1)S(1)} %pad_maximum_fusion.3.part), channel_id=1, source_target_pairs={{0,8},{8,0},{16,24},{24,16},{1,9},{9,1},{17,25},{25,17},{2,10},{10... | collective-permute-start | bytes 786440 | tf_op jit(solution)/shard_map/ppermute | solution.py:25
  40.2 0.8 %store_first.1.kept = f32[1024,256]{1,0:T(8,128)} custom-call(bf16[512,256]{1,0:T(8,128)(2,1)S(1)} %pad_maximum_fusion.3.part), custom_call_target="tpu_custom_call" | custom-call | flops 1000000 | bytes 1000000 | tf_op jit(solution)/shard_map/store_first/pallas_call | solution.py:270
  41.0 0.3 collective-permute-done.10.part
  41.3 0.8 %store_second.1 = f32[1024,256]{1,0:T(8,128)} custom-call(bf16[512,256]{1,0:T(8,128)(2,1)S(1)} %collective-permute-done.10.part, f32[1024,256]{1,0:T(8,128)} %store_first.1.kept), custom_call_target="tpu_custom_call", output_to_operand_aliasing={{}: (1, {})} | custom-call | flops 1000000 | bytes 1000000 | tf_op jit(solution)/shard_map/store_second/pallas_call | solution.py:270
  (27 shorter events, 0.5 us)
Async XLA Ops:
  0.6 0.9 %copy-start.1 = (bf16[4,32,256]{2,1,0:T(8,128)(2,1)S(1)}, bf16[4,32,256]{2,1,0:T(8,128)(2,1)}, u32[]{:S(2)}) copy-start(bf16[4,32,256]{2,1,0:T(8,128)(2,1)} %param.7) | copy-start | bytes 196612
  1.5 4.5 %copy-start.3 = (s32[4]{0:T(128)S(1)}, s32[4]{0:T(128)}, u32[]{:S(2)}) copy-start(s32[4]{0:T(128)} %param.11) | copy-start | bytes 52
  1.5 4.5 %copy-start.4 = (s32[4]{0:T(128)S(1)}, s32[4]{0:T(128)}, u32[]{:S(2)}) copy-start(s32[4]{0:T(128)} %param.10) | copy-start | bytes 52
  1.6 4.7 %copy-start.2 = (bf16[4,4,5,64]{3,1,2,0:T(4,128)(2,1)S(1)}, bf16[4,4,5,64]{3,1,2,0:T(4,128)(2,1)}, u32[]{:S(2)}) copy-start(bf16[4,4,5,64]{3,1,2,0:T(4,128)(2,1)} %param.9) | copy-start | bytes 30724
  1.6 7.4 %collective-permute-start = (bf16[8,32,256]{2,1,0:T(8,128)(2,1)S(1)}, bf16[8,32,256]{2,1,0:T(8,128)(2,1)S(1)}, u32[]{:S(2)}, u32[]{:S(2)}) collective-permute-start(bf16[8,32,256]{2,1,0:T(8,128)(2,1)S(1)} %constant_dynamic-update-slice_fusion), channel_id=1, source_target_pairs={{0,1},{1,2},{2,3},{3,4},{4,5},{5,6},{6,7},{7,0},{8,9},{9,10},{10,1... | collective-permute-start | bytes 393224 | tf_op jit(solution)/shard_map/ppermute | solution.py:20
  2.9 5.1 %collective-permute-start.1 = (bf16[8,32,256]{2,1,0:T(8,128)(2,1)S(1)}, bf16[8,32,256]{2,1,0:T(8,128)(2,1)S(1)}, u32[]{:S(2)}, u32[]{:S(2)}) collective-permute-start(bf16[8,32,256]{2,1,0:T(8,128)(2,1)S(1)} %constant_dynamic-update-slice_fusion), channel_id=1, source_target_pairs={{0,7},{1,0},{2,1},{3,2},{4,3},{5,4},{6,5},{7,6},{8,15},{9,8},{10,9... | collective-permute-start | bytes 393224 | tf_op jit(solution)/shard_map/ppermute | solution.py:20
  6.4 2.5 %collective-permute-start.2 = (bf16[8,32,256]{2,1,0:T(8,128)(2,1)S(1)}, bf16[8,32,256]{2,1,0:T(8,128)(2,1)S(1)}, u32[]{:S(2)}, u32[]{:S(2)}) collective-permute-start(bf16[8,32,256]{2,1,0:T(8,128)(2,1)S(1)} %constant_dynamic-update-slice_fusion), channel_id=1, source_target_pairs={{0,8},{8,0},{16,24},{24,16},{1,9},{9,1},{17,25},{25,17},{2,10},{10... | collective-permute-start | bytes 393224 | tf_op jit(solution)/shard_map/ppermute | solution.py:25
  9.0 3.9 %collective-permute-start.3 = (bf16[544,256]{1,0:T(8,128)(2,1)S(1)}, bf16[544,256]{1,0:T(8,128)(2,1)S(1)}, u32[]{:S(2)}, u32[]{:S(2)}) collective-permute-start(bf16[544,256]{1,0:T(8,128)(2,1)S(1)} %pad_maximum_fusion.2), channel_id=1, source_target_pairs={{0,8},{8,0},{16,24},{24,16},{1,9},{9,1},{17,25},{25,17},{2,10},{10... | collective-permute-start | bytes 835592 | tf_op jit(solution)/shard_map/ppermute | solution.py:25
  13.2 4.2 %collective-permute-start.4 = (bf16[208,256]{1,0:T(8,128)(2,1)S(1)}, bf16[208,256]{1,0:T(8,128)(2,1)S(1)}, u32[]{:S(2)}, u32[]{:S(2)}) collective-permute-start(bf16[208,256]{1,0:T(8,128)(2,1)S(1)} %pad_maximum_fusion.4), channel_id=1, source_target_pairs={{0,16},{8,24},{16,0},{24,8},{1,17},{9,25},{17,1},{25,9},{2,18},{10... | collective-permute-start | bytes 319496 | tf_op jit(solution)/shard_map/ppermute | solution.py:25
  14.6 6.5 %collective-permute-start.5 = (bf16[256,256]{1,0:T(8,128)(2,1)S(1)}, bf16[256,256]{1,0:T(8,128)(2,1)S(1)}, u32[]{:S(2)}, u32[]{:S(2)}) collective-permute-start(bf16[256,256]{1,0:T(8,128)(2,1)S(1)} %weight_inner.1), channel_id=1, source_target_pairs={{0,16},{8,24},{16,0},{24,8},{1,17},{9,25},{17,1},{25,9},{2,18},{10... | collective-permute-start | bytes 393224 | tf_op jit(solution)/shard_map/ppermute | solution.py:25
  17.4 3.0 %collective-permute-start.6 = (bf16[192,256]{1,0:T(8,128)(2,1)S(1)}, bf16[192,256]{1,0:T(8,128)(2,1)S(1)}, u32[]{:S(2)}, u32[]{:S(2)}) collective-permute-start(bf16[192,256]{1,0:T(8,128)(2,1)S(1)} %slice.23), channel_id=1, source_target_pairs={{0,8},{8,0},{16,24},{24,16},{1,9},{9,1},{17,25},{25,17},{2,10},{10... | collective-permute-start | bytes 294920 | tf_op jit(solution)/shard_map/ppermute | solution.py:25
  21.2 2.3 %copy-start = (bf16[4,256,256]{2,1,0:T(8,128)(2,1)S(1)}, bf16[4,256,256]{2,1,0:T(8,128)(2,1)}, u32[]{:S(2)}) copy-start(bf16[4,256,256]{2,1,0:T(8,128)(2,1)} %weight.1) | copy-start | bytes 1572868
  21.2 6.2 %collective-permute-start.7 = (bf16[256,256]{1,0:T(8,128)(2,1)S(1)}, bf16[256,256]{1,0:T(8,128)(2,1)S(1)}, u32[]{:S(2)}, u32[]{:S(2)}) collective-permute-start(bf16[256,256]{1,0:T(8,128)(2,1)S(1)} %add_convert_fusion.2), channel_id=1, source_target_pairs={{0,2},{1,3},{2,0},{3,1},{4,6},{5,7},{6,4},{7,5},{8,12},{9,13},{10,... | collective-permute-start | bytes 393224 | tf_op jit(solution)/shard_map/ppermute | solution.py:429
  27.4 3.9 %collective-permute-start.8 = (bf16[256,256]{1,0:T(8,128)(2,1)S(1)}, bf16[256,256]{1,0:T(8,128)(2,1)S(1)}, u32[]{:S(2)}, u32[]{:S(2)}) collective-permute-start(bf16[256,256]{1,0:T(8,128)(2,1)S(1)} %add_convert_fusion.1), channel_id=1, source_target_pairs={{0,4},{1,5},{2,6},{3,7},{4,0},{5,1},{6,2},{7,3},{8,10},{9,11},{10,... | collective-permute-start | bytes 393224 | tf_op jit(solution)/shard_map/ppermute | solution.py:429
  31.3 3.9 %collective-permute-start.9 = (bf16[256,256]{1,0:T(8,128)(2,1)S(1)}, bf16[256,256]{1,0:T(8,128)(2,1)S(1)}, u32[]{:S(2)}, u32[]{:S(2)}) collective-permute-start(bf16[256,256]{1,0:T(8,128)(2,1)S(1)} %add_convert_fusion), channel_id=1, source_target_pairs={{0,1},{1,0},{2,3},{3,2},{4,5},{5,4},{6,7},{7,6},{8,9},{9,8},{10,11... | collective-permute-start | bytes 393224 | tf_op jit(solution)/shard_map/ppermute | solution.py:25
  35.3 6.1 %collective-permute-start.10 = (bf16[512,256]{1,0:T(8,128)(2,1)S(1)}, bf16[512,256]{1,0:T(8,128)(2,1)S(1)}, u32[]{:S(2)}, u32[]{:S(2)}) collective-permute-start(bf16[512,256]{1,0:T(8,128)(2,1)S(1)} %pad_maximum_fusion.3.part), channel_id=1, source_target_pairs={{0,8},{8,0},{16,24},{24,16},{1,9},{9,1},{17,25},{25,17},{2,10},{10... | collective-permute-start | bytes 786440 | tf_op jit(solution)/shard_map/ppermute | solution.py:25
